TPU v7x, 32 devices: a whole 2x2x4 slice. The times are simulated.
32 devices in a mesh: page: 8 (over z, x), win: 4 (over y, core).
Axes of the slice: x: 2, y: 2, z: 4, core: 2. Of those that a mesh axis runs over, the one named last changes fastest.
Arguments:
- visual: bfloat16 [8, 48, 36, 768], P('page', 'win'), may hold values from -6 to 6
- queries: bfloat16 [8, 256, 768], P('page'), may hold values from -6 to 6
- query_lengths: int32 [8], P('page'), may hold values from 1 to 256, as said below
- column_regions: int32 [8, 36], P('page'), may hold values from 0 to 2, never falling along the last dimension, each value on 1 to 18 neighbouring positions
- gain_window: bfloat16 [768], P('win'), may hold values from 0.099609375 to 1.8984375
- window_qkv: bfloat16 [768, 2304], P('win'), may hold values from -0.21875 to 0.21875
- window_out: bfloat16 [768, 768], P('win'), may hold values from -0.875 to 0.875
- position_bias: bfloat16 [12, 529], P('win'), may hold values from -4 to 4
- gain_visual: bfloat16 [768], P('win'), may hold values from 0.099609375 to 1.8984375
- gain_query: bfloat16 [768], P('win'), may hold values from 0.099609375 to 1.8984375
- attend_query: bfloat16 [768, 768], P('win'), may hold values from -0.21875 to 0.21875
- attend_kv: bfloat16 [768, 1536], P('win'), may hold values from -0.21875 to 0.21875
- attend_out: bfloat16 [768, 768], P('win'), may hold values from -1.25 to 1.25
- cross_query: bfloat16 [768, 768], P('win'), may hold values from -0.21875 to 0.21875
- cross_kv: bfloat16 [768, 1536], P('win'), may hold values from -0.21875 to 0.21875
- cross_out: bfloat16 [768, 768], P('win'), may hold values from -0.625 to 0.625
- gain_feed: bfloat16 [768], P('win'), may hold values from 0.099609375 to 1.8984375
- visual_up: bfloat16 [768, 3072], P('win'), may hold values from -0.21875 to 0.21875
- visual_down: bfloat16 [3072, 768], P('win'), may hold values from -0.15625 to 0.15625
- gain_query_feed: bfloat16 [768], P('win'), may hold values from 0.099609375 to 1.8984375
- query_up: bfloat16 [768, 3072], P('win'), may hold values from -0.21875 to 0.21875
- query_down: bfloat16 [3072, 768], P('win'), may hold values from -0.15625 to 0.15625
- cotangent_visual: bfloat16 [8, 48, 36, 768], P('page', 'win'), may hold values from -6 to 6
- cotangent_query: bfloat16 [8, 256, 768], P('page'), may hold values from -6 to 6
Outputs:
- visual_out: bfloat16 [8, 48, 36, 768], P('page', 'win')
- query_out: bfloat16 [8, 256, 768], P('page')
- visual_grad: bfloat16 [8, 48, 36, 768], P('page', 'win')
- query_grad: bfloat16 [8, 256, 768], P('page')
- grad_gain_window: float32 [768], P('win')
- grad_window_qkv: float32 [768, 2304], P('win')
- grad_window_out: float32 [768, 768], P('win')
- grad_position_bias: float32 [12, 529], P('win')
- grad_gain_visual: float32 [768], P('win')
- grad_gain_query: float32 [768], P('win')
- grad_attend_query: float32 [768, 768], P('win')
- grad_attend_kv: float32 [768, 1536], P('win')
- grad_attend_out: float32 [768, 768], P('win')
- grad_cross_query: float32 [768, 768], P('win')
- grad_cross_kv: float32 [768, 1536], P('win')
- grad_cross_out: float32 [768, 768], P('win')
- grad_gain_feed: float32 [768], P('win')
- grad_visual_up: float32 [768, 3072], P('win')
- grad_visual_down: float32 [3072, 768], P('win')
- grad_gain_query_feed: float32 [768], P('win')
- grad_query_up: float32 [768, 3072], P('win')
- grad_query_down: float32 [3072, 768], P('win')
Inputs may be any that keep to these rules, and one draw needn't show every extreme that they name: `query_lengths`: the longest page of every draw has exactly 256 live query slots. `column_regions`: region numbers never fall from left to right along a page's columns, and each of the 3 numbers covers at least one column.
All inputs are finite; a program needn't handle non-finite values.
Results may differ from a plain program's by a relative error of at most 0.02.
Values may be sent and summed in bfloat16 or wider, within the bound.
No kernel may reach another device: no remote copies, remote signals or barrier semaphores. Data moves between devices by JAX's collectives and lax.ppermute only.
A program may use at most 256 MiB of HBM per device.

v0:
```python
import jax
import jax.numpy as jnp
from jax import lax
from jax.sharding import PartitionSpec as P

HEADS = 12
WS = 12


epsilon = 1e-05
masked_fill = -1000000000.0


def padded_2(block, sides, width):
    for axis, dim in sides:
        count = lax.axis_size(axis)
        forward = [(i, i + 1) for i in range(count - 1)]
        backward = [(target, source) for source, target in forward]
        low = lax.ppermute(
            lax.slice_in_dim(block, block.shape[dim] - width, None, axis=dim), axis, forward
        )
        high = lax.ppermute(lax.slice_in_dim(block, 0, width, axis=dim), axis, backward)
        block = jnp.concatenate([low, block, high], axis=dim)
    return block


def combined_all(part, axis, combine):
    gathered = jax.tree.map(lambda a: lax.all_gather(a, axis), part)

    def take(source):
        return jax.tree.map(lambda a: lax.dynamic_index_in_dim(a, source, 0, False), gathered)

    return lax.fori_loop(
        1, lax.axis_size(axis), lambda source, state: combine(state, take(source)), take(0)
    )


def norm_apply(tensor, gain_vec):
    centre = tensor - jnp.mean(tensor, axis=-1, keepdims=True)
    spread = jnp.mean(centre * centre, axis=-1, keepdims=True)
    return centre * lax.rsqrt(spread + epsilon) * gain_vec


def norm_back(tensor, gain_vec, upstream):
    result, pullback = jax.vjp(norm_apply, tensor, gain_vec)
    return pullback(upstream)


def gelu_exact(tensor):
    return jax.nn.gelu(tensor, approximate=False)


def gelu_back(tensor, upstream):
    result, pullback = jax.vjp(gelu_exact, tensor)
    return pullback(upstream)[0]


def matmul(left_op, right_op):
    return jnp.dot(left_op, right_op, preferred_element_type=jnp.float32)


def left_tmul(left_op, right_op):
    return jnp.einsum("ni,nj->ij", left_op, right_op, preferred_element_type=jnp.float32)


def right_tmul(left_op, right_op):
    return jnp.einsum("ni,ji->nj", left_op, right_op, preferred_element_type=jnp.float32)


def split_heads(tensor):
    return tensor.reshape(tensor.shape[:-1] + (HEADS, tensor.shape[-1] // HEADS))


def to_windows(tensor, row_count):
    columns = tensor.shape[1] // WS
    shaped = tensor.reshape(2, row_count, columns, WS, tensor.shape[-1])
    return shaped.transpose(0, 2, 1, 3, 4).reshape(2, columns, row_count * WS, tensor.shape[-1])


def from_windows(tensor, row_count):
    columns = tensor.shape[1]
    shaped = tensor.reshape(2, columns, row_count, WS, tensor.shape[-1])
    return shaped.transpose(0, 2, 1, 3, 4).reshape(2 * row_count, columns * WS, tensor.shape[-1])


def offset_table():
    places = jnp.arange(WS, dtype=jnp.int32)
    offsets = places[:, None] - places[None, :] + WS - 1
    return (jnp.arange(2 * WS - 1, dtype=jnp.int32)[:, None, None] == offsets[None]).astype(
        jnp.float32
    )


def bias_expand(bias_table):
    head_count = bias_table.shape[0]
    onehot = offset_table()
    cube_view = bias_table.reshape(head_count, 2 * WS - 1, 2 * WS - 1)
    expanded = jnp.einsum(
        "hab,aij,bkl->hikjl", cube_view, onehot, onehot, precision=lax.Precision.HIGHEST
    )
    return expanded.reshape(head_count, WS * WS, WS * WS)


def bias_reduce(grad_in):
    head_count = grad_in.shape[0]
    onehot = offset_table()
    cube_view = grad_in.reshape(head_count, WS, WS, WS, WS)
    reduced = jnp.einsum(
        "hikjl,aij,bkl->hab", cube_view, onehot, onehot, precision=lax.Precision.HIGHEST
    )
    return reduced.reshape(head_count, (2 * WS - 1) ** 2)


def window_masks(regions, page_width):
    half_win = WS // 2
    first_row = lax.axis_index("win") * WS - half_win
    rows_ext = first_row + jnp.arange(2 * WS, dtype=jnp.int32)
    row_ok = (rows_ext >= 0) & (rows_ext < lax.axis_size("win") * WS)
    padded = jnp.pad(regions, (half_win, half_win), constant_values=-1)
    columns = (page_width + WS) // WS
    col_grid = (padded >= 0).reshape(columns, WS)
    region_grid = padded.reshape(columns, WS)
    key_ok = row_ok.reshape(2, WS)[:, None, :, None] & col_grid[None, :, None, :]
    key_ok = key_ok.reshape(2, columns, WS * WS)
    key_region = jnp.broadcast_to(region_grid[:, None, :], (columns, WS, WS)).reshape(
        columns, WS * WS
    )
    query_region = jnp.broadcast_to(region_grid[:, None, :], (columns, half_win, WS)).reshape(
        columns, half_win * WS
    )
    same_region = query_region[:, :, None] == key_region[:, None, :]
    return key_ok[:, :, None, :] & same_region[None]


def window_scores(query_win, key_win, bias_slots, allowed, scaling):
    scores = jnp.einsum(
        "snqhd,snkhd->snhqk", query_win, key_win, preferred_element_type=jnp.float32
    )
    scores = scores * scaling + bias_slots[:, None]
    return jnp.where(allowed[:, :, None], scores, masked_fill)


def pair_scores(query_heads, key_heads, scaling):
    return (
        jnp.einsum("qhd,khd->hqk", query_heads, key_heads, preferred_element_type=jnp.float32)
        * scaling
    )


def combine_totals(former, latter):
    peak_former, mass_former = former
    peak_latter, mass_latter = latter
    peak_both = jnp.maximum(peak_former, peak_latter)
    return (
        peak_both,
        mass_former * jnp.exp(peak_former - peak_both)
        + mass_latter * jnp.exp(peak_latter - peak_both),
    )


def body(
    visual,
    queries,
    query_lengths,
    column_regions,
    gain_window,
    window_qkv,
    window_out,
    position_bias,
    gain_visual,
    gain_query,
    attend_query,
    attend_kv,
    attend_out,
    cross_query,
    cross_kv,
    cross_out,
    gain_feed,
    visual_up,
    visual_down,
    gain_query_feed,
    query_up,
    query_down,
    cotangent_visual,
    cotangent_query,
):
    fetched = (
        lax.all_gather(gain_window, "win", axis=0, tiled=True),
        lax.all_gather(window_qkv, "win", axis=0, tiled=True),
        lax.all_gather(window_out, "win", axis=0, tiled=True),
        lax.all_gather(position_bias, "win", axis=0, tiled=True),
        lax.all_gather(gain_visual, "win", axis=0, tiled=True),
        lax.all_gather(gain_query, "win", axis=0, tiled=True),
        lax.all_gather(attend_query, "win", axis=0, tiled=True),
        lax.all_gather(attend_kv, "win", axis=0, tiled=True),
        lax.all_gather(attend_out, "win", axis=0, tiled=True),
        lax.all_gather(cross_query, "win", axis=0, tiled=True),
        lax.all_gather(cross_kv, "win", axis=0, tiled=True),
        lax.all_gather(cross_out, "win", axis=0, tiled=True),
        lax.all_gather(gain_feed, "win", axis=0, tiled=True),
        lax.all_gather(visual_up, "win", axis=0, tiled=True),
        lax.all_gather(visual_down, "win", axis=0, tiled=True),
        lax.all_gather(gain_query_feed, "win", axis=0, tiled=True),
        lax.all_gather(query_up, "win", axis=0, tiled=True),
        lax.all_gather(query_down, "win", axis=0, tiled=True),
    )
    (
        full_gain_window,
        full_window_qkv,
        full_window_out,
        full_position_bias,
        full_gain_visual,
        full_gain_query,
        full_attend_query,
        full_attend_kv,
        full_attend_out,
        full_cross_query,
        full_cross_kv,
        full_cross_out,
        full_gain_feed,
        full_visual_up,
        full_visual_down,
        full_gain_query_feed,
        full_query_up,
        full_query_down,
    ) = fetched
    half_win = WS // 2
    page_width = visual.shape[2]
    model_dim = visual.shape[3]
    query_rows = queries.shape[1]
    head_size = model_dim // HEADS
    scaling = head_size ** (-0.5)
    columns = page_width // WS + 1
    column_pad = ((0, 0), (half_win, half_win), (0, 0))
    visual_in = visual[0].astype(jnp.float32)
    query_in = queries[0].astype(jnp.float32)
    norm_own = norm_apply(visual_in, full_gain_window.astype(jnp.float32)).astype(jnp.bfloat16)
    packed_own = matmul(norm_own, full_window_qkv).astype(jnp.bfloat16)
    visual_ext = padded_2(visual[0], (("win", 0),), half_win)
    rim_rows = jnp.concatenate((visual_ext[:half_win], visual_ext[half_win + WS :]), axis=0)
    rim_norm = norm_apply(
        rim_rows.astype(jnp.float32), full_gain_window.astype(jnp.float32)
    ).astype(jnp.bfloat16)
    rim_pairs = matmul(rim_norm, full_window_qkv[:, model_dim:]).astype(jnp.bfloat16)
    pairs_ext = jnp.concatenate(
        (rim_pairs[:half_win], packed_own[..., model_dim:], rim_pairs[half_win:]), axis=0
    )
    query_win = split_heads(to_windows(jnp.pad(packed_own[..., :model_dim], column_pad), half_win))
    pairs_win = to_windows(jnp.pad(pairs_ext, column_pad), WS)
    key_win = split_heads(pairs_win[..., :model_dim])
    value_win = split_heads(pairs_win[..., model_dim:])
    allowed = window_masks(column_regions[0], page_width)
    bias_full = bias_expand(full_position_bias.astype(jnp.float32))
    bias_slots = jnp.stack((bias_full[:, half_win * WS :], bias_full[:, : half_win * WS]))
    scores_win = window_scores(query_win, key_win, bias_slots, allowed, scaling)
    peak_win = jnp.max(scores_win, axis=-1, keepdims=True)
    window_lse = peak_win + jnp.log(jnp.sum(jnp.exp(scores_win - peak_win), axis=-1, keepdims=True))
    prob_win = jnp.exp(scores_win - window_lse).astype(jnp.bfloat16)
    heads_win = jnp.einsum(
        "snhqk,snkhd->snqhd", prob_win, value_win, preferred_element_type=jnp.float32
    ).astype(jnp.bfloat16)
    heads_grid = from_windows(heads_win.reshape(2, columns, half_win * WS, model_dim), half_win)[
        :, half_win : half_win + page_width
    ]
    heads_flat = heads_grid.reshape(-1, model_dim)
    visual_mid = visual_in.reshape(-1, model_dim) + matmul(heads_flat, full_window_out)
    norm_vis = norm_apply(visual_mid, full_gain_visual.astype(jnp.float32)).astype(jnp.bfloat16)
    norm_qry = norm_apply(query_in, full_gain_query.astype(jnp.float32)).astype(jnp.bfloat16)
    attend_val = matmul(norm_qry, full_attend_query).astype(jnp.bfloat16)
    vis_pairs = matmul(norm_vis, full_attend_kv).astype(jnp.bfloat16)
    qry_pairs = matmul(norm_qry, full_attend_kv).astype(jnp.bfloat16)
    length = query_lengths[0]
    slot_ids = jnp.arange(query_rows, dtype=jnp.int32)
    live_keys = slot_ids < length
    causal = (slot_ids[None, :] <= slot_ids[:, None]) & live_keys[None, :]
    attend_heads = split_heads(attend_val)
    vis_keys = split_heads(vis_pairs[:, :model_dim])
    vis_values = split_heads(vis_pairs[:, model_dim:])
    qry_keys = split_heads(qry_pairs[:, :model_dim])
    qry_values = split_heads(qry_pairs[:, model_dim:])
    score_vis = pair_scores(attend_heads, vis_keys, scaling)
    score_qry = jnp.where(causal[None], pair_scores(attend_heads, qry_keys, scaling), masked_fill)
    peak_vis = jnp.max(score_vis, axis=-1)
    mass_vis = jnp.sum(jnp.exp(score_vis - peak_vis[..., None]), axis=-1)
    peak_all, mass_all = combined_all((peak_vis, mass_vis), "win", combine_totals)
    peak_qry = jnp.max(score_qry, axis=-1)
    mass_qry = jnp.sum(jnp.exp(score_qry - peak_qry[..., None]), axis=-1)
    peak_both, mass_both = combine_totals((peak_all, mass_all), (peak_qry, mass_qry))
    query_lse = peak_both + jnp.log(mass_both)
    prob_vis = jnp.exp(score_vis - query_lse[..., None]).astype(jnp.bfloat16)
    prob_qry = jnp.exp(score_qry - query_lse[..., None]).astype(jnp.bfloat16)
    partial_value = jnp.einsum(
        "hqk,khd->qhd", prob_vis, vis_values, preferred_element_type=jnp.float32
    ).reshape(query_rows, model_dim)
    summed = lax.psum(partial_value.astype(jnp.bfloat16), "win").astype(jnp.float32)
    own_mix = jnp.einsum(
        "hqk,khd->qhd", prob_qry, qry_values, preferred_element_type=jnp.float32
    ).reshape(query_rows, model_dim)
    heads_qry = (summed + own_mix).astype(jnp.bfloat16)
    query_mid = query_in + matmul(heads_qry, full_attend_out)
    cross_val = matmul(norm_vis, full_cross_query).astype(jnp.bfloat16)
    cross_pairs = matmul(norm_qry, full_cross_kv).astype(jnp.bfloat16)
    cross_heads_q = split_heads(cross_val)
    cross_keys = split_heads(cross_pairs[:, :model_dim])
    cross_values = split_heads(cross_pairs[:, model_dim:])
    score_cross = jnp.where(
        live_keys[None, None, :], pair_scores(cross_heads_q, cross_keys, scaling), masked_fill
    )
    peak_cross = jnp.max(score_cross, axis=-1, keepdims=True)
    cross_lse = peak_cross + jnp.log(
        jnp.sum(jnp.exp(score_cross - peak_cross), axis=-1, keepdims=True)
    )
    prob_cross = jnp.exp(score_cross - cross_lse).astype(jnp.bfloat16)
    heads_cross = jnp.einsum(
        "hvk,khd->vhd", prob_cross, cross_values, preferred_element_type=jnp.float32
    )
    heads_cross = heads_cross.reshape(-1, model_dim).astype(jnp.bfloat16)
    visual_late = visual_mid + matmul(heads_cross, full_cross_out)
    normed_feed = norm_apply(visual_late, full_gain_feed.astype(jnp.float32)).astype(jnp.bfloat16)
    hidden_vis = matmul(normed_feed, full_visual_up)
    active_vis = gelu_exact(hidden_vis).astype(jnp.bfloat16)
    visual_final = visual_late + matmul(active_vis, full_visual_down)
    normed_qfeed = norm_apply(query_mid, full_gain_query_feed.astype(jnp.float32)).astype(
        jnp.bfloat16
    )
    hidden_qry = matmul(normed_qfeed, full_query_up)
    active_qry = gelu_exact(hidden_qry).astype(jnp.bfloat16)
    query_final = query_mid + matmul(active_qry, full_query_down)
    (
        full_gain_window,
        full_window_qkv,
        full_window_out,
        full_position_bias,
        full_gain_visual,
        full_gain_query,
        full_attend_query,
        full_attend_kv,
        full_attend_out,
        full_cross_query,
        full_cross_kv,
        full_cross_out,
        full_gain_feed,
        full_visual_up,
        full_visual_down,
        full_gain_query_feed,
        full_query_up,
        full_query_down,
    ) = fetched
    grad_top_vis = cotangent_visual[0].astype(jnp.float32).reshape(-1, model_dim)
    dz_feed = grad_top_vis.astype(jnp.bfloat16)
    grad_visual_down = left_tmul(active_vis, dz_feed)
    d_hidden_vis = gelu_back(hidden_vis, right_tmul(dz_feed, full_visual_down)).astype(jnp.bfloat16)
    grad_visual_up = left_tmul(normed_feed, d_hidden_vis)
    dx_feed, grad_gain_feed = norm_back(
        visual_late, full_gain_feed.astype(jnp.float32), right_tmul(d_hidden_vis, full_visual_up)
    )
    grad_late = grad_top_vis + dx_feed
    grad_top_qry = cotangent_query[0].astype(jnp.float32)
    dz_qfeed = grad_top_qry.astype(jnp.bfloat16)
    grad_query_down = left_tmul(active_qry, dz_qfeed)
    d_hidden_qry = gelu_back(hidden_qry, right_tmul(dz_qfeed, full_query_down)).astype(jnp.bfloat16)
    grad_query_up = left_tmul(normed_qfeed, d_hidden_qry)
    dy_feed, grad_gain_query_feed = norm_back(
        query_mid, full_gain_query_feed.astype(jnp.float32), right_tmul(d_hidden_qry, full_query_up)
    )
    grad_qmid = grad_top_qry + dy_feed
    dz_cross = grad_late.astype(jnp.bfloat16)
    grad_cross_out = left_tmul(heads_cross, dz_cross)
    d_heads_cross = split_heads(right_tmul(dz_cross, full_cross_out).astype(jnp.bfloat16))
    score_cross = jnp.where(
        live_keys[None, None, :], pair_scores(cross_heads_q, cross_keys, scaling), masked_fill
    )
    prob_cross_f = jnp.exp(score_cross - cross_lse)
    dprob_cross = jnp.einsum(
        "vhd,khd->hvk", d_heads_cross, cross_values, preferred_element_type=jnp.float32
    )
    row_cross = jnp.sum(prob_cross_f * dprob_cross, axis=-1, keepdims=True)
    dscore_cross = (prob_cross_f * (dprob_cross - row_cross)).astype(jnp.bfloat16)
    dq_cross = (
        jnp.einsum(
            "hvk,khd->vhd", dscore_cross, cross_keys, preferred_element_type=jnp.float32
        ).reshape(-1, model_dim)
        * scaling
    ).astype(jnp.bfloat16)
    dk_cross = (
        jnp.einsum(
            "hvk,vhd->khd", dscore_cross, cross_heads_q, preferred_element_type=jnp.float32
        ).reshape(query_rows, model_dim)
        * scaling
    )
    dv_cross = jnp.einsum(
        "hvk,vhd->khd",
        prob_cross_f.astype(jnp.bfloat16),
        d_heads_cross,
        preferred_element_type=jnp.float32,
    ).reshape(query_rows, model_dim)
    dz_attend = grad_qmid.astype(jnp.bfloat16)
    grad_attend_out = left_tmul(heads_qry, dz_attend)
    d_heads_qry = split_heads(right_tmul(dz_attend, full_attend_out).astype(jnp.bfloat16))
    prob_vis_f = jnp.exp(pair_scores(attend_heads, vis_keys, scaling) - query_lse[..., None])
    score_qry = jnp.where(causal[None], pair_scores(attend_heads, qry_keys, scaling), masked_fill)
    prob_qry_f = jnp.exp(score_qry - query_lse[..., None])
    dprob_vis = jnp.einsum(
        "qhd,khd->hqk", d_heads_qry, vis_values, preferred_element_type=jnp.float32
    )
    dprob_qry = jnp.einsum(
        "qhd,khd->hqk", d_heads_qry, qry_values, preferred_element_type=jnp.float32
    )
    row_part = jnp.sum(prob_vis_f * dprob_vis, axis=-1)
    row_total = lax.psum(row_part, "win") + jnp.sum(prob_qry_f * dprob_qry, axis=-1)
    dscore_vis = (prob_vis_f * (dprob_vis - row_total[..., None])).astype(jnp.bfloat16)
    dscore_qry = (prob_qry_f * (dprob_qry - row_total[..., None])).astype(jnp.bfloat16)
    dq_part = (
        jnp.einsum(
            "hqk,khd->qhd", dscore_vis, vis_keys, preferred_element_type=jnp.float32
        ).reshape(query_rows, model_dim)
        * scaling
    )
    dq_local = (
        jnp.einsum(
            "hqk,khd->qhd", dscore_qry, qry_keys, preferred_element_type=jnp.float32
        ).reshape(query_rows, model_dim)
        * scaling
    )
    dk_vis = (
        jnp.einsum(
            "hqk,qhd->khd", dscore_vis, attend_heads, preferred_element_type=jnp.float32
        ).reshape(-1, model_dim)
        * scaling
    )
    dv_vis = jnp.einsum(
        "hqk,qhd->khd",
        prob_vis_f.astype(jnp.bfloat16),
        d_heads_qry,
        preferred_element_type=jnp.float32,
    ).reshape(-1, model_dim)
    dpairs_vis = jnp.concatenate((dk_vis, dv_vis), axis=-1).astype(jnp.bfloat16)
    dk_qry = (
        jnp.einsum(
            "hqk,qhd->khd", dscore_qry, attend_heads, preferred_element_type=jnp.float32
        ).reshape(query_rows, model_dim)
        * scaling
    )
    dv_qry = jnp.einsum(
        "hqk,qhd->khd",
        prob_qry_f.astype(jnp.bfloat16),
        d_heads_qry,
        preferred_element_type=jnp.float32,
    ).reshape(query_rows, model_dim)
    dpairs_qry = jnp.concatenate((dk_qry, dv_qry), axis=-1).astype(jnp.bfloat16)
    dq_sum, dcross_sum = (
        lax.psum(dq_part.astype(jnp.bfloat16), "win").astype(jnp.float32),
        lax.psum(jnp.concatenate((dk_cross, dv_cross), axis=-1).astype(jnp.bfloat16), "win").astype(
            jnp.float32
        ),
    )
    dq_attend = (dq_sum + dq_local).astype(jnp.bfloat16)
    dpairs_cross = dcross_sum.astype(jnp.bfloat16)
    grad_attend_query = left_tmul(norm_qry, dq_attend)
    grad_cross_kv = left_tmul(norm_qry, dpairs_cross)
    grad_cross_query = left_tmul(norm_vis, dq_cross)
    inverse = 1.0 / lax.axis_size("win")
    grad_attend_kv = left_tmul(norm_vis, dpairs_vis) + left_tmul(norm_qry, dpairs_qry) * inverse
    d_norm_qry = (
        right_tmul(dq_attend, full_attend_query)
        + right_tmul(dpairs_qry, full_attend_kv)
        + right_tmul(dpairs_cross, full_cross_kv)
    )
    dy_norm, grad_gain_query = norm_back(query_in, full_gain_query.astype(jnp.float32), d_norm_qry)
    query_back = (grad_qmid + dy_norm).astype(jnp.bfloat16)
    d_norm_vis = right_tmul(dq_cross, full_cross_query) + right_tmul(dpairs_vis, full_attend_kv)
    dx_norm, grad_gain_visual = norm_back(
        visual_mid, full_gain_visual.astype(jnp.float32), d_norm_vis
    )
    grad_mid = grad_late + dx_norm
    dz_window = grad_mid.astype(jnp.bfloat16)
    grad_window_out = left_tmul(heads_flat, dz_window)
    d_heads_grid = (
        right_tmul(dz_window, full_window_out)
        .astype(jnp.bfloat16)
        .reshape(WS, page_width, model_dim)
    )
    d_heads_win = split_heads(to_windows(jnp.pad(d_heads_grid, column_pad), half_win))
    scores_win = window_scores(query_win, key_win, bias_slots, allowed, scaling)
    prob_win_f = jnp.exp(scores_win - window_lse)
    dprob_win = jnp.einsum(
        "snqhd,snkhd->snhqk", d_heads_win, value_win, preferred_element_type=jnp.float32
    )
    row_win = jnp.sum(prob_win_f * dprob_win, axis=-1, keepdims=True)
    dscore_win = (prob_win_f * (dprob_win - row_win)).astype(jnp.bfloat16)
    slot_sums = jnp.sum(dscore_win.astype(jnp.float32), axis=1)
    grad_position_bias = bias_reduce(jnp.concatenate((slot_sums[1], slot_sums[0]), axis=1))
    dq_win = (
        jnp.einsum("snhqk,snkhd->snqhd", dscore_win, key_win, preferred_element_type=jnp.float32)
        * scaling
    )
    dk_win = (
        jnp.einsum("snhqk,snqhd->snkhd", dscore_win, query_win, preferred_element_type=jnp.float32)
        * scaling
    )
    dv_win = jnp.einsum(
        "snhqk,snqhd->snkhd",
        prob_win_f.astype(jnp.bfloat16),
        d_heads_win,
        preferred_element_type=jnp.float32,
    )
    dq_grid = from_windows(dq_win.reshape(2, columns, half_win * WS, model_dim), half_win)[
        :, half_win : half_win + page_width
    ]
    dpairs_win = jnp.concatenate(
        (
            dk_win.reshape(2, columns, WS * WS, model_dim),
            dv_win.reshape(2, columns, WS * WS, model_dim),
        ),
        axis=-1,
    )
    dpairs_grid = from_windows(dpairs_win, WS)[:, half_win : half_win + page_width]
    outgoing = jnp.concatenate((dpairs_grid[:half_win], dpairs_grid[half_win + WS :]), axis=0)
    incoming = padded_2(outgoing.astype(jnp.bfloat16), (("win", 0),), half_win).astype(
        outgoing.dtype
    )
    dpairs_own = dpairs_grid[half_win : half_win + WS] + jnp.concatenate(
        (incoming[:half_win], incoming[half_win + WS :]), axis=0
    )
    d_packed = (
        jnp.concatenate((dq_grid, dpairs_own), axis=-1)
        .astype(jnp.bfloat16)
        .reshape(-1, 3 * model_dim)
    )
    grad_window_qkv = left_tmul(norm_own.reshape(-1, model_dim), d_packed)
    dx_window, grad_gain_window = norm_back(
        visual_in.reshape(-1, model_dim),
        full_gain_window.astype(jnp.float32),
        right_tmul(d_packed, full_window_qkv),
    )
    visual_back = (grad_mid + dx_window).astype(jnp.bfloat16)
    shares = (
        lax.psum_scatter(
            grad_gain_window.astype(jnp.bfloat16), "win", scatter_dimension=0, tiled=True
        ).astype(jnp.float32),
        lax.psum_scatter(
            grad_window_qkv.astype(jnp.bfloat16), "win", scatter_dimension=0, tiled=True
        ).astype(jnp.float32),
        lax.psum_scatter(
            grad_window_out.astype(jnp.bfloat16), "win", scatter_dimension=0, tiled=True
        ).astype(jnp.float32),
        lax.psum_scatter(
            grad_position_bias.astype(jnp.bfloat16), "win", scatter_dimension=0, tiled=True
        ).astype(jnp.float32),
        lax.psum_scatter(
            grad_gain_visual.astype(jnp.bfloat16), "win", scatter_dimension=0, tiled=True
        ).astype(jnp.float32),
        lax.psum_scatter(
            (grad_gain_query * inverse).astype(jnp.bfloat16), "win", scatter_dimension=0, tiled=True
        ).astype(jnp.float32),
        lax.psum_scatter(
            (grad_attend_query * inverse).astype(jnp.bfloat16),
            "win",
            scatter_dimension=0,
            tiled=True,
        ).astype(jnp.float32),
        lax.psum_scatter(
            grad_attend_kv.astype(jnp.bfloat16), "win", scatter_dimension=0, tiled=True
        ).astype(jnp.float32),
        lax.psum_scatter(
            (grad_attend_out * inverse).astype(jnp.bfloat16), "win", scatter_dimension=0, tiled=True
        ).astype(jnp.float32),
        lax.psum_scatter(
            grad_cross_query.astype(jnp.bfloat16), "win", scatter_dimension=0, tiled=True
        ).astype(jnp.float32),
        lax.psum_scatter(
            (grad_cross_kv * inverse).astype(jnp.bfloat16), "win", scatter_dimension=0, tiled=True
        ).astype(jnp.float32),
        lax.psum_scatter(
            grad_cross_out.astype(jnp.bfloat16), "win", scatter_dimension=0, tiled=True
        ).astype(jnp.float32),
        lax.psum_scatter(
            grad_gain_feed.astype(jnp.bfloat16), "win", scatter_dimension=0, tiled=True
        ).astype(jnp.float32),
        lax.psum_scatter(
            grad_visual_up.astype(jnp.bfloat16), "win", scatter_dimension=0, tiled=True
        ).astype(jnp.float32),
        lax.psum_scatter(
            grad_visual_down.astype(jnp.bfloat16), "win", scatter_dimension=0, tiled=True
        ).astype(jnp.float32),
        lax.psum_scatter(
            (grad_gain_query_feed * inverse).astype(jnp.bfloat16),
            "win",
            scatter_dimension=0,
            tiled=True,
        ).astype(jnp.float32),
        lax.psum_scatter(
            (grad_query_up * inverse).astype(jnp.bfloat16), "win", scatter_dimension=0, tiled=True
        ).astype(jnp.float32),
        lax.psum_scatter(
            (grad_query_down * inverse).astype(jnp.bfloat16), "win", scatter_dimension=0, tiled=True
        ).astype(jnp.float32),
    )
    totals = lax.psum(
        (
            shares[0],
            shares[1],
            shares[2],
            shares[3],
            shares[4],
            shares[5],
            shares[6],
            shares[7],
            shares[8],
            shares[9],
            shares[10],
            shares[11],
            shares[12],
            shares[13],
            shares[14],
            shares[15],
            shares[16],
            shares[17],
        ),
        "page",
    )
    return (
        visual_final.reshape(1, WS, page_width, model_dim).astype(jnp.bfloat16),
        query_final.reshape(1, query_rows, model_dim).astype(jnp.bfloat16),
        visual_back.reshape(1, WS, page_width, model_dim),
        query_back.reshape(1, query_rows, model_dim),
        totals[0],
        totals[1],
        totals[2],
        totals[3],
        totals[4],
        totals[5],
        totals[6],
        totals[7],
        totals[8],
        totals[9],
        totals[10],
        totals[11],
        totals[12],
        totals[13],
        totals[14],
        totals[15],
        totals[16],
        totals[17],
    )


def solution(mesh):
    return jax.shard_map(
        body,
        mesh=mesh,
        in_specs=(
            P("page", "win", None, None),
            P("page", None, None),
            P("page"),
            P("page", None),
            P("win"),
            P("win", None),
            P("win", None),
            P("win", None),
            P("win"),
            P("win"),
            P("win", None),
            P("win", None),
            P("win", None),
            P("win", None),
            P("win", None),
            P("win", None),
            P("win"),
            P("win", None),
            P("win", None),
            P("win"),
            P("win", None),
            P("win", None),
            P("page", "win", None, None),
            P("page", None, None),
        ),
        out_specs=(
            P("page", "win", None, None),
            P("page", None, None),
            P("page", "win", None, None),
            P("page", None, None),
            P("win"),
            P("win", None),
            P("win", None),
            P("win", None),
            P("win"),
            P("win"),
            P("win", None),
            P("win", None),
            P("win", None),
            P("win", None),
            P("win", None),
            P("win", None),
            P("win"),
            P("win", None),
            P("win", None),
            P("win"),
            P("win", None),
            P("win", None),
        ),
        check_vma=False,
    )
```

profile of v0, /device:TPU:0, one launch (start us, length us, event | category | flops | bytes accessed | tf_op | source)
XLA Modules:
  0.0 1619.2 jit_solution(15507496015413056560)
XLA Ops:
  21.3 14.8 all-reduce.17
  43.2 9.1 convolution_bitcast_fusion
  52.3 17.3 %copy.147 = f32[12,12,12,12,12]{4,3,2,1,0:T(8,128)} copy(f32[12,12,12,12,12]{4,0,2,3,1:T(8,128)} %convolution_bitcast_fusion) | data formatting | bytes 1990656 | tf_op jit(solution)/shard_map/hab,aij,bkl->hikjl/transpose | solution.py:98
  69.7 9.5 reshape.491
  262.6 14.7 all-gather.36.cloned.1.call-done
  281.5 34.7 %all-gather.38.cloned.1.call-done = bf16[768,3072]{1,0:T(8,128)(2,1)} async-done(((bf16[192,3072]{1,0:T(8,128)(2,1)}), bf16[768,3072]{1,0:T(8,128)(2,1)}) %all-gather.38.cloned.1.call-update) | async-done | bytes 4718608 | tf_op jit(solution)/shard_map/all_gather | solution.py:204
  316.2 12.2 multiply_convert_fusion.8
  328.4 27.0 %all-gather.40.cloned.1.call-done = bf16[3072,768]{1,0:T(8,128)(2,1)} async-done(((bf16[768,768]{1,0:T(8,128)(2,1)}), bf16[3072,768]{1,0:T(8,128)(2,1)}) %all-gather.40.cloned.1.call-update) | async-done | bytes 4718608 | tf_op jit(solution)/shard_map/all_gather | solution.py:205
  368.6 7.1 multiply_reduce_fusion.1
  375.7 12.5 psum.155
  402.6 7.5 fusion.127
  410.2 23.6 %all-gather.30.cloned.1.call-done = bf16[3072,768]{1,0:T(8,128)(2,1)} async-done(((bf16[768,768]{1,0:T(8,128)(2,1)}), bf16[3072,768]{1,0:T(8,128)(2,1)}) %all-gather.30.cloned.1.call-update) | async-done | bytes 4718608 | tf_op jit(solution)/shard_map/all_gather | solution.py:202
  433.8 16.5 %add_convert_fusion = (bf16[432,3072]{1,0:T(8,128)(2,1)S(1)}, f32[432,3072]{1,0:T(8,128)}) fusion(f32[432,3072]{1,0:T(8,128)} %fusion.127, bf16[432,768]{1,0:T(8,128)(2,1)S(1)} %copy-done.35, bf16[3072,768]{1,0:T(8,128)(2,1)} %all-gather.30.cloned.1.call-done), kind=kOutput, calls=%fused_computation.27 | convolution fusion | flops 2133983232 | bytes 18653184 | tf_op jit(solution)/shard_map/ni,ji->nj/dot_general | solution.py:67
  494.8 19.2 %all-reduce.25.cloned.1.call-done = (bf16[256,768]{0,1:T(8,128)(2,1)}, bf16[256,1536]{0,1:T(8,128)(2,1)}) async-done(((bf16[256,768]{0,1:T(8,128)(2,1)}, bf16[256,1536]{0,1:T(8,128)(2,1)}), (bf16[256,768]{0,1:T(8,128)(2,1)}, bf16[256,1536]{0,1:T(8,128)(2,1)})) %all-reduce.25.cloned.1.call-update) | async-done | bytes 1179664 | tf_op jit(solution)/shard_map/psum | solution.py:452
  543.5 10.3 copy.168
  553.8 8.6 concatenate.55
  562.4 7.7 multiply_reduce_fusion
  573.1 7.8 convert_reduce_fusion
  584.5 10.2 copy.166
  594.7 8.5 concatenate.54
  603.1 8.1 maximum_bitcast_fusion
  611.2 9.4 copy.169
  620.6 9.2 reshape.509
  703.1 8.5 reshape.514
  711.6 14.5 convolution_bitcast_fusion.2
  745.5 14.4 all-reduce.16
  760.3 13.9 reduce-scatter.13.cloned.1.call-done
  774.2 50.5 %reduce-scatter.29.cloned.1.call-done = bf16[192,3072]{1,0:T(8,128)(2,1)} async-done(((bf16[768,3072]{1,0:T(8,128)(2,1)}), bf16[192,3072]{1,0:T(8,128)(2,1)}) %reduce-scatter.29.cloned.1.call-update) | async-done | bytes 1179664 | tf_op jit(solution)/shard_map/reduce_scatter | solution.py:580
  824.7 50.2 %reduce-scatter.31.cloned.1.call-done = bf16[768,768]{1,0:T(8,128)(2,1)} async-done(((bf16[3072,768]{1,0:T(8,128)(2,1)}), bf16[768,768]{1,0:T(8,128)(2,1)}) %reduce-scatter.31.cloned.1.call-update) | async-done | bytes 1179664 | tf_op jit(solution)/shard_map/reduce_scatter | solution.py:583
  874.9 50.6 %reduce-scatter.33.cloned.1.call-done = bf16[192,3072]{1,0:T(8,128)(2,1)} async-done(((bf16[768,3072]{1,0:T(8,128)(2,1)}), bf16[192,3072]{1,0:T(8,128)(2,1)}) %reduce-scatter.33.cloned.1.call-update) | async-done | bytes 1179664 | tf_op jit(solution)/shard_map/reduce_scatter | solution.py:592
  925.5 50.3 %reduce-scatter.35.cloned.1.call-done = bf16[768,768]{1,0:T(8,128)(2,1)} async-done(((bf16[3072,768]{1,0:T(8,128)(2,1)}), bf16[768,768]{1,0:T(8,128)(2,1)}) %reduce-scatter.35.cloned.1.call-update) | async-done | bytes 1179664 | tf_op jit(solution)/shard_map/reduce_scatter | solution.py:595
  975.8 636.6 %all-reduce.26 = (f32[192]{0:T(256)}, f32[192,2304]{1,0:T(8,128)}, f32[192,768]{1,0:T(8,128)}, f32[3,529]{1,0:T(4,128)}, f32[192]{0:T(256)}, /*index=5*/f32[192]...) all-reduce(f32[192]{0:T(256)S(1)} %dynamic-slice_convert_fusion.5, ...), channel_id=1, replica_groups=mesh['page'=8,'win'=4] {'page'}, use_global_device_ids=true, to_apply=%region_43.44 | all-reduce | flops 4131315 | bytes 24792984 | tf_op jit(solution)/shard_map/psum | solution.py:599
  (638 shorter events, 409.2 us)
Async XLA Ops:
  7.2 82.5 %all-gather.34.cloned.1.call-start = ((), (), s32[]{:S(2)}) async-start(), calls=%async_computation.20 | async-start | bytes 1474560 | tf_op jit(solution)/shard_map/all_gather | solution.py:194
  7.9 84.5 %all-gather.32.cloned.1.call-start = ((), (), s32[]{:S(2)}) async-start(), calls=%async_computation.19 | async-start | bytes 2949120 | tf_op jit(solution)/shard_map/all_gather | solution.py:195
  8.8 92.5 %all-gather.18.cloned.1.call-start = ((), (), s32[]{:S(2)}) async-start(), calls=%async_computation.12 | async-start | bytes 4423680 | tf_op jit(solution)/shard_map/all_gather | solution.py:189
  9.5 177.6 %all-gather.20.cloned.1.call-start = ((), (), s32[]{:S(2)}) async-start(), calls=%async_computation.13 | async-start | bytes 1474560 | tf_op jit(solution)/shard_map/all_gather | solution.py:190
  10.1 222.0 %all-gather.22.cloned.1.call-start = ((), (), s32[]{:S(2)}) async-start(), calls=%async_computation.14 | async-start | bytes 2949120 | tf_op jit(solution)/shard_map/all_gather | solution.py:198
  10.7 230.7 %all-gather.24.cloned.1.call-start = ((), (), s32[]{:S(2)}) async-start(), calls=%async_computation.15 | async-start | bytes 1474560 | tf_op jit(solution)/shard_map/all_gather | solution.py:197
  11.2 242.8 %all-gather.26.cloned.1.call-start = ((), (), s32[]{:S(2)}) async-start(), calls=%async_computation.16 | async-start | bytes 1474560 | tf_op jit(solution)/shard_map/all_gather | solution.py:199
  12.2 74.1 %collective-permute-start.1 = (bf16[6,36,768]{2,1,0:T(8,128)(2,1)}, bf16[6,36,768]{2,1,0:T(8,128)(2,1)S(1)}, u32[]{:S(2)}, u32[]{:S(2)}) collective-permute-start(bf16[6,36,768]{2,1,0:T(8,128)(2,1)} %get-tuple-element.243), channel_id=1, source_target_pairs={{1,0},{2,1},{3,2},{5,4},{6,5},{7,6},{9,8},{10,9},{11,10},{13,12},{... | collective-permute-start | bytes 995336 | tf_op jit(solution)/shard_map/ppermute | solution.py:22
  13.5 72.9 %collective-permute-start = (bf16[6,36,768]{2,1,0:T(8,128)(2,1)}, bf16[6,36,768]{2,1,0:T(8,128)(2,1)}, u32[]{:S(2)}, u32[]{:S(2)}) collective-permute-start(bf16[6,36,768]{2,1,0:T(8,128)(2,1)} %get-tuple-element.242), channel_id=1, source_target_pairs={{0,1},{1,2},{2,3},{4,5},{5,6},{6,7},{8,9},{9,10},{10,11},{12,13},{... | collective-permute-start | bytes 995336 | tf_op jit(solution)/shard_map/ppermute | solution.py:19
  17.3 243.2 %all-reduce.23.cloned.1.call-start = ((), (), s32[]{:S(2)}) async-start(), calls=%async_computation.21 | async-start | bytes 786432 | tf_op jit(solution)/shard_map/psum | solution.py:295
  82.2 108.1 %copy-start.100 = (f32[768]{0:T(1024)}, f32[768]{0:T(1024)S(1)}, u32[]{:S(2)}) copy-start(f32[768]{0:T(1024)S(1)} %convert_element_type.384) | copy-start | bytes 9220
  98.5 289.7 %copy-start.3 = (f32[12,256,256]{1,2,0:T(8,128)}, f32[12,256,256]{1,2,0:T(8,128)S(1)}, u32[]{:S(2)}) copy-start(f32[12,256,256]{1,2,0:T(8,128)S(1)} %get-tuple-element.255) | copy-start | bytes 9437188
  223.9 53.4 %all-gather.36.cloned.1.call-start = ((), (), s32[]{:S(2)}) async-start(), calls=%async_computation.22 | async-start | bytes 1474560 | tf_op jit(solution)/shard_map/all_gather | solution.py:196
  224.6 91.6 %all-gather.38.cloned.1.call-start = ((), (), s32[]{:S(2)}) async-start(), calls=%async_computation.23 | async-start | bytes 5898240 | tf_op jit(solution)/shard_map/all_gather | solution.py:204
  225.2 130.2 %all-gather.40.cloned.1.call-start = ((), (), s32[]{:S(2)}) async-start(), calls=%async_computation.24 | async-start | bytes 5898240 | tf_op jit(solution)/shard_map/all_gather | solution.py:205
  225.9 176.7 %all-gather.28.cloned.1.call-start = ((), (), s32[]{:S(2)}) async-start(), calls=%async_computation.17 | async-start | bytes 5898240 | tf_op jit(solution)/shard_map/all_gather | solution.py:201
  226.5 207.2 %all-gather.30.cloned.1.call-start = ((), (), s32[]{:S(2)}) async-start(), calls=%async_computation.18 | async-start | bytes 5898240 | tf_op jit(solution)/shard_map/all_gather | solution.py:202
  227.3 286.7 %all-reduce.25.cloned.1.call-start = ((), (), s32[]{:S(2)}) async-start(), calls=%async_computation.37 | async-start | bytes 2359296 | tf_op jit(solution)/shard_map/psum | solution.py:452
  476.4 283.8 %reduce-scatter.15.cloned.1.call-start = ((), (), s32[]{:S(2)}) async-start(), calls=%async_computation.26 | async-start | bytes 1474560 | tf_op jit(solution)/shard_map/reduce_scatter | solution.py:544
  482.2 277.9 %reduce-scatter.21.cloned.1.call-start = ((), (), s32[]{:S(2)}) async-start(), calls=%async_computation.29 | async-start | bytes 1474560 | tf_op jit(solution)/shard_map/reduce_scatter | solution.py:565
  484.1 276.1 %reduce-scatter.23.cloned.1.call-start = ((), (), s32[]{:S(2)}) async-start(), calls=%async_computation.30 | async-start | bytes 1474560 | tf_op jit(solution)/shard_map/reduce_scatter | solution.py:568
  486.1 274.2 %reduce-scatter.27.cloned.1.call-start = ((), (), s32[]{:S(2)}) async-start(), calls=%async_computation.32 | async-start | bytes 1474560 | tf_op jit(solution)/shard_map/reduce_scatter | solution.py:574
  489.5 270.8 %reduce-scatter.17.cloned.1.call-start = ((), (), s32[]{:S(2)}) async-start(), calls=%async_computation.27 | async-start | bytes 1474560 | tf_op jit(solution)/shard_map/reduce_scatter | solution.py:556
  518.4 241.8 %reduce-scatter.19.cloned.1.call-start = ((), (), s32[]{:S(2)}) async-start(), calls=%async_computation.28 | async-start | bytes 2949120 | tf_op jit(solution)/shard_map/reduce_scatter | solution.py:562
  526.8 233.5 %reduce-scatter.25.cloned.1.call-start = ((), (), s32[]{:S(2)}) async-start(), calls=%async_computation.31 | async-start | bytes 2949120 | tf_op jit(solution)/shard_map/reduce_scatter | solution.py:571
  572.6 201.7 %reduce-scatter.13.cloned.1.call-start = ((), (), s32[]{:S(2)}) async-start(), calls=%async_computation.25 | async-start | bytes 4423680 | tf_op jit(solution)/shard_map/reduce_scatter | solution.py:541
  635.0 14.1 collective-permute-start.3
  636.3 12.8 collective-permute-start.2
  659.1 165.6 %reduce-scatter.29.cloned.1.call-start = ((), (), s32[]{:S(2)}) async-start(), calls=%async_computation.33 | async-start | bytes 5898240 | tf_op jit(solution)/shard_map/reduce_scatter | solution.py:580
  666.7 208.3 %reduce-scatter.31.cloned.1.call-start = ((), (), s32[]{:S(2)}) async-start(), calls=%async_computation.34 | async-start | bytes 5898240 | tf_op jit(solution)/shard_map/reduce_scatter | solution.py:583
  678.7 246.8 %reduce-scatter.33.cloned.1.call-start = ((), (), s32[]{:S(2)}) async-start(), calls=%async_computation.35 | async-start | bytes 5898240 | tf_op jit(solution)/shard_map/reduce_scatter | solution.py:592
  685.0 290.8 %reduce-scatter.35.cloned.1.call-start = ((), (), s32[]{:S(2)}) async-start(), calls=%async_computation.36 | async-start | bytes 5898240 | tf_op jit(solution)/shard_map/reduce_scatter | solution.py:595
  (161 other events, 952.0 us)
Sparse Core Ops, SparseCore 0:
  9.6 21.0 all-gather.33
  32.2 26.3 all-gather.31
  60.2 30.7 all-gather.17
  92.5 17.4 all-gather.19
  111.4 24.0 all-gather.21
  136.9 17.4 all-gather.23
  155.9 17.4 all-gather.25
  224.0 34.0 all-reduce.22
  259.8 17.4 all-gather.35
  278.7 37.4 all-gather.37
  317.9 37.4 all-gather.39
  356.9 37.7 all-gather.27
  396.3 37.4 all-gather.29
  476.5 37.4 all-reduce.24
  517.1 25.7 reduce-scatter.14
  545.4 25.7 reduce-scatter.20
  573.7 25.6 reduce-scatter.22
  601.9 25.7 reduce-scatter.26
  631.0 25.7 reduce-scatter.16
  659.7 34.5 reduce-scatter.18
  697.5 33.0 reduce-scatter.24
  733.2 40.9 reduce-scatter.12
  776.9 47.7 reduce-scatter.28
  827.1 47.8 reduce-scatter.30
  877.6 47.8 reduce-scatter.32
  927.9 47.8 reduce-scatter.34
where the time goes:
time: 1630 us; the launch traced here: 1620 us
  blocking collectives  695 us (43%)
  waiting for transfers between devices  342 us (21%)
  matrix products  240 us (15%)
  local copies, waits for them, and re-layouts  229 us (14%)
  other arithmetic  81.8 us (5%)
  between operations  19.3 us (1%)
    psum x1, blocking collectives, body(): lax.psum((shares[0], shares[1], shares[2], shares[3], shares[4], shares[5...  637 us
    dot_general x14, matrix products, matmul(): return jnp.dot(left_op, right_op, preferred_element_type=jnp.float32)  55.2 us
    reduce_scatter x1, waiting for transfers between devices, body(): lax.psum_scatter((grad_query_up * inverse).astype(jnp.bfloat16), 'win', s...  50.6 us
    reduce_scatter x1, waiting for transfers between devices, body(): lax.psum_scatter(grad_visual_up.astype(jnp.bfloat16), 'win', scatter_dime...  50.5 us
    reduce_scatter x1, waiting for transfers between devices, body(): lax.psum_scatter((grad_query_down * inverse).astype(jnp.bfloat16), 'win',...  50.3 us
    reduce_scatter x1, waiting for transfers between devices, body(): lax.psum_scatter(grad_visual_down.astype(jnp.bfloat16), 'win', scatter_di...  50.2 us
    dot_general x13, matrix products, left_tmul(): jnp.einsum('ni,nj->ij', left_op, right_op, preferred_element_type=jnp.flo...  43.3 us
    dot_general x13, matrix products, right_tmul(): jnp.einsum('ni,ji->nj', left_op, right_op, preferred_element_type=jnp.flo...  42.7 us
  transfers between devices with their start and end apart: 30, of which 10 were waited for; matrix products, arithmetic and copies ran while one was open for 30% of the time, Pallas kernels for 0%

commit v1 on v0

v1 whole, which is shorter than its diff:
```python
import functools

import jax
import jax.numpy as jnp
import numpy as np
from jax import lax
from jax.experimental import pallas as pl
from jax.experimental.pallas import tpu as pltpu
from jax.sharding import PartitionSpec as P

HEADS = 12
WS = 12
SPAN = 2 * WS - 1
LANES = 256

epsilon = 1e-05
masked_fill = -1000000000.0
bf16 = jnp.bfloat16
f32 = jnp.float32
VMEM_BYTES = 48 * 1024 * 1024


def swap(tensor, axis, bit):
    count = lax.axis_size(axis)
    return lax.ppermute(tensor, axis, [(i, i ^ bit) for i in range(count)])


def bits_of(count):
    bits = []
    while count > 1:
        count //= 2
        bits.append(count)
    return bits


def gather_blocks(block, axis="win"):
    for bit in bits_of(lax.axis_size(axis)):
        block = jnp.concatenate([block, swap(block, axis, bit)], axis=0)
    return block


def scatter_sum(parts, axis="win"):
    bits = bits_of(lax.axis_size(axis))
    for bit in reversed(bits):
        half = parts.shape[0] // 2
        arrived = swap(parts[half:].astype(bf16), axis, bit)
        parts = parts[:half].astype(f32) + arrived.astype(f32)
    return parts


def total_sum(part, axis="win"):
    for bit in reversed(bits_of(lax.axis_size(axis))):
        mine = lax.reduce_precision(part.astype(f32), 8, 7)
        part = mine + swap(mine.astype(bf16), axis, bit).astype(f32)
    return part


def tiny_sum(part, axes):
    for axis in axes:
        for bit in reversed(bits_of(lax.axis_size(axis))):
            part = part + swap(part, axis, bit)
    return part


def pick(stack, index):
    return lax.dynamic_index_in_dim(stack, index, 0, False)


def trade(stack, axis="win"):
    count = lax.axis_size(axis)
    me = lax.axis_index(axis)
    return [pick(stack, me)] + [swap(pick(stack, me ^ k), axis, k) for k in range(1, count)]


def in_order(blocks, axis="win"):
    me = lax.axis_index(axis)
    stack = jnp.stack(blocks) if isinstance(blocks, (list, tuple)) else blocks
    return [pick(stack, me ^ j) for j in range(lax.axis_size(axis))]


def xor_order(count):
    order = [0]
    for bit in bits_of(count):
        order = order + [k ^ bit for k in order]
    return order


def rounded(tensor):
    return lax.reduce_precision(tensor, 8, 7)


def add_low(left, right):
    return rounded(left.astype(f32) + right.astype(f32)).astype(bf16)


def line_pairs(pairs):
    return [(2 * a + x, 2 * b + x) for a, b in pairs for x in (0, 1)]


INWARD = line_pairs([(0, 1), (3, 2)])
MIDDLE = line_pairs([(1, 2), (2, 1)])
OUTWARD = line_pairs([(1, 0), (2, 3)])
SIDE = [(i, i ^ 1) for i in range(8)]
MIDDLE_SIDE = [(i, i ^ 1) for i in range(2, 6)]


def page_total_across(tensor):
    half = tensor.shape[0] // 2
    me = lax.axis_index("page")
    side, depth = me % 2, me // 2
    stack = tensor.reshape((2, half) + tensor.shape[1:])
    own = add_low(pick(stack, side), lax.ppermute(pick(stack, 1 - side), "page", SIDE))
    own = add_low(own, lax.ppermute(own, "page", INWARD))
    own = add_low(own, lax.ppermute(own, "page", MIDDLE))
    outer = (depth == 0) | (depth == 3)
    own = jnp.where(outer, lax.ppermute(own, "page", OUTWARD), own)
    other = lax.ppermute(own, "page", SIDE)
    first = side == 0
    return jnp.concatenate([jnp.where(first, own, other), jnp.where(first, other, own)], axis=0)


def page_total_along(tensor):
    half = tensor.shape[0] // 2
    depth = lax.axis_index("page") // 2
    own = add_low(tensor, lax.ppermute(tensor, "page", INWARD))
    stack = own.reshape((2, half) + tensor.shape[1:])
    low = depth < 2
    keep = jnp.where(low, stack[0], stack[1])
    give = jnp.where(low, stack[1], stack[0])
    keep = add_low(keep, lax.ppermute(give, "page", MIDDLE))
    keep = add_low(keep, lax.ppermute(keep, "page", MIDDLE_SIDE))
    other = lax.ppermute(keep, "page", MIDDLE)
    full = jnp.concatenate([jnp.where(low, keep, other), jnp.where(low, other, keep)], axis=0)
    outer = (depth == 0) | (depth == 3)
    return jnp.where(outer, lax.ppermute(full, "page", OUTWARD), full)


def page_total(across, along):
    if lax.axis_size("page") == 8:
        return page_total_across(across), page_total_along(along)
    return lax.psum(across, "page"), lax.psum(along, "page")


def normalise(tensor):
    centre = tensor - jnp.mean(tensor, axis=-1, keepdims=True)
    spread = lax.rsqrt(jnp.mean(centre * centre, axis=-1, keepdims=True) + epsilon)
    return centre * spread, spread


def norm_low(tensor, gain):
    return (normalise(tensor)[0] * gain).astype(bf16)


def norm_back(tensor, gain, upstream):
    unit, spread = normalise(tensor)
    scaled = upstream * gain
    return spread * (
        scaled
        - jnp.mean(scaled, axis=-1, keepdims=True)
        - unit * jnp.mean(scaled * unit, axis=-1, keepdims=True)
    )


def gelu_both(hidden):
    phi = 0.5 * (1.0 + lax.erf(hidden * np.float32(np.sqrt(0.5))))
    density = jnp.exp(-0.5 * hidden * hidden) * np.float32(1.0 / np.sqrt(2.0 * np.pi))
    return hidden * phi, phi + hidden * density


def matmul(left, right):
    return jnp.dot(left, right, preferred_element_type=f32)


def left_tmul(left, right):
    return lax.dot_general(left, right, (((0,), (0,)), ((), ())), preferred_element_type=f32)


def right_tmul(left, right):
    return lax.dot_general(left, right, (((1,), (1,)), ((), ())), preferred_element_type=f32)


def pad_lanes(tensor, width):
    return jnp.pad(tensor, ((0, 0), (0, width - tensor.shape[1])))


def head_mask(head, head_size, width, scale):
    lane = lax.broadcasted_iota(jnp.int32, (1, width), 1)
    inside = (lane >= head * head_size) & (lane < (head + 1) * head_size)
    return jnp.where(inside, np.float32(scale), np.float32(0.0)).astype(bf16)


def softmax_rows(scores):
    peak = jnp.max(scores, axis=-1, keepdims=True)
    mass = jnp.exp(scores - peak)
    return mass * (1.0 / jnp.sum(mass, axis=-1, keepdims=True))


def window_probs(query, key, mask, heads, head_size, scale):
    stacked = jnp.concatenate(
        [query * head_mask(h, head_size, query.shape[1], scale) for h in range(heads)], axis=0
    )
    return stacked, softmax_rows(right_tmul(stacked, key) + mask)


def window_forward_kernel(heads, head_size, scale, packed, spread, gathered, slots, rows, out):
    cells = WS * WS
    win = matmul(spread[...], packed[...]).astype(bf16)
    count = win.shape[0] // cells
    width = win.shape[1] // 3
    mixed = []
    for j in range(count):
        part = win[j * cells : (j + 1) * cells]
        query, key, value = part[:, :width], part[:, width : 2 * width], part[:, 2 * width :]
        mask = slots[j * heads * cells : (j + 1) * heads * cells, :] + rows[0]
        _, probs = window_probs(query, key, mask, heads, head_size, scale)
        probs = probs.astype(bf16)
        total = None
        for h in range(heads):
            term = matmul(
                probs[h * cells : (h + 1) * cells], value * head_mask(h, head_size, width, 1.0)
            )
            total = term if total is None else total + term
        mixed.append(total.astype(bf16))
    grid = matmul(gathered[...], jnp.concatenate(mixed, axis=0)).astype(bf16)
    out[...] = grid[:, : out.shape[1]]


def window_backward_kernel(
    heads, head_size, scale, packed, upstream, spread, gathered, slots, rows, out, bias_out, bias_sum
):
    cells = WS * WS
    win = matmul(spread[...], packed[...]).astype(bf16)
    top = matmul(spread[...], upstream[...]).astype(bf16)
    count = win.shape[0] // cells
    width = win.shape[1] // 3

    @pl.when(pl.program_id(0) == 0)
    def _():
        bias_sum[...] = jnp.zeros_like(bias_sum)

    results = []
    for j in range(count):
        part = win[j * cells : (j + 1) * cells]
        query, key, value = part[:, :width], part[:, width : 2 * width], part[:, 2 * width :]
        given = top[j * cells : (j + 1) * cells]
        mask = slots[j * heads * cells : (j + 1) * heads * cells, :] + rows[0]
        stacked, probs = window_probs(query, key, mask, heads, head_size, scale)
        given = jnp.concatenate(
            [given * head_mask(h, head_size, width, 1.0) for h in range(heads)], axis=0
        )
        dprobs = right_tmul(given, value)
        inner = jnp.sum(probs * dprobs, axis=-1, keepdims=True)
        dscores = (probs * (dprobs - inner)).astype(bf16)
        bias_sum[...] += dscores.astype(f32)
        dquery = None
        for h in range(heads):
            term = matmul(
                dscores[h * cells : (h + 1) * cells], key * head_mask(h, head_size, width, scale)
            )
            dquery = term if dquery is None else dquery + term
        dkey = left_tmul(dscores, stacked)
        dvalue = left_tmul(probs.astype(bf16), given)
        results.append(
            jnp.concatenate([dquery.astype(bf16), dkey.astype(bf16), dvalue.astype(bf16)], axis=1)
        )
    out[...] = matmul(gathered[...], jnp.concatenate(results, axis=0)).astype(bf16)

    @pl.when(pl.program_id(0) == pl.num_programs(0) - 1)
    def _():
        bias_out[...] = bias_sum[...]


def query_scores(query, keys_vis, keys_qry, causal, mask):
    masked = query * mask
    return masked, right_tmul(masked, keys_vis), right_tmul(masked, keys_qry) + causal


def joint_softmax(score_vis, score_qry):
    peak = jnp.maximum(
        jnp.max(score_vis, axis=-1, keepdims=True), jnp.max(score_qry, axis=-1, keepdims=True)
    )
    mass_vis = jnp.exp(score_vis - peak)
    mass_qry = jnp.exp(score_qry - peak)
    inverse = 1.0 / (
        jnp.sum(mass_vis, axis=-1, keepdims=True) + jnp.sum(mass_qry, axis=-1, keepdims=True)
    )
    return mass_vis * inverse, mass_qry * inverse


def query_forward_kernel(
    heads, head_size, scale, query, keys_qry, values_qry, keys_vis, values_vis, causal, out
):
    width = query.shape[1]
    total = None
    for h in range(heads):
        _, score_vis, score_qry = query_scores(
            query[...], keys_vis[...], keys_qry[...], causal[...], head_mask(h, head_size, width, scale)
        )
        prob_vis, prob_qry = joint_softmax(score_vis, score_qry)
        mask = head_mask(h, head_size, width, 1.0)
        term = matmul(prob_vis.astype(bf16), values_vis[...] * mask)
        term = term + matmul(prob_qry.astype(bf16), values_qry[...] * mask)
        total = term if total is None else total + term
    out[...] = total.astype(bf16)[:, : out.shape[1]]


def query_backward_kernel(
    heads,
    head_size,
    scale,
    query,
    keys_qry,
    values_qry,
    keys_vis,
    values_vis,
    causal,
    upstream,
    dquery,
    dkeys_qry,
    dvalues_qry,
    dkeys_vis,
    dvalues_vis,
):
    width = query.shape[1]
    sums = [None] * 5

    def add(place, term):
        sums[place] = term if sums[place] is None else sums[place] + term

    for h in range(heads):
        masked, score_vis, score_qry = query_scores(
            query[...], keys_vis[...], keys_qry[...], causal[...], head_mask(h, head_size, width, scale)
        )
        prob_vis, prob_qry = joint_softmax(score_vis, score_qry)
        given = upstream[...] * head_mask(h, head_size, width, 1.0)
        dprob_vis = right_tmul(given, values_vis[...])
        dprob_qry = right_tmul(given, values_qry[...])
        inner = jnp.sum(prob_vis * dprob_vis, axis=-1, keepdims=True) + jnp.sum(
            prob_qry * dprob_qry, axis=-1, keepdims=True
        )
        dscore_vis = (prob_vis * (dprob_vis - inner)).astype(bf16)
        dscore_qry = (prob_qry * (dprob_qry - inner)).astype(bf16)
        mask = head_mask(h, head_size, width, scale)
        add(0, matmul(dscore_vis, keys_vis[...] * mask) + matmul(dscore_qry, keys_qry[...] * mask))
        add(1, left_tmul(dscore_qry, masked))
        add(2, left_tmul(prob_qry.astype(bf16), given))
        add(3, left_tmul(dscore_vis, masked))
        add(4, left_tmul(prob_vis.astype(bf16), given))
    for ref, value in zip((dquery, dkeys_qry, dvalues_qry, dkeys_vis, dvalues_vis), sums):
        ref[...] = value.astype(bf16)


def cross_forward_kernel(heads, head_size, scale, query, keys, values, live, out):
    width = query.shape[1]
    total = None
    for h in range(heads):
        masked = query[...] * head_mask(h, head_size, width, scale)
        probs = softmax_rows(right_tmul(masked, keys[...]) + live[...])
        term = matmul(probs.astype(bf16), values[...] * head_mask(h, head_size, width, 1.0))
        total = term if total is None else total + term
    out[...] = total.astype(bf16)[:, : out.shape[1]]


def cross_backward_kernel(
    heads, head_size, scale, query, keys, values, live, upstream, dquery, dkeys, dvalues
):
    width = query.shape[1]

    @pl.when(pl.program_id(0) == 0)
    def _():
        dkeys[...] = jnp.zeros_like(dkeys)
        dvalues[...] = jnp.zeros_like(dvalues)

    total = None
    for h in range(heads):
        masked = query[...] * head_mask(h, head_size, width, scale)
        probs = softmax_rows(right_tmul(masked, keys[...]) + live[...])
        given = upstream[...] * head_mask(h, head_size, width, 1.0)
        dprobs = right_tmul(given, values[...])
        inner = jnp.sum(probs * dprobs, axis=-1, keepdims=True)
        dscores = (probs * (dprobs - inner)).astype(bf16)
        term = matmul(dscores, keys[...] * head_mask(h, head_size, width, scale))
        total = term if total is None else total + term
        dkeys[...] += left_tmul(dscores, masked)
        dvalues[...] += left_tmul(probs.astype(bf16), given)
    dquery[...] = total.astype(bf16)


def params():
    return pltpu.CompilerParams(vmem_limit_bytes=VMEM_BYTES)


def whole(shape):
    return pl.BlockSpec(shape, lambda *_: (0,) * len(shape))


def window_places(page_width):
    half = WS // 2
    columns = page_width // WS + 1
    matrix = np.zeros((columns * WS * WS, WS * page_width), np.float32)
    for j in range(columns):
        for r in range(WS):
            for c in range(WS):
                column = j * WS + c - half
                if 0 <= column < page_width:
                    matrix[j * WS * WS + r * WS + c, r * page_width + column] = 1.0
    return matrix


def bias_slots(table, regions, page_width):
    half = WS // 2
    columns = page_width // WS + 1
    heads = table.shape[0]
    flipped = table.reshape(heads, SPAN, SPAN)[:, ::-1, ::-1]
    wide = jnp.stack([flipped[:, :, WS - 1 - c : 2 * WS - 1 - c] for c in range(WS)], axis=1)
    wide = wide.reshape(heads, WS, SPAN * WS)
    bias = jnp.stack(
        [wide[:, :, (WS - 1 - r) * WS : (2 * WS - 1 - r) * WS] for r in range(WS)], axis=1
    ).reshape(heads, WS * WS, WS * WS)
    padded = jnp.pad(regions, (half, half), constant_values=-1).reshape(columns, WS)
    of_place = jnp.tile(padded, (1, WS))
    allowed = (of_place[:, :, None] == of_place[:, None, :]) & (of_place[:, None, :] >= 0)
    mask = jnp.where(allowed, 0.0, masked_fill).astype(f32)
    slots = bias[None] + mask[:, None]
    return slots.reshape(columns * heads * WS * WS, WS * WS)


def bias_gather(grad, heads):
    shaped = grad.reshape(heads, WS, WS, WS * WS)
    wide = sum(
        jnp.pad(shaped[:, r], ((0, 0), (0, 0), ((WS - 1 - r) * WS, r * WS))) for r in range(WS)
    ).reshape(heads, WS, SPAN, WS)
    flipped = wide[:, :, ::-1, ::-1]
    table = sum(jnp.pad(flipped[:, c], ((0, 0), (0, 0), (c, WS - 1 - c))) for c in range(WS))
    return table.reshape(heads, SPAN * SPAN)


def body(
    visual,
    queries,
    query_lengths,
    column_regions,
    gain_window,
    window_qkv,
    window_out,
    position_bias,
    gain_visual,
    gain_query,
    attend_query,
    attend_kv,
    attend_out,
    cross_query,
    cross_kv,
    cross_out,
    gain_feed,
    visual_up,
    visual_down,
    gain_query_feed,
    query_up,
    query_down,
    cotangent_visual,
    cotangent_query,
):
    shards = lax.axis_size("win")
    me = lax.axis_index("win")
    row_count, page_width, model = visual.shape[1:]
    own = row_count * page_width
    tokens = own * shards
    slots_count = queries.shape[1]
    heads = HEADS // shards
    head_size = model // HEADS
    part = heads * head_size
    wide = -(-part // LANES) * LANES
    scale = head_size ** (-0.5)
    half_cells = WS // 2 * page_width
    stripes = shards + 1
    stripe = WS * page_width

    def column_blocks(weight, pieces):
        step = weight.shape[1] // (pieces * shards)
        return [
            [weight[:, (s * shards + j) * step : (s * shards + j + 1) * step] for s in range(pieces)]
            for j in range(shards)
        ]

    def columns_here(*items):
        blocks = [column_blocks(w, n) for w, n in items]
        stack = jnp.stack(
            [jnp.concatenate(sum([b[j] for b in blocks], []), axis=1) for j in range(shards)]
        )
        return jnp.concatenate(in_order(trade(stack)), axis=0)

    def widen(weight, pieces):
        return jnp.concatenate(
            [pad_lanes(weight[:, s * part : (s + 1) * part], wide) for s in range(pieces)], axis=1
        )

    def narrow(weight, pieces):
        return [weight[:, s * wide : s * wide + part] for s in range(pieces)]

    vis_low = gather_blocks(visual[0].reshape(own, model))
    gains = jnp.stack(
        [gain_window, gain_visual, gain_query, gain_feed, gain_query_feed]
    )
    gain_rows = gather_blocks(gains[None])
    gain_order = in_order([gain_rows[xor_order(shards).index(k)] for k in range(shards)])
    gains_all = jnp.concatenate(gain_order, axis=1).astype(f32)
    g_window, g_visual, g_query, g_feed, g_qfeed = [gains_all[i] for i in range(5)]
    qkv_w = widen(columns_here((window_qkv, 3)), 3)
    mixed_w = columns_here((attend_kv, 2), (cross_query, 1), (attend_query, 1), (cross_kv, 2))
    vis_w = widen(mixed_w[:, : 3 * part], 3)
    qry_w = widen(
        jnp.concatenate([mixed_w[:, 3 * part : 4 * part], mixed_w[:, : 2 * part], mixed_w[:, 4 * part :]], axis=1),
        5,
    )
    outs = gather_blocks(jnp.stack([window_out, cross_out, attend_out])[None])
    outs = [outs[:, i].reshape(model, model) for i in range(3)]
    up_w = columns_here((visual_up, 1), (query_up, 1))
    hidden_count = up_w.shape[1] // 2
    vup_w, qup_w = up_w[:, :hidden_count], up_w[:, hidden_count:]
    top_low = gather_blocks(cotangent_visual[0].reshape(own, model))

    vis = vis_low.astype(f32)
    norm_win = norm_low(vis, g_window)
    packed = matmul(norm_win, qkv_w).astype(bf16)

    order = xor_order(shards)

    def to_page(tensor):
        blocks = tensor.reshape((shards, own) + tensor.shape[1:])
        place = jnp.asarray(np.argsort(order), jnp.int32)
        ordered = [pick(blocks, place[me ^ j]) for j in range(shards)]
        zeros = jnp.zeros((half_cells,) + tensor.shape[1:], tensor.dtype)
        return jnp.concatenate([zeros] + ordered + [zeros], axis=0)

    def from_page(tensor):
        blocks = tensor[half_cells : half_cells + tokens].reshape((shards, own) + tensor.shape[1:])
        return jnp.concatenate([pick(blocks, me ^ k) for k in order], axis=0)

    packed_page = to_page(packed)
    slots = bias_slots(position_bias.astype(f32), column_regions[0], page_width)
    places = window_places(page_width)
    spread = jnp.asarray(places, bf16)
    collect = jnp.asarray(places.T, bf16)
    row_mask = np.zeros((stripes, 1, WS * WS), np.float32)
    row_mask[0, :, : WS * WS // 2] = masked_fill
    row_mask[-1, :, WS * WS // 2 :] = masked_fill
    row_mask = jnp.asarray(row_mask)
    static = (heads, head_size, scale)
    window_specs = [
        whole(spread.shape),
        whole(collect.shape),
        whole(slots.shape),
        pl.BlockSpec((1, 1, WS * WS), lambda i: (i, 0, 0)),
    ]
    heads_page = pl.pallas_call(
        functools.partial(window_forward_kernel, *static),
        grid=(stripes,),
        in_specs=[pl.BlockSpec((stripe, 3 * wide), lambda i: (i, 0))] + window_specs,
        out_specs=pl.BlockSpec((stripe, part), lambda i: (i, 0)),
        out_shape=jax.ShapeDtypeStruct((stripes * stripe, part), bf16),
        compiler_params=params(),
    )(packed_page, spread, collect, slots, row_mask)
    heads_win = from_page(heads_page)

    def gather_features(tensor, by_token):
        parts = gather_blocks(tensor[None])
        columns = []
        for place in range(shards):
            piece = parts[place]
            if by_token:
                blocks = piece.reshape(shards, own, part)
                piece = jnp.concatenate([blocks[order.index(k ^ order[place])] for k in order], axis=0)
            columns.append(piece)
        return jnp.concatenate(columns, axis=1)

    mid = vis + matmul(gather_features(heads_win, True), outs[0])
    norm_vis = norm_low(mid, g_visual)
    proj_vis = matmul(norm_vis, vis_w).astype(bf16)

    query_in = queries[0].astype(f32)
    norm_qry = norm_low(query_in, g_query)
    proj_qry = matmul(norm_qry, qry_w).astype(bf16)
    length = query_lengths[0]
    slot_ids = jnp.arange(slots_count, dtype=jnp.int32)
    live = slot_ids < length
    live_mask = jnp.where(live, 0.0, masked_fill).astype(f32)[None]
    reach = (slot_ids[None, :] <= slot_ids[:, None]) & live[None, :]
    causal_mask = jnp.where(reach, 0.0, masked_fill).astype(f32)

    def qry_piece(i):
        return pl.BlockSpec((slots_count, wide), lambda *_: (0, i))

    def vis_piece(i):
        return pl.BlockSpec((tokens, wide), lambda *_: (0, i))

    query_specs = [
        qry_piece(0),
        qry_piece(1),
        qry_piece(2),
        vis_piece(0),
        vis_piece(1),
        whole(causal_mask.shape),
    ]
    query_args = (proj_qry, proj_qry, proj_qry, proj_vis, proj_vis, causal_mask)
    heads_qry = pl.pallas_call(
        functools.partial(query_forward_kernel, *static),
        grid=(1,),
        in_specs=query_specs,
        out_specs=whole((slots_count, part)),
        out_shape=jax.ShapeDtypeStruct((slots_count, part), bf16),
        compiler_params=params(),
    )(*query_args)
    query_mid = query_in + matmul(gather_features(heads_qry, False), outs[2])

    block = own
    cross_specs = [
        pl.BlockSpec((block, wide), lambda i: (i, 2)),
        qry_piece(3),
        qry_piece(4),
        whole(live_mask.shape),
    ]
    cross_args = (proj_vis, proj_qry, proj_qry, live_mask)
    heads_cross = pl.pallas_call(
        functools.partial(cross_forward_kernel, *static),
        grid=(tokens // block,),
        in_specs=cross_specs,
        out_specs=pl.BlockSpec((block, part), lambda i: (i, 0)),
        out_shape=jax.ShapeDtypeStruct((tokens, part), bf16),
        compiler_params=params(),
    )(*cross_args)
    late = mid + matmul(gather_features(heads_cross, True), outs[1])

    norm_feed = norm_low(late, g_feed)
    act_vis, slope_vis = gelu_both(matmul(norm_feed, vup_w))
    act_vis = act_vis.astype(bf16)
    visual_final = late[:own] + scatter_sum(matmul(act_vis, visual_down).astype(bf16))

    norm_qfeed = norm_low(query_mid, g_qfeed)
    act_qry, slope_qry = gelu_both(matmul(norm_qfeed, qup_w))
    act_qry = act_qry.astype(bf16)
    query_final = query_mid + total_sum(matmul(act_qry, query_down))

    dhid_qry = (right_tmul(cotangent_query[0], query_down) * slope_qry).astype(bf16)
    grad_query_down = left_tmul(act_qry, cotangent_query[0])
    grad_query_up = left_tmul(norm_qfeed, dhid_qry)
    dqfeed = total_sum(right_tmul(dhid_qry, qup_w))
    grad_qmid = cotangent_query[0].astype(f32) + norm_back(query_mid, g_qfeed, dqfeed)

    dhid_vis = (right_tmul(top_low, visual_down) * slope_vis).astype(bf16)
    grad_visual_down = left_tmul(act_vis, top_low)
    grad_visual_up = left_tmul(norm_feed, dhid_vis)
    dfeed = scatter_sum(right_tmul(dhid_vis, vup_w).astype(bf16))
    grad_late = cotangent_visual[0].reshape(own, model).astype(f32) + norm_back(
        late[:own], g_feed, dfeed
    )

    dz_attend = grad_qmid.astype(bf16)
    grad_attend_out = left_tmul(heads_qry, dz_attend)
    dheads_qry = pad_lanes(right_tmul(dz_attend, attend_out).astype(bf16), wide)
    qry_out = jax.ShapeDtypeStruct((slots_count, wide), bf16)
    vis_out = jax.ShapeDtypeStruct((tokens, wide), bf16)
    dq, dkq, dvq, dkv, dvv = pl.pallas_call(
        functools.partial(query_backward_kernel, *static),
        grid=(1,),
        in_specs=query_specs + [whole((slots_count, wide))],
        out_specs=[whole(qry_out.shape)] * 3 + [whole(vis_out.shape)] * 2,
        out_shape=[qry_out] * 3 + [vis_out] * 2,
        compiler_params=params(),
    )(*query_args, dheads_qry)

    dz_cross = gather_blocks(grad_late.astype(bf16))
    grad_cross_out = left_tmul(heads_cross, dz_cross)
    dheads_cross = pad_lanes(right_tmul(dz_cross, cross_out).astype(bf16), wide)
    dcq, dck, dcv = pl.pallas_call(
        functools.partial(cross_backward_kernel, *static),
        grid=(tokens // block,),
        in_specs=cross_specs + [pl.BlockSpec((block, wide), lambda i: (i, 0))],
        out_specs=[pl.BlockSpec((block, wide), lambda i: (i, 0))]
        + [whole((slots_count, wide))] * 2,
        out_shape=[vis_out] + [jax.ShapeDtypeStruct((slots_count, wide), f32)] * 2,
        compiler_params=params(),
    )(*cross_args, dheads_cross)
    dproj_vis = jnp.concatenate([dkv, dvv, dcq], axis=1)
    dproj_qry = jnp.concatenate([dq, dkq, dvq, dck.astype(bf16), dcv.astype(bf16)], axis=1)
    grad_vis_w = left_tmul(norm_vis, dproj_vis)
    grad_qry_w = left_tmul(norm_qry, dproj_qry)

    dnorm_vis = scatter_sum(right_tmul(dproj_vis, vis_w).astype(bf16))
    grad_mid = grad_late + norm_back(mid[:own], g_visual, dnorm_vis)
    dnorm_qry = total_sum(right_tmul(dproj_qry, qry_w))
    query_back = (grad_qmid + norm_back(query_in, g_query, dnorm_qry)).astype(bf16)

    dz_window = gather_blocks(grad_mid.astype(bf16))
    grad_window_out = left_tmul(heads_win, dz_window)
    dheads_win = to_page(pad_lanes(right_tmul(dz_window, window_out).astype(bf16), wide))
    dpacked_page, bias_grad = pl.pallas_call(
        functools.partial(window_backward_kernel, *static),
        grid=(stripes,),
        in_specs=[
            pl.BlockSpec((stripe, 3 * wide), lambda i: (i, 0)),
            pl.BlockSpec((stripe, wide), lambda i: (i, 0)),
        ]
        + window_specs,
        out_specs=[
            pl.BlockSpec((stripe, 3 * wide), lambda i: (i, 0)),
            whole((heads * WS * WS, WS * WS)),
        ],
        out_shape=[
            jax.ShapeDtypeStruct((stripes * stripe, 3 * wide), bf16),
            jax.ShapeDtypeStruct((heads * WS * WS, WS * WS), f32),
        ],
        scratch_shapes=[pltpu.VMEM((heads * WS * WS, WS * WS), f32)],
        compiler_params=params(),
    )(packed_page, dheads_win, spread, collect, slots, row_mask)
    dpacked = from_page(dpacked_page)
    grad_qkv_w = left_tmul(norm_win, dpacked)
    dnorm_win = scatter_sum(right_tmul(dpacked, qkv_w).astype(bf16))
    visual_back = (grad_mid + norm_back(vis[:own], g_window, dnorm_win)).astype(bf16)

    def gain_grad(gain, *pairs):
        return sum(jnp.sum(w.astype(f32) * g, axis=1) for w, g in pairs) / gain

    gain_grads = jnp.stack(
        [
            gain_grad(g_window, (qkv_w, grad_qkv_w)),
            gain_grad(g_visual, (vis_w, grad_vis_w)),
            gain_grad(g_query, (qry_w, grad_qry_w)),
            gain_grad(g_feed, (vup_w, grad_visual_up)),
            gain_grad(g_qfeed, (qup_w, grad_query_up)),
        ]
    )
    small = jnp.concatenate(
        [
            tiny_sum(gain_grads, ("win",)).reshape(-1),
            bias_gather(bias_grad, heads).reshape(-1),
        ]
    )
    small = tiny_sum(small, ("page",))
    gain_total = lax.dynamic_slice_in_dim(
        small[: 5 * model].reshape(5, model), me * (model // shards), model // shards, 1
    )
    bias_total = small[5 * model :].reshape(heads, SPAN * SPAN)

    def rows_here(*blocks):
        cols = jnp.concatenate([b.astype(bf16) for b in blocks], axis=1)
        stack = cols.reshape(shards, cols.shape[0] // shards, cols.shape[1])
        return jnp.concatenate(trade(stack), axis=0)

    def laid_out(blocks, widths):
        ordered = in_order(blocks.reshape((shards, blocks.shape[0] // shards, blocks.shape[1])))
        result, start = [], 0
        for step, pieces in widths:
            result.append(
                jnp.concatenate(
                    [
                        b[:, start + s * step : start + (s + 1) * step]
                        for s in range(pieces)
                        for b in ordered
                    ],
                    axis=1,
                ).astype(f32)
            )
            start += step * pieces
        return result

    vup_t, vdown_t = page_total(rows_here(grad_visual_up), grad_visual_down.astype(bf16))
    qup_t, qdown_t = page_total(rows_here(grad_query_up), grad_query_down.astype(bf16))
    gk, gv, gcq = narrow(grad_vis_w, 3)
    gaq, gkq, gvq, gck, gcv = narrow(grad_qry_w, 5)
    mixed_t, attend_t = page_total(
        rows_here(gk + gkq, gv + gvq, gcq, gaq, gck, gcv),
        jnp.concatenate([grad_cross_out, grad_attend_out], axis=0).astype(bf16),
    )
    qkv_t, wout_t = page_total(rows_here(*narrow(grad_qkv_w, 3)), grad_window_out.astype(bf16))
    (out_qkv,) = laid_out(qkv_t, [(part, 3)])
    out_akv, out_cq, out_aq, out_ckv = laid_out(mixed_t, [(part, 2), (part, 1), (part, 1), (part, 2)])
    (out_vup,) = laid_out(vup_t, [(hidden_count, 1)])
    (out_qup,) = laid_out(qup_t, [(hidden_count, 1)])
    rows = model // shards

    return (
        visual_final.reshape(1, row_count, page_width, model).astype(bf16),
        query_final.reshape(1, slots_count, model).astype(bf16),
        visual_back.reshape(1, row_count, page_width, model),
        query_back.reshape(1, slots_count, model),
        gain_total[0],
        out_qkv,
        wout_t.astype(f32),
        bias_total,
        gain_total[1],
        gain_total[2],
        out_aq,
        out_akv,
        attend_t[rows:].astype(f32),
        out_cq,
        out_ckv,
        attend_t[:rows].astype(f32),
        gain_total[3],
        out_vup,
        vdown_t.astype(f32),
        gain_total[4],
        out_qup,
        qdown_t.astype(f32),
    )


def solution(mesh):
    tokens_spec = P("page", "win", None, None)
    slots_spec = P("page", None, None)
    gain, weight = P("win"), P("win", None)
    parameters = (
        gain, weight, weight, weight, gain, gain, weight, weight, weight, weight, weight, weight,
        gain, weight, weight, gain, weight, weight,
    )
    return jax.shard_map(
        body,
        mesh=mesh,
        in_specs=(tokens_spec, slots_spec, P("page"), P("page", None)) + parameters + (tokens_spec, slots_spec),
        out_specs=(tokens_spec, slots_spec, tokens_spec, slots_spec) + parameters,
        check_vma=False,
    )
```

time: 1630 us -> 817 us (0.50)
  blocking collectives: 695 us -> 0 us
  matrix products: 240 us -> 77.3 us
  starting transfers between devices: 12.4 us -> 137 us
  waiting for transfers between devices: 342 us -> 231 us
  local copies, waits for them, and re-layouts: 229 us -> 170 us
  Pallas kernels: 0 us -> 58.8 us
  other arithmetic: 81.8 us -> 116 us
    psum x2 -> x0, blocking collectives: 649 us -> none  [the longest x1 637 us: body(): lax.psum((shares[0], shares[1], shares[2], shares[3], shares[4], shares[5...]
    ppermute x4 -> x98, waiting for transfers between devices: 0.01 us -> 231 us  [the longest x58 100 us: swap(): return lax.ppermute(tensor, axis, [(i, i ^ bit) for i in range(count)])]
    reduce_scatter x12 -> x0, waiting for transfers between devices: 216 us -> none  [the longest x1 50.6 us: body(): lax.psum_scatter((grad_query_up * inverse).astype(jnp.bfloat16), 'win', s...]
    dot_general x68 -> x30, matrix products: 240 us -> 77.3 us  [the longest x10 37.6 us: matmul(): return jnp.dot(left, right, preferred_element_type=f32)]
    ppermute x4 -> x98, starting transfers between devices: 10.4 us -> 137 us  [the longest x58 43.6 us: swap(): return lax.ppermute(tensor, axis, [(i, i ^ bit) for i in range(count)])]
    all_gather x12 -> x0, waiting for transfers between devices: 99.9 us -> none  [the longest x1 34.7 us: body(): lax.all_gather(query_up, 'win', axis=0, tiled=True)]
    pallas_call x0 -> x6, Pallas kernels: none -> 58.8 us  [the longest x1 22.3 us: body(): pl.pallas_call(functools.partial(window_backward_kernel, *static), grid=(...]
    transpose x8 -> x0, local copies, waits for them, and re-layouts: 48.1 us -> none  [the longest x1 17.3 us: bias_expand(): jnp.einsum('hab,aij,bkl->hikjl', cube_view, onehot, onehot, precision=lax...]
  transfers between devices with their start and end apart: 30 -> 98, of which waited for: 10 -> 32; matrix products, arithmetic and copies ran while one was open for 30% -> 36% of each run, Pallas kernels for 0% -> 4%
where the time goes in v1:
time: 817 us; the launch traced here: 804 us
  waiting for transfers between devices  231 us (28%)
  local copies, waits for them, and re-layouts  170 us (21%)
  starting transfers between devices  137 us (17%)
  other arithmetic  116 us (14%)
  matrix products  77.3 us (9%)
  Pallas kernels  58.8 us (7%)
  between operations  13.5 us (2%)
    ppermute x58, waiting for transfers between devices, swap(): return lax.ppermute(tensor, axis, [(i, i ^ bit) for i in range(count)])  100 us
    unnamed x382, local copies, waits for them, and re-layouts  48.9 us
    ppermute x58, starting transfers between devices, swap(): return lax.ppermute(tensor, axis, [(i, i ^ bit) for i in range(count)])  43.6 us
    dot_general x10, matrix products, matmul(): return jnp.dot(left, right, preferred_element_type=f32)  37.6 us
    ppermute x4, waiting for transfers between devices, page_total_across(): own = jnp.where(outer, lax.ppermute(own, 'page', OUTWARD), own)  35 us
    ppermute x4, waiting for transfers between devices, page_total_across(): lax.ppermute(pick(stack, 1 - side), 'page', SIDE)  32.9 us
    ppermute x4, starting transfers between devices, page_total_along(): own = add_low(tensor, lax.ppermute(tensor, 'page', INWARD))  30 us
    ppermute x4, starting transfers between devices, page_total_across(): own = add_low(own, lax.ppermute(own, 'page', INWARD))  28.6 us
  transfers between devices with their start and end apart: 98, of which 32 were waited for; matrix products, arithmetic and copies ran while one was open for 36% of the time, Pallas kernels for 4%

profile of v1, /device:TPU:0, one launch (start us, length us, event | category | flops | bytes accessed | tf_op | source)
XLA Modules:
  0.0 803.8 jit_solution(2856158213378289199)
XLA Ops:
  65.4 9.5 %collective-permute-done.12 = bf16[192,1152]{1,0:T(8,128)(2,1)} collective-permute-done((bf16[192,1152]{1,0:T(8,128)(2,1)}, bf16[192,1152]{1,0:T(8,128)(2,1)}, u32[]{:S(2)}, u32[]{:S(2)}) %collective-permute-start.12) | collective-permute-done | bytes 442400 | tf_op jit(solution)/shard_map/ppermute | solution.py:25
  108.1 10.3 %collective-permute-done.9 = bf16[1,3,192,768]{3,2,1,0:T(8,128)(2,1)S(1)} collective-permute-done((bf16[1,3,192,768]{3,2,1,0:T(8,128)(2,1)S(1)}, bf16[1,3,192,768]{3,2,1,0:T(8,128)(2,1)S(1)}, u32[]{:S(2)}, u32[]{:S(2)}) %collective-permute-start.9) | collective-permute-done | bytes 884768 | tf_op jit(solution)/shard_map/ppermute | solution.py:25
  131.0 13.1 %shard_map.444 = bf16[2160,192]{1,0:T(8,128)(2,1)S(1)} custom-call(bf16[2160,768]{1,0:T(8,128)(2,1)} %copy-done.23, bf16[576,432]{1,0:T(8,128)(2,1)S(1)} %copy-done.10, bf16[432,576]{1,0:T(8,128)(2,1)S(1)} %copy-done.12, f32[1728,144]{1,0:T(8,128)S(1)} %bitcast.481, f32[5,1,144]{2,1,0:T(1,128)S(1)} %copy-done.15), custom_call_target="tpu_custom_call" | custom-call | tf_op jit(solution)/shard_map/pallas_call | solution.py:556
  153.0 15.0 %collective-permute-done.7 = bf16[1,1728,192]{1,2,0:T(8,128)(2,1)S(1)} collective-permute-done((bf16[1,1728,192]{1,2,0:T(8,128)(2,1)}, bf16[1,1728,192]{1,2,0:T(8,128)(2,1)S(1)}, u32[]{:S(2)}, u32[]{:S(2)}) %collective-permute-start.7) | collective-permute-done | bytes 663584 | tf_op jit(solution)/shard_map/ppermute | solution.py:25
  184.9 12.0 %concatenate.237 = bf16[1728,192]{0,1:T(8,128)(2,1)} concatenate(bf16[432,192]{0,1:T(8,128)(2,1)} %get-tuple-element.132, bf16[432,192]{0,1:T(8,128)(2,1)S(1)} %get-tuple-element.131, bf16[432,192]{0,1:T(8,128)(2,1)S(1)} %get-tuple-element.130, bf16[432,192]{0,1:T(8,128)(2,1)S(1)} %get-tuple-element.125), dimensions={0} | concatenate | bytes 1327104 | tf_op jit(solution)/shard_map/concatenate | solution.py:573
  196.9 5.3 fusion.164
  222.9 12.2 %collective-permute-done.21 = bf16[1,256,192]{2,1,0:T(8,128)(2,1)S(1)} collective-permute-done((bf16[1,256,192]{2,1,0:T(8,128)(2,1)S(1)}, bf16[1,256,192]{2,1,0:T(8,128)(2,1)S(1)}, u32[]{:S(2)}, u32[]{:S(2)}) %collective-permute-start.21) | collective-permute-done | bytes 98336 | tf_op jit(solution)/shard_map/ppermute | solution.py:25
  264.2 6.5 collective-permute-done.30
  272.1 6.5 collective-permute-done.24
  283.9 6.4 shard_map.447
  309.0 14.3 %fusion.165 = (f32[1728]{0:T(1024)S(1)}, f32[1728,768]{1,0:T(8,128)S(1)}) fusion(f32[1728,768]{1,0:T(8,128)} %copy-done.17, bf16[768,768]{1,0:T(8,128)(2,1)} %bitcast.524, bf16[432,192]{1,0:T(8,128)(2,1)} %bitcast.541, bf16[432,192]{1,0:T(8,128)(2,1)} %bitcast.542, bf16[432,192]{1,0:T(8,128)(2,1)} %bitcast.543, bf16[432,192]{1,0:T(8,128)(2,1)} %bitcast.544, ...), kind=kOutput, calls=%fused_computation.585 | convolution fusion | flops 2075588864 | bytes 14457600 | tf_op jit(solution)/shard_map/dot_general | solution.py:171
  325.9 6.1 multiply_convert_fusion
  365.6 5.7 collective-permute-done.87
  379.8 13.6 %collective-permute-done.75 = bf16[384,768]{1,0:T(8,128)(2,1)S(1)} collective-permute-done((bf16[384,768]{1,0:T(8,128)(2,1)S(1)}, bf16[384,768]{1,0:T(8,128)(2,1)S(1)}, u32[]{:S(2)}, u32[]{:S(2)}) %collective-permute-start.75) | collective-permute-done | bytes 589856 | tf_op jit(solution)/shard_map/ppermute | solution.py:112
  394.3 11.0 %collective-permute-done.88 = bf16[384,768]{1,0:T(8,128)(2,1)S(1)} collective-permute-done((bf16[384,768]{1,0:T(8,128)(2,1)S(1)}, bf16[384,768]{1,0:T(8,128)(2,1)S(1)}, u32[]{:S(2)}, u32[]{:S(2)}) %collective-permute-start.88) | collective-permute-done | bytes 589856 | tf_op jit(solution)/shard_map/ppermute | solution.py:112
  416.7 6.3 collective-permute-done.76
  425.1 8.7 %collective-permute-done.89 = bf16[384,768]{1,0:T(8,128)(2,1)S(1)} collective-permute-done((bf16[384,768]{1,0:T(8,128)(2,1)S(1)}, bf16[384,768]{1,0:T(8,128)(2,1)S(1)}, u32[]{:S(2)}, u32[]{:S(2)}) %collective-permute-start.89) | collective-permute-done | bytes 589856 | tf_op jit(solution)/shard_map/ppermute | solution.py:113
  465.4 6.6 collective-permute-done.78
  473.6 7.9 collective-permute-done.91
  486.0 8.6 %collective-permute-done.92 = bf16[384,768]{1,0:T(8,128)(2,1)S(1)} collective-permute-done((bf16[384,768]{1,0:T(8,128)(2,1)S(1)}, bf16[384,768]{1,0:T(8,128)(2,1)S(1)}, u32[]{:S(2)}, u32[]{:S(2)}) %collective-permute-start.92) | collective-permute-done | bytes 589856 | tf_op jit(solution)/shard_map/ppermute | solution.py:117
  504.4 9.0 %shard_map.448 = (bf16[1728,256]{1,0:T(8,128)(2,1)S(1)}, f32[256,256]{1,0:T(8,128)S(1)}, f32[256,256]{1,0:T(8,128)S(1)}) custom-call(bf16[1728,768]{1,0:T(8,128)(2,1)S(1)} %copy-done.5, bf16[256,1280]{1,0:T(8,128)(2,1)S(1)} %convolution_convert_fusion.6.keys.values.query.keys_qry.values_qry, ...), custom_call_target="tpu_custom_call" | custom-call | tf_op jit(solution)/shard_map/pallas_call | solution.py:675
  533.3 9.0 %collective-permute-start.67 = (bf16[384,768]{1,0:T(8,128)(2,1)S(1)}, bf16[384,768]{1,0:T(8,128)(2,1)S(1)}, u32[]{:S(2)}, u32[]{:S(2)}) collective-permute-start(bf16[384,768]{1,0:T(8,128)(2,1)S(1)} %pad_maximum_fusion.36), channel_id=1, source_target_pairs={{0,8},{4,12},{24,16},{28,20},{1,9},{5,13},{25,17},{29,21},{2,10},{... | collective-permute-start | bytes 1769480 | tf_op jit(solution)/shard_map/ppermute | solution.py:125
  546.8 8.1 %collective-permute-done.67 = bf16[384,768]{1,0:T(8,128)(2,1)S(1)} collective-permute-done((bf16[384,768]{1,0:T(8,128)(2,1)S(1)}, bf16[384,768]{1,0:T(8,128)(2,1)S(1)}, u32[]{:S(2)}, u32[]{:S(2)}) %collective-permute-start.67) | collective-permute-done | bytes 589856 | tf_op jit(solution)/shard_map/ppermute | solution.py:125
  569.5 8.3 %collective-permute-done.62 = bf16[384,1152]{1,0:T(8,128)(2,1)S(1)} collective-permute-done((bf16[384,1152]{1,0:T(8,128)(2,1)S(1)}, bf16[384,1152]{1,0:T(8,128)(2,1)S(1)}, u32[]{:S(2)}, u32[]{:S(2)}) %collective-permute-start.62) | collective-permute-done | bytes 884768 | tf_op jit(solution)/shard_map/ppermute | solution.py:112
  578.1 18.9 %collective-permute-start.63 = (bf16[384,1152]{1,0:T(8,128)(2,1)S(1)}, bf16[384,1152]{1,0:T(8,128)(2,1)S(1)}, u32[]{:S(2)}, u32[]{:S(2)}) collective-permute-start(bf16[384,1152]{1,0:T(8,128)(2,1)S(1)} %fusion.43), channel_id=1, source_target_pairs={{0,8},{4,12},{24,16},{28,20},{1,9},{5,13},{25,17},{29,21},{2,10},{... | collective-permute-start | bytes 2654216 | tf_op jit(solution)/shard_map/ppermute | solution.py:113
  601.7 11.8 %collective-permute-done.63 = bf16[384,1152]{1,0:T(8,128)(2,1)S(1)} collective-permute-done((bf16[384,1152]{1,0:T(8,128)(2,1)S(1)}, bf16[384,1152]{1,0:T(8,128)(2,1)S(1)}, u32[]{:S(2)}, u32[]{:S(2)}) %collective-permute-start.63) | collective-permute-done | bytes 884768 | tf_op jit(solution)/shard_map/ppermute | solution.py:113
  615.7 7.2 collective-permute-done.71
  636.7 22.3 %shard_map.449 = (bf16[2160,768]{1,0:T(8,128)(2,1)}, f32[432,144]{1,0:T(8,128)S(1)}) custom-call(bf16[2160,768]{1,0:T(8,128)(2,1)} %copy-done.23, bf16[2160,256]{1,0:T(8,128)(2,1)S(1)} %copy-done.14, bf16[576,432]{1,0:T(8,128)(2,1)S(1)} %copy-done.11, bf16[432,576]{1,0:T(8,128)(2,1)S(1)} %copy-done.13, f32[1728,144]{1,0:T(8,128)S(1)} %bitcast.482, ...), custom_call_target="tpu_custom_call" | custom-call | tf_op jit(solution)/shard_map/pallas_call | solution.py:697
  687.5 14.2 %collective-permute-start.54 = (bf16[192,768]{1,0:T(8,128)(2,1)S(1)}, bf16[192,768]{1,0:T(8,128)(2,1)S(1)}, u32[]{:S(2)}, u32[]{:S(2)}) collective-permute-start(bf16[192,768]{1,0:T(8,128)(2,1)S(1)} %convolution_convert_fusion.13), channel_id=1, source_target_pairs={{0,8},{4,12},{24,16},{28,20},{1,9},{5,13},{25,17},{29,21},{2,10},{... | collective-permute-start | bytes 884744 | tf_op jit(solution)/shard_map/ppermute | solution.py:125
  717.5 12.4 %collective-permute-done.65 = bf16[384,1152]{1,0:T(8,128)(2,1)} collective-permute-done((bf16[384,1152]{1,0:T(8,128)(2,1)S(1)}, bf16[384,1152]{1,0:T(8,128)(2,1)}, u32[]{:S(2)}, u32[]{:S(2)}) %collective-permute-start.65) | collective-permute-done | bytes 884768 | tf_op jit(solution)/shard_map/ppermute | solution.py:116
  741.8 8.4 %collective-permute-done.66 = bf16[384,1152]{1,0:T(8,128)(2,1)} collective-permute-done((bf16[384,1152]{1,0:T(8,128)(2,1)S(1)}, bf16[384,1152]{1,0:T(8,128)(2,1)}, u32[]{:S(2)}, u32[]{:S(2)}) %collective-permute-start.66) | collective-permute-done | bytes 884768 | tf_op jit(solution)/shard_map/ppermute | solution.py:117
  781.1 8.2 %collective-permute-done.52 = bf16[384,576]{0,1:T(8,128)(2,1)S(1)} collective-permute-done((bf16[384,576]{0,1:T(8,128)(2,1)S(1)}, bf16[384,576]{0,1:T(8,128)(2,1)S(1)}, u32[]{:S(2)}, u32[]{:S(2)}) %collective-permute-start.52) | collective-permute-done | bytes 442400 | tf_op jit(solution)/shard_map/ppermute | solution.py:116
  (920 shorter events, 467.2 us)
Async XLA Ops:
  4.1 37.2 %collective-permute-start.2 = (bf16[1,5,192]{2,1,0:T(8,128)(2,1)S(1)}, bf16[1,5,192]{2,1,0:T(8,128)(2,1)S(1)}, u32[]{:S(2)}, u32[]{:S(2)}) collective-permute-start(bf16[1,5,192]{2,1,0:T(8,128)(2,1)S(1)} %bitcast.562), channel_id=1, source_target_pairs={{0,2},{1,3},{2,0},{3,1},{4,6},{5,7},{6,4},{7,5},{8,10},{9,11},{10,... | collective-permute-start | bytes 5768 | tf_op jit(solution)/shard_map/ppermute | solution.py:25
  8.4 84.4 %collective-permute-start = (bf16[432,768]{1,0:T(8,128)(2,1)S(1)}, bf16[432,768]{1,0:T(8,128)(2,1)}, u32[]{:S(2)}, u32[]{:S(2)}) collective-permute-start(bf16[432,768]{1,0:T(8,128)(2,1)S(1)} %reshape_squeeze.10), channel_id=1, source_target_pairs={{0,2},{1,3},{2,0},{3,1},{4,6},{5,7},{6,4},{7,5},{8,10},{9,11},{10,... | collective-permute-start | bytes 1990664 | tf_op jit(solution)/shard_map/ppermute | solution.py:25
  12.0 40.0 %collective-permute-start.6 = (bf16[192,576]{1,0:T(8,128)(2,1)}, bf16[192,576]{1,0:T(8,128)(2,1)}, u32[]{:S(2)}, u32[]{:S(2)}) collective-permute-start(bf16[192,576]{1,0:T(8,128)(2,1)} %get-tuple-element.183), channel_id=1, source_target_pairs={{0,3},{1,2},{2,1},{3,0},{4,7},{5,6},{6,5},{7,4},{8,11},{9,10},{10,... | collective-permute-start | bytes 663560 | tf_op jit(solution)/shard_map/ppermute | solution.py:25
  12.7 39.9 %collective-permute-start.5 = (bf16[192,576]{1,0:T(8,128)(2,1)}, bf16[192,576]{1,0:T(8,128)(2,1)}, u32[]{:S(2)}, u32[]{:S(2)}) collective-permute-start(bf16[192,576]{1,0:T(8,128)(2,1)} %get-tuple-element.184), channel_id=1, source_target_pairs={{0,2},{1,3},{2,0},{3,1},{4,6},{5,7},{6,4},{7,5},{8,10},{9,11},{10,... | collective-permute-start | bytes 663560 | tf_op jit(solution)/shard_map/ppermute | solution.py:25
  14.9 88.8 %collective-permute-start.25 = (bf16[432,768]{1,0:T(8,128)(2,1)}, bf16[432,768]{1,0:T(8,128)(2,1)}, u32[]{:S(2)}, u32[]{:S(2)}) collective-permute-start(bf16[432,768]{1,0:T(8,128)(2,1)} %reshape_squeeze.26), channel_id=1, source_target_pairs={{0,2},{1,3},{2,0},{3,1},{4,6},{5,7},{6,4},{7,5},{8,10},{9,11},{10,... | collective-permute-start | bytes 1990664 | tf_op jit(solution)/shard_map/ppermute | solution.py:25
  64.4 31.5 %collective-permute-start.18 = (bf16[192,1536]{1,0:T(8,128)(2,1)}, bf16[192,1536]{1,0:T(8,128)(2,1)}, u32[]{:S(2)}, u32[]{:S(2)}) collective-permute-start(bf16[192,1536]{1,0:T(8,128)(2,1)} %get-tuple-element.89), channel_id=1, source_target_pairs={{0,3},{1,2},{2,1},{3,0},{4,7},{5,6},{6,5},{7,4},{8,11},{9,10},{10,... | collective-permute-start | bytes 1769480 | tf_op jit(solution)/shard_map/ppermute | solution.py:25
  74.9 25.3 %collective-permute-start.17 = (bf16[192,1536]{1,0:T(8,128)(2,1)}, bf16[192,1536]{1,0:T(8,128)(2,1)}, u32[]{:S(2)}, u32[]{:S(2)}) collective-permute-start(bf16[192,1536]{1,0:T(8,128)(2,1)} %get-tuple-element.90), channel_id=1, source_target_pairs={{0,2},{1,3},{2,0},{3,1},{4,6},{5,7},{6,4},{7,5},{8,10},{9,11},{10,... | collective-permute-start | bytes 1769480 | tf_op jit(solution)/shard_map/ppermute | solution.py:25
  106.1 63.0 %collective-permute-start.26 = (bf16[864,768]{1,0:T(8,128)(2,1)}, bf16[864,768]{1,0:T(8,128)(2,1)}, u32[]{:S(2)}, u32[]{:S(2)}) collective-permute-start(bf16[864,768]{1,0:T(8,128)(2,1)} %pad_maximum_fusion.17), channel_id=1, source_target_pairs={{0,1},{1,0},{2,3},{3,2},{4,5},{5,4},{6,7},{7,6},{8,9},{9,8},{10,11... | collective-permute-start | bytes 3981320 | tf_op jit(solution)/shard_map/ppermute | solution.py:25
  119.9 55.7 %collective-permute-start.10 = (bf16[2,3,192,768]{3,2,1,0:T(8,128)(2,1)}, bf16[2,3,192,768]{3,2,1,0:T(8,128)(2,1)}, u32[]{:S(2)}, u32[]{:S(2)}) collective-permute-start(bf16[2,3,192,768]{3,2,1,0:T(8,128)(2,1)} %pad_maximum_fusion.8), channel_id=1, source_target_pairs={{0,1},{1,0},{2,3},{3,2},{4,5},{5,4},{6,7},{7,6},{8,9},{9,8},{10,11... | collective-permute-start | bytes 5308424 | tf_op jit(solution)/shard_map/ppermute | solution.py:25
  214.3 35.0 %collective-permute-start.14 = (bf16[1,1728,192]{1,2,0:T(8,128)(2,1)}, bf16[1,1728,192]{1,2,0:T(8,128)(2,1)}, u32[]{:S(2)}, u32[]{:S(2)}) collective-permute-start(bf16[1,1728,192]{1,2,0:T(8,128)(2,1)} %copy.253), channel_id=1, source_target_pairs={{0,2},{1,3},{2,0},{3,1},{4,6},{5,7},{6,4},{7,5},{8,10},{9,11},{10,... | collective-permute-start | bytes 1990664 | tf_op jit(solution)/shard_map/ppermute | solution.py:25
  244.8 48.0 %collective-permute-start.93 = (bf16[768,768]{1,0:T(8,128)(2,1)}, bf16[768,768]{1,0:T(8,128)(2,1)}, u32[]{:S(2)}, u32[]{:S(2)}) collective-permute-start(bf16[768,768]{1,0:T(8,128)(2,1)} %convolution_convert_fusion.9), channel_id=1, source_target_pairs={{0,8},{4,12},{24,16},{28,20},{1,9},{5,13},{25,17},{29,21},{2,10},{... | collective-permute-start | bytes 3538952 | tf_op jit(solution)/shard_map/ppermute | solution.py:125
  257.2 40.0 %collective-permute-start.15 = (bf16[2,1728,192]{1,2,0:T(8,128)(2,1)}, bf16[2,1728,192]{1,2,0:T(8,128)(2,1)}, u32[]{:S(2)}, u32[]{:S(2)}) collective-permute-start(bf16[2,1728,192]{1,2,0:T(8,128)(2,1)} %copy.259), channel_id=1, source_target_pairs={{0,1},{1,0},{2,3},{3,2},{4,5},{5,4},{6,7},{7,6},{8,9},{9,8},{10,11... | collective-permute-start | bytes 3981320 | tf_op jit(solution)/shard_map/ppermute | solution.py:25
  295.7 56.6 %collective-permute-start.94 = (bf16[384,768]{1,0:T(8,128)(2,1)}, bf16[384,768]{1,0:T(8,128)(2,1)}, u32[]{:S(2)}, u32[]{:S(2)}) collective-permute-start(bf16[384,768]{1,0:T(8,128)(2,1)} %broadcast_select_fusion.5), channel_id=1, source_target_pairs={{8,16},{12,20},{16,8},{20,12},{9,17},{13,21},{17,9},{21,13},{10,18... | collective-permute-start | bytes 1769480 | tf_op jit(solution)/shard_map/ppermute | solution.py:130
  364.6 48.9 %collective-permute-start.27 = (bf16[864,768]{1,0:T(8,128)(2,1)S(1)}, bf16[864,768]{1,0:T(8,128)(2,1)S(1)}, u32[]{:S(2)}, u32[]{:S(2)}) collective-permute-start(bf16[864,768]{1,0:T(8,128)(2,1)S(1)} %slice.1169), channel_id=1, source_target_pairs={{0,1},{1,0},{2,3},{3,2},{4,5},{5,4},{6,7},{7,6},{8,9},{9,8},{10,11... | collective-permute-start | bytes 3981320 | tf_op jit(solution)/shard_map/ppermute | solution.py:25
  371.2 38.7 %collective-permute-start.80 = (bf16[768,768]{1,0:T(8,128)(2,1)S(1)}, bf16[768,768]{1,0:T(8,128)(2,1)S(1)}, u32[]{:S(2)}, u32[]{:S(2)}) collective-permute-start(bf16[768,768]{1,0:T(8,128)(2,1)S(1)} %convolution_convert_fusion.10), channel_id=1, source_target_pairs={{0,8},{4,12},{24,16},{28,20},{1,9},{5,13},{25,17},{29,21},{2,10},{... | collective-permute-start | bytes 3538952 | tf_op jit(solution)/shard_map/ppermute | solution.py:125
  378.9 26.4 %collective-permute-start.88 = (bf16[384,768]{1,0:T(8,128)(2,1)S(1)}, bf16[384,768]{1,0:T(8,128)(2,1)S(1)}, u32[]{:S(2)}, u32[]{:S(2)}) collective-permute-start(bf16[384,768]{1,0:T(8,128)(2,1)S(1)} %dynamic-slice_bitcast_fusion.5), channel_id=1, source_target_pairs={{0,4},{4,0},{8,12},{12,8},{16,20},{20,16},{24,28},{28,24},{1,5},{5... | collective-permute-start | bytes 1769480 | tf_op jit(solution)/shard_map/ppermute | solution.py:112
  379.6 35.6 %collective-permute-start.19 = (bf16[864,768]{1,0:T(8,128)(2,1)S(1)}, bf16[864,768]{1,0:T(8,128)(2,1)S(1)}, u32[]{:S(2)}, u32[]{:S(2)}) collective-permute-start(bf16[864,768]{1,0:T(8,128)(2,1)S(1)} %slice.1161), channel_id=1, source_target_pairs={{0,1},{1,0},{2,3},{3,2},{4,5},{5,4},{6,7},{7,6},{8,9},{9,8},{10,11... | collective-permute-start | bytes 3981320 | tf_op jit(solution)/shard_map/ppermute | solution.py:25
  413.6 45.6 %collective-permute-start.97 = (bf16[768,768]{1,0:T(8,128)(2,1)}, bf16[768,768]{1,0:T(8,128)(2,1)}, u32[]{:S(2)}, u32[]{:S(2)}) collective-permute-start(bf16[768,768]{1,0:T(8,128)(2,1)} %pad_maximum_fusion.25), channel_id=1, source_target_pairs={{8,0},{12,4},{16,24},{20,28},{9,1},{13,5},{17,25},{21,29},{10,2},{... | collective-permute-start | bytes 3538952 | tf_op jit(solution)/shard_map/ppermute | solution.py:135
  455.7 25.7 %collective-permute-start.91 = (bf16[384,768]{1,0:T(8,128)(2,1)S(1)}, bf16[384,768]{1,0:T(8,128)(2,1)S(1)}, u32[]{:S(2)}, u32[]{:S(2)}) collective-permute-start(bf16[384,768]{1,0:T(8,128)(2,1)S(1)} %reduce-precision_convert_fusion.6), channel_id=1, source_target_pairs={{8,0},{12,4},{16,24},{20,28},{9,1},{13,5},{17,25},{21,29},{10,2},{... | collective-permute-start | bytes 1769480 | tf_op jit(solution)/shard_map/ppermute | solution.py:116
  465.3 32.3 %collective-permute-start.32 = (bf16[864,768]{1,0:T(8,128)(2,1)S(1)}, bf16[864,768]{1,0:T(8,128)(2,1)S(1)}, u32[]{:S(2)}, u32[]{:S(2)}) collective-permute-start(bf16[864,768]{1,0:T(8,128)(2,1)S(1)} %pad_maximum_fusion.18), channel_id=1, source_target_pairs={{0,1},{1,0},{2,3},{3,2},{4,5},{5,4},{6,7},{7,6},{8,9},{9,8},{10,11... | collective-permute-start | bytes 3981320 | tf_op jit(solution)/shard_map/ppermute | solution.py:25
  484.3 58.0 %collective-permute-start.84 = (bf16[768,768]{1,0:T(8,128)(2,1)}, bf16[768,768]{1,0:T(8,128)(2,1)}, u32[]{:S(2)}, u32[]{:S(2)}) collective-permute-start(bf16[768,768]{1,0:T(8,128)(2,1)} %pad_maximum_fusion.22), channel_id=1, source_target_pairs={{8,0},{12,4},{16,24},{20,28},{9,1},{13,5},{17,25},{21,29},{10,2},{... | collective-permute-start | bytes 3538952 | tf_op jit(solution)/shard_map/ppermute | solution.py:135
  522.8 43.6 %collective-permute-start.33 = (bf16[864,768]{1,0:T(8,128)(2,1)}, bf16[864,768]{1,0:T(8,128)(2,1)}, u32[]{:S(2)}, u32[]{:S(2)}) collective-permute-start(bf16[864,768]{1,0:T(8,128)(2,1)} %slice.1174), channel_id=1, source_target_pairs={{0,1},{1,0},{2,3},{3,2},{4,5},{5,4},{6,7},{7,6},{8,9},{9,8},{10,11... | collective-permute-start | bytes 3981320 | tf_op jit(solution)/shard_map/ppermute | solution.py:25
  530.8 25.6 %collective-permute-start.61 = (bf16[192,1152]{1,0:T(8,128)(2,1)S(1)}, bf16[192,1152]{1,0:T(8,128)(2,1)S(1)}, u32[]{:S(2)}, u32[]{:S(2)}) collective-permute-start(bf16[192,1152]{1,0:T(8,128)(2,1)S(1)} %get-tuple-element.101), channel_id=1, source_target_pairs={{0,3},{1,2},{2,1},{3,0},{4,7},{5,6},{6,5},{7,4},{8,11},{9,10},{10,... | collective-permute-start | bytes 1327112 | tf_op jit(solution)/shard_map/ppermute | solution.py:25
  565.6 31.4 %collective-permute-start.70 = (bf16[192,768]{1,0:T(8,128)(2,1)S(1)}, bf16[192,768]{1,0:T(8,128)(2,1)S(1)}, u32[]{:S(2)}, u32[]{:S(2)}) collective-permute-start(bf16[192,768]{1,0:T(8,128)(2,1)S(1)} %reduce-precision_convert_fusion.15), channel_id=1, source_target_pairs={{8,16},{12,20},{16,8},{20,12},{9,17},{13,21},{17,9},{21,13},{10,18... | collective-permute-start | bytes 884744 | tf_op jit(solution)/shard_map/ppermute | solution.py:132
  568.1 28.9 %collective-permute-start.34 = (bf16[432,768]{1,0:T(8,128)(2,1)S(1)}, bf16[432,768]{1,0:T(8,128)(2,1)S(1)}, u32[]{:S(2)}, u32[]{:S(2)}) collective-permute-start(bf16[432,768]{1,0:T(8,128)(2,1)S(1)} %slice.1462), channel_id=1, source_target_pairs={{0,2},{1,3},{2,0},{3,1},{4,6},{5,7},{6,4},{7,5},{8,10},{9,11},{10,... | collective-permute-start | bytes 1990664 | tf_op jit(solution)/shard_map/ppermute | solution.py:25
  578.1 35.4 %collective-permute-start.63 = (bf16[384,1152]{1,0:T(8,128)(2,1)S(1)}, bf16[384,1152]{1,0:T(8,128)(2,1)S(1)}, u32[]{:S(2)}, u32[]{:S(2)}) collective-permute-start(bf16[384,1152]{1,0:T(8,128)(2,1)S(1)} %fusion.43), channel_id=1, source_target_pairs={{0,8},{4,12},{24,16},{28,20},{1,9},{5,13},{25,17},{29,21},{2,10},{... | collective-permute-start | bytes 2654216 | tf_op jit(solution)/shard_map/ppermute | solution.py:113
  678.0 30.8 %collective-permute-start.48 = (bf16[192,576]{1,0:T(8,128)(2,1)}, bf16[192,576]{1,0:T(8,128)(2,1)S(1)}, u32[]{:S(2)}, u32[]{:S(2)}) collective-permute-start(bf16[192,576]{1,0:T(8,128)(2,1)} %get-tuple-element.175), channel_id=1, source_target_pairs={{0,3},{1,2},{2,1},{3,0},{4,7},{5,6},{6,5},{7,4},{8,11},{9,10},{10,... | collective-permute-start | bytes 663560 | tf_op jit(solution)/shard_map/ppermute | solution.py:25
  679.6 29.3 %collective-permute-start.47 = (bf16[192,576]{1,0:T(8,128)(2,1)}, bf16[192,576]{1,0:T(8,128)(2,1)S(1)}, u32[]{:S(2)}, u32[]{:S(2)}) collective-permute-start(bf16[192,576]{1,0:T(8,128)(2,1)} %get-tuple-element.176), channel_id=1, source_target_pairs={{0,2},{1,3},{2,0},{3,1},{4,6},{5,7},{6,4},{7,5},{8,10},{9,11},{10,... | collective-permute-start | bytes 663560 | tf_op jit(solution)/shard_map/ppermute | solution.py:25
  679.9 33.4 %collective-permute-start.46 = (bf16[192,576]{1,0:T(8,128)(2,1)}, bf16[192,576]{1,0:T(8,128)(2,1)S(1)}, u32[]{:S(2)}, u32[]{:S(2)}) collective-permute-start(bf16[192,576]{1,0:T(8,128)(2,1)} %get-tuple-element.177), channel_id=1, source_target_pairs={{0,1},{1,0},{2,3},{3,2},{4,5},{5,4},{6,7},{7,6},{8,9},{9,8},{10,11... | collective-permute-start | bytes 663560 | tf_op jit(solution)/shard_map/ppermute | solution.py:25
  687.5 25.9 %collective-permute-start.54 = (bf16[192,768]{1,0:T(8,128)(2,1)S(1)}, bf16[192,768]{1,0:T(8,128)(2,1)S(1)}, u32[]{:S(2)}, u32[]{:S(2)}) collective-permute-start(bf16[192,768]{1,0:T(8,128)(2,1)S(1)} %convolution_convert_fusion.13), channel_id=1, source_target_pairs={{0,8},{4,12},{24,16},{28,20},{1,9},{5,13},{25,17},{29,21},{2,10},{... | collective-permute-start | bytes 884744 | tf_op jit(solution)/shard_map/ppermute | solution.py:125
  708.8 47.7 %collective-permute-start.37 = (bf16[864,768]{1,0:T(8,128)(2,1)}, bf16[864,768]{1,0:T(8,128)(2,1)}, u32[]{:S(2)}, u32[]{:S(2)}) collective-permute-start(bf16[864,768]{1,0:T(8,128)(2,1)} %slice.1179), channel_id=1, source_target_pairs={{0,1},{1,0},{2,3},{3,2},{4,5},{5,4},{6,7},{7,6},{8,9},{9,8},{10,11... | collective-permute-start | bytes 3981320 | tf_op jit(solution)/shard_map/ppermute | solution.py:25
  740.6 34.1 %collective-permute-start.58 = (bf16[192,768]{1,0:T(8,128)(2,1)}, bf16[192,768]{1,0:T(8,128)(2,1)}, u32[]{:S(2)}, u32[]{:S(2)}) collective-permute-start(bf16[192,768]{1,0:T(8,128)(2,1)} %pad_maximum_fusion.40), channel_id=1, source_target_pairs={{8,0},{12,4},{16,24},{20,28},{9,1},{13,5},{17,25},{21,29},{10,2},{... | collective-permute-start | bytes 884744 | tf_op jit(solution)/shard_map/ppermute | solution.py:135
  (228 other events, 3013.9 us)

commit v2 on v1

v2 whole, which is shorter than its diff:
```python
import functools

import jax
import jax.numpy as jnp
import numpy as np
from jax import lax
from jax.experimental import pallas as pl
from jax.experimental.pallas import tpu as pltpu
from jax.sharding import PartitionSpec as P

HEADS = 12
WS = 12
SPAN = 2 * WS - 1
LANES = 256

epsilon = 1e-05
masked_fill = -1000000000.0
bf16 = jnp.bfloat16
f32 = jnp.float32
VMEM_BYTES = 48 * 1024 * 1024


def swap(tensor, axis, bit):
    count = lax.axis_size(axis)
    return lax.ppermute(tensor, axis, [(i, i ^ bit) for i in range(count)])


def bits_of(count):
    bits = []
    while count > 1:
        count //= 2
        bits.append(count)
    return bits


def gather_blocks(block, axis="win"):
    for bit in bits_of(lax.axis_size(axis)):
        block = jnp.concatenate([block, swap(block, axis, bit)], axis=0)
    return block


def scatter_sum(parts, axis="win"):
    bits = bits_of(lax.axis_size(axis))
    for bit in reversed(bits):
        half = parts.shape[0] // 2
        arrived = swap(parts[half:].astype(bf16), axis, bit)
        parts = parts[:half].astype(f32) + arrived.astype(f32)
    return parts


def total_sum(part, axis="win"):
    for bit in reversed(bits_of(lax.axis_size(axis))):
        mine = lax.reduce_precision(part.astype(f32), 8, 7)
        last = mine.astype(bf16)
        part = mine + swap(last, axis, bit).astype(f32)
    return part, last


def tiny_sum(part, axes):
    for axis in axes:
        for bit in reversed(bits_of(lax.axis_size(axis))):
            part = part + swap(part, axis, bit)
    return part


def pick(stack, index):
    return lax.dynamic_index_in_dim(stack, index, 0, False)


def trade(stack, axis="win"):
    count = lax.axis_size(axis)
    me = lax.axis_index(axis)
    return [pick(stack, me)] + [swap(pick(stack, me ^ k), axis, k) for k in range(1, count)]


def in_order(blocks, axis="win"):
    me = lax.axis_index(axis)
    stack = jnp.stack(blocks) if isinstance(blocks, (list, tuple)) else blocks
    return [pick(stack, me ^ j) for j in range(lax.axis_size(axis))]


def xor_order(count):
    order = [0]
    for bit in bits_of(count):
        order = order + [k ^ bit for k in order]
    return order


def rounded(tensor):
    return lax.reduce_precision(tensor, 8, 7)


def add_low(left, right):
    return rounded(left.astype(f32) + right.astype(f32)).astype(bf16)


LINE = 4


def line_swap(tensor, k):
    pairs = [(2 * a + x, 2 * (a ^ k) + x) for a in range(LINE) for x in (0, 1)]
    return lax.ppermute(tensor, "page", pairs)


def line_scatter(parts, depth):
    terms = [pick(parts, depth)] + [line_swap(pick(parts, depth ^ k), k) for k in range(1, LINE)]
    return rounded(total([t.astype(f32) for t in terms])).astype(bf16)


def line_gather(own):
    return [own] + [line_swap(own, k) for k in range(1, LINE)]


def exchange(blocks):
    return [blocks[0]] + [swap(blocks[k], "win", k) for k in range(1, len(blocks))]


def tie(first, *later):
    return lax.optimization_barrier((first,) + later)[1:]


def gather_four(block, axis="win"):
    count = lax.axis_size(axis)
    parts = [block]
    for bit in bits_of(count):
        parts = parts + [swap(p, axis, bit) for p in parts]
    return parts


def scatter_pieces(keep, send):
    bits = bits_of(lax.axis_size("win"))
    arrived = swap(send, "win", bits[-1])
    half = keep.shape[0] // 2
    second = (keep[half:].astype(f32) + arrived[half:].astype(f32)).astype(bf16)
    return (keep, arrived, swap(second, "win", bits[0])), second


def normalise(tensor):
    centre = tensor - jnp.mean(tensor, axis=-1, keepdims=True)
    spread = lax.rsqrt(jnp.mean(centre * centre, axis=-1, keepdims=True) + epsilon)
    return centre * spread, spread


def norm_low(tensor, gain):
    return (normalise(tensor)[0] * gain).astype(bf16)


def norm_back(tensor, gain, upstream):
    unit, spread = normalise(tensor)
    scaled = upstream * gain
    return spread * (
        scaled
        - jnp.mean(scaled, axis=-1, keepdims=True)
        - unit * jnp.mean(scaled * unit, axis=-1, keepdims=True)
    )


def gelu_both(hidden):
    phi = 0.5 * (1.0 + lax.erf(hidden * np.float32(np.sqrt(0.5))))
    density = jnp.exp(-0.5 * hidden * hidden) * np.float32(1.0 / np.sqrt(2.0 * np.pi))
    return hidden * phi, phi + hidden * density


def matmul(left, right):
    return jnp.dot(left, right, preferred_element_type=f32)


def left_tmul(left, right):
    return lax.dot_general(left, right, (((0,), (0,)), ((), ())), preferred_element_type=f32)


def right_tmul(left, right):
    return lax.dot_general(left, right, (((1,), (1,)), ((), ())), preferred_element_type=f32)


def pad_lanes(tensor, width):
    return jnp.pad(tensor, ((0, 0), (0, width - tensor.shape[1])))


def head_mask(head, head_size, width, scale):
    lane = lax.broadcasted_iota(jnp.int32, (1, width), 1)
    inside = (lane >= head * head_size) & (lane < (head + 1) * head_size)
    return jnp.where(inside, np.float32(scale), np.float32(0.0)).astype(bf16)


def softmax_rows(scores):
    peak = jnp.max(scores, axis=-1, keepdims=True)
    mass = jnp.exp(scores - peak)
    return mass * (1.0 / jnp.sum(mass, axis=-1, keepdims=True))


def by_head(tensor, heads, head_size, scale):
    return [tensor * head_mask(h, head_size, tensor.shape[1], scale) for h in range(heads)]


def total(terms):
    result = terms[0]
    for term in terms[1:]:
        result = result + term
    return result


def window_rows(spread_top, spread_low, before, after, window, cells):
    half = cells // 2
    return jnp.concatenate(
        [spread_top[window * half : (window + 1) * half], spread_low[window * half : (window + 1) * half]],
        axis=0,
    ).astype(bf16)


def pack_lanes(tensor, wide):
    rows, part = tensor.shape
    first = packed_rows(rows, part, wide)
    spare = wide - part
    tail = tensor[first:]
    side = [tail[:, s : s + spare] for s in range(0, part, spare)]
    rest = first - tail.shape[0] * len(side)
    side.append(jnp.zeros((rest, spare), tensor.dtype))
    return jnp.concatenate([tensor[:first], jnp.concatenate(side, axis=0)], axis=1)


def packed_rows(rows, part, wide):
    return -(-rows * part // (wide * 16)) * 16


def unpack_lanes(packed, rows, part):
    first, wide = packed.shape
    spare, tail = wide - part, rows - first
    side = packed[:, part:]
    last = jnp.concatenate([side[s * tail : (s + 1) * tail] for s in range(part // spare)], axis=1)
    return jnp.concatenate([packed[:, :part], last], axis=0)


def pick_block(blocks, place, target):
    for k, block in enumerate(blocks):

        @pl.when(place == k)
        def _(block=block):
            target[...] = block[: target.shape[0], :]


def window_forward_kernel(
    heads, head_size, scale, place, near, second, third, fourth, chunk, top_in, low_in, top_out, low_out,
    slots, rows, visual, weight, gains, norm, packed, mixed, before, after, held, chosen,
):
    step, last = pl.program_id(0), pl.num_programs(0) - 1
    cells = WS * WS
    half = cells // 2
    width = weight.shape[1] // 3
    blocks = (near, second, third, fourth)
    shards = len(blocks)
    me = place[shards]
    own, piece = chosen.shape[0], chunk.shape[0]

    @pl.when(step == 0)
    def _():
        before[...] = jnp.zeros_like(before)
        held[...] = jnp.zeros_like(held)
        order = xor_order(shards)
        starts = (None, own, own, own + piece)
        for p, k in enumerate(order):
            source = chunk[...] if p == 0 else blocks[p][starts[p] : starts[p] + piece, :]
            weight[pl.ds(pl.multiple_of((me ^ k) * piece, piece), piece), :] = source
        for device in range(shards):

            @pl.when(me == device)
            def _(device=device):
                lines = [None] * shards
                for p, k in enumerate(order):
                    lines[device ^ k] = blocks[p][blocks[p].shape[0] - 16 :, :piece].astype(f32)
                gains[...] = jnp.concatenate(lines, axis=1)

    @pl.when(step < last)
    def _():
        pick_block(blocks, place[jnp.minimum(step, last - 1)], chosen)
        visual[...] = chosen[...]
        low = norm_low(chosen[...].astype(f32), gains[0:1, :])
        norm[...] = low
        after[...] = matmul(low, weight[...]).astype(bf16)
        packed[...] = after[...]

    @pl.when(step == last)
    def _():
        after[...] = jnp.zeros_like(after)

    top = matmul(top_in[...], before[...])
    low = matmul(low_in[...], after[...])
    upper, lower = [], []
    for j in range(top.shape[0] // half):
        part = window_rows(top, low, before, after, j, cells)
        query, key, value = part[:, :width], part[:, width : 2 * width], part[:, 2 * width :]
        stacked = jnp.concatenate(by_head(query, heads, head_size, scale), axis=0)
        mask = slots[j * heads * cells : (j + 1) * heads * cells, :] + rows[0]
        probs = softmax_rows(right_tmul(stacked, key) + mask).astype(bf16)
        values = by_head(value, heads, head_size, 1.0)
        result = total([matmul(probs[h * cells : (h + 1) * cells], values[h]) for h in range(heads)])
        upper.append(result[:half])
        lower.append(result[half:])
    above = matmul(top_out[...], jnp.concatenate(upper, axis=0).astype(bf16))
    below = matmul(low_out[...], jnp.concatenate(lower, axis=0).astype(bf16))

    @pl.when(step > 0)
    def _():
        block = jnp.concatenate([held[...], above], axis=0)
        mixed[...] = pack_lanes(block[:, : heads * head_size], width).astype(bf16)

    held[...] = below
    before[...] = after[...]


def window_backward_kernel(
    heads, head_size, scale, place, near, second, third, fourth, packed, mixed, weight_out, weight, top_in,
    low_in, top_out, low_out, slots, rows, grads, dnorm, bias_out, out_grad, before, after, top_before,
    top_after, held, upper, lower, upstream,
):
    step, last = pl.program_id(0), pl.num_programs(0) - 1
    cells = WS * WS
    half = cells // 2
    width = weight.shape[1] // 3

    @pl.when(step == 0)
    def _():
        before[...] = jnp.zeros_like(before)
        top_before[...] = jnp.zeros_like(top_before)
        bias_out[...] = jnp.zeros_like(bias_out)
        out_grad[...] = jnp.zeros_like(out_grad)
        held[...] = jnp.zeros_like(held)

    @pl.when(step < last)
    def _():
        pick_block((near, second, third, fourth), place[jnp.minimum(step, last - 1)], upstream)
        after[...] = packed[...]
        top_after[...] = right_tmul(upstream[...], weight_out[...]).astype(bf16)
        whole_heads = unpack_lanes(mixed[...], upstream.shape[0], heads * head_size)
        out_grad[...] += left_tmul(whole_heads, upstream[...])

    @pl.when(step == last)
    def _():
        after[...] = jnp.zeros_like(after)
        top_after[...] = jnp.zeros_like(top_after)

    top = matmul(top_in[...], before[...])
    low = matmul(low_in[...], after[...])
    given_top = matmul(top_in[...], top_before[...])
    given_low = matmul(low_in[...], top_after[...])
    for j in range(top.shape[0] // half):
        part = window_rows(top, low, before, after, j, cells)
        given = window_rows(given_top, given_low, before, after, j, cells)
        query, key, value = part[:, :width], part[:, width : 2 * width], part[:, 2 * width :]
        stacked = jnp.concatenate(by_head(query, heads, head_size, scale), axis=0)
        mask = slots[j * heads * cells : (j + 1) * heads * cells, :] + rows[0]
        probs = softmax_rows(right_tmul(stacked, key) + mask)
        given = jnp.concatenate(by_head(given, heads, head_size, 1.0), axis=0)
        dprobs = right_tmul(given, value)
        inner = jnp.sum(probs * dprobs, axis=-1, keepdims=True)
        dscores = (probs * (dprobs - inner)).astype(bf16)
        bias_out[...] += dscores.astype(f32)
        keys = by_head(key, heads, head_size, scale)
        dquery = total([matmul(dscores[h * cells : (h + 1) * cells], keys[h]) for h in range(heads)])
        dkey = left_tmul(dscores, stacked)
        dvalue = left_tmul(probs.astype(bf16), given)
        for s, result in enumerate((dquery, dkey, dvalue)):
            upper[j * half : (j + 1) * half, s * width : (s + 1) * width] = result[:half]
            lower[j * half : (j + 1) * half, s * width : (s + 1) * width] = result[half:]
    above = matmul(top_out[...], upper[...].astype(bf16))
    below = matmul(low_out[...], lower[...].astype(bf16))

    block = jnp.concatenate([held[...], above], axis=0).astype(bf16)
    grads[...] = block
    held[...] = below
    dnorm[...] = right_tmul(block, weight[...]).astype(bf16)
    before[...] = after[...]
    top_before[...] = top_after[...]


def middle_kernel(
    heads, head_size, scale, visual, own, second, third, fourth, out_own, out_second, out_third, out_fourth,
    gains, weight, keys, values, live, mid, norm, proj, mixed,
):
    pieces = (own, second, third, fourth)
    weights = (out_own, out_second, out_third, out_fourth)
    part = heads * head_size
    result = visual[...].astype(f32) + total(
        [matmul(unpack_lanes(p[...], mid.shape[0], part), w[...]) for p, w in zip(pieces, weights)]
    )
    mid[...] = result
    low = norm_low(result, gains[1:2, :])
    norm[...] = low
    packed = matmul(low, weight[...]).astype(bf16)
    proj[...] = packed
    width = keys.shape[1]
    query = by_head(packed[:, 2 * width :], heads, head_size, scale)
    value = by_head(values[...], heads, head_size, 1.0)
    terms = []
    for h in range(heads):
        probs = softmax_rows(right_tmul(query[h], keys[...]) + live[...])
        terms.append(matmul(probs.astype(bf16), value[h]))
    mixed[...] = pack_lanes(total(terms)[:, :part], width).astype(bf16)


def feed_kernel(
    part, place, mid, own, second, third, fourth, weight_out, gains, up, down, cotangent,
    late, norm, act, dhidden, keep, send,
):
    step, halfway = pl.program_id(0), pl.num_programs(0) // 2
    pieces = (own, second, third, fourth)
    terms = []
    for piece, k in zip(pieces, xor_order(len(pieces))):
        rows = weight_out[pl.ds(pl.multiple_of((place[0] ^ k) * part, part), part), :]
        terms.append(matmul(unpack_lanes(piece[...], mid.shape[0], part), rows))
    result = mid[...] + total(terms)

    @pl.when(step == 0)
    def _():
        late[...] = result

    low = norm_low(result, gains[3:4, :])
    norm[...] = low
    value, slope = gelu_both(matmul(low, up[...]))
    act[...] = value.astype(bf16)
    back = (right_tmul(cotangent[...], down[...]) * slope).astype(bf16)
    dhidden[...] = back
    dnorm = right_tmul(back, up[...]).astype(bf16)

    @pl.when(step < halfway)
    def _():
        keep[...] = dnorm

    @pl.when(step >= halfway)
    def _():
        send[...] = dnorm


def query_scores(query, keys_vis, keys_qry, causal, mask):
    masked = query * mask
    return masked, right_tmul(masked, keys_vis), right_tmul(masked, keys_qry) + causal


def joint_softmax(score_vis, score_qry):
    peak = jnp.maximum(
        jnp.max(score_vis, axis=-1, keepdims=True), jnp.max(score_qry, axis=-1, keepdims=True)
    )
    mass_vis = jnp.exp(score_vis - peak)
    mass_qry = jnp.exp(score_qry - peak)
    inverse = 1.0 / (
        jnp.sum(mass_vis, axis=-1, keepdims=True) + jnp.sum(mass_qry, axis=-1, keepdims=True)
    )
    return mass_vis * inverse, mass_qry * inverse


def query_forward_kernel(
    heads, head_size, scale, query, keys_qry, values_qry, keys_vis, values_vis, causal, out
):
    width = query.shape[1]
    terms = []
    for h in range(heads):
        _, score_vis, score_qry = query_scores(
            query[...], keys_vis[...], keys_qry[...], causal[...], head_mask(h, head_size, width, scale)
        )
        prob_vis, prob_qry = joint_softmax(score_vis, score_qry)
        mask = head_mask(h, head_size, width, 1.0)
        terms.append(matmul(prob_vis.astype(bf16), values_vis[...] * mask))
        terms.append(matmul(prob_qry.astype(bf16), values_qry[...] * mask))
    out[...] = total(terms).astype(bf16)[:, : out.shape[1]]


def query_backward_kernel(
    heads, head_size, scale, query, keys_qry, values_qry, keys_vis, values_vis, causal, upstream,
    dquery, dkeys_qry, dvalues_qry, dkeys_vis, dvalues_vis,
):
    width = query.shape[1]
    sums = [[], [], [], [], []]
    for h in range(heads):
        masked, score_vis, score_qry = query_scores(
            query[...], keys_vis[...], keys_qry[...], causal[...], head_mask(h, head_size, width, scale)
        )
        prob_vis, prob_qry = joint_softmax(score_vis, score_qry)
        given = upstream[...] * head_mask(h, head_size, width, 1.0)
        dprob_vis = right_tmul(given, values_vis[...])
        dprob_qry = right_tmul(given, values_qry[...])
        inner = jnp.sum(prob_vis * dprob_vis, axis=-1, keepdims=True) + jnp.sum(
            prob_qry * dprob_qry, axis=-1, keepdims=True
        )
        dscore_vis = (prob_vis * (dprob_vis - inner)).astype(bf16)
        dscore_qry = (prob_qry * (dprob_qry - inner)).astype(bf16)
        mask = head_mask(h, head_size, width, scale)
        sums[0].append(matmul(dscore_vis, keys_vis[...] * mask))
        sums[0].append(matmul(dscore_qry, keys_qry[...] * mask))
        sums[1].append(left_tmul(dscore_qry, masked))
        sums[2].append(left_tmul(prob_qry.astype(bf16), given))
        sums[3].append(left_tmul(dscore_vis, masked))
        sums[4].append(left_tmul(prob_vis.astype(bf16), given))
    for ref, terms in zip((dquery, dkeys_qry, dvalues_qry, dkeys_vis, dvalues_vis), sums):
        ref[...] = total(terms).astype(bf16)


def cross_backward_kernel(
    heads, head_size, scale, proj, keys, values, live, near, second, third, fourth, weight_out, mixed,
    dkeys_vis, dvalues_vis, weight, dproj, dkeys, dvalues, out_grad, keep, send, upstream,
):
    step, halfway = pl.program_id(0), pl.num_programs(0) // 2
    width = keys.shape[1]

    @pl.when(step == 0)
    def _():
        dkeys[...] = jnp.zeros_like(dkeys)
        dvalues[...] = jnp.zeros_like(dvalues)
        out_grad[...] = jnp.zeros_like(out_grad)

    pick_block((near, second, third, fourth), step, upstream)
    out_grad[...] += left_tmul(unpack_lanes(mixed[...], upstream.shape[0], heads * head_size), upstream[...])
    top = right_tmul(upstream[...], weight_out[...]).astype(bf16)
    query = by_head(proj[:, 2 * width :], heads, head_size, scale)
    given = by_head(top, heads, head_size, 1.0)
    scaled = by_head(keys[...], heads, head_size, scale)
    terms = []
    for h in range(heads):
        probs = softmax_rows(right_tmul(query[h], keys[...]) + live[...])
        dprobs = right_tmul(given[h], values[...])
        inner = jnp.sum(probs * dprobs, axis=-1, keepdims=True)
        dscores = (probs * (dprobs - inner)).astype(bf16)
        terms.append(matmul(dscores, scaled[h]))
        dkeys[...] += left_tmul(dscores, query[h])
        dvalues[...] += left_tmul(probs.astype(bf16), given[h])
    block = jnp.concatenate([dkeys_vis[...], dvalues_vis[...], total(terms).astype(bf16)], axis=1)
    dproj[...] = block
    dnorm = right_tmul(block, weight[...]).astype(bf16)

    @pl.when(step < halfway)
    def _():
        keep[...] = dnorm

    @pl.when(step >= halfway)
    def _():
        send[...] = dnorm


def norm_back_kernel(line, tensor, gains, first, second, third, residual, *outs):
    upstream = first[...].astype(f32) + second[...].astype(f32) + third[...].astype(f32)
    gain = gains[line : line + 1, :]
    result = residual[...].astype(f32) + norm_back(tensor[...].astype(f32), gain, upstream)
    for out in outs:
        out[...] = result.astype(out.dtype)


def split_columns_kernel(shards, pieces, place, *refs):
    weights, outs = refs[: len(pieces)], refs[len(pieces) :]
    for me in range(shards):

        @pl.when(place[0] == me)
        def _(me=me):
            for k in range(shards):
                j = me ^ k
                blocks = []
                for weight, count in zip(weights, pieces):
                    step = weight.shape[1] // (count * shards)
                    for s in range(count):
                        start = (s * shards + j) * step
                        blocks.append(weight[:, start : start + step])
                outs[k][...] = jnp.concatenate(blocks, axis=1)


def join_rows_kernel(shards, part, wide, place, *refs):
    blocks, out = refs[:shards], refs[shards]
    rows = blocks[0].shape[0]
    for k in range(shards):
        block = blocks[k][...]
        if wide != part:
            gap = jnp.zeros((rows, wide - part), block.dtype)
            columns = []
            for start in range(0, block.shape[1], part):
                columns += [block[:, start : start + part], gap]
            block = jnp.concatenate(columns, axis=1)
        out[pl.ds(pl.multiple_of((place[0] ^ k) * rows, rows), rows), :] = block


def entry_kernel(shards, pieces, wide, place, visual, weight, gains, to_far, to_near, chunk):
    own, rows = visual.shape[0], weight.shape[0]
    part = weight.shape[1] // (pieces * shards)
    lanes = visual.shape[1]
    gap = jnp.zeros((rows, wide - part), bf16)
    line = jnp.concatenate([gains[...], jnp.zeros((gains.shape[0], lanes - gains.shape[1]), bf16)], axis=1)
    to_far[:own, :] = visual[...]
    to_near[:own, :] = visual[...]
    to_far[own + 2 * rows :, :] = line
    to_near[own + rows :, :] = line
    for me in range(shards):

        @pl.when(place[0] == me)
        def _(me=me):
            for k in range(shards):
                columns = []
                for s in range(pieces):
                    start = (s * shards + (me ^ k)) * part
                    columns += [weight[:, start : start + part], gap]
                block = jnp.concatenate(columns, axis=1)
                if k == 0:
                    chunk[...] = block
                elif k == 1:
                    to_near[own : own + rows, :] = block
                else:
                    to_far[own + (k - 2) * rows : own + (k - 1) * rows, :] = block


def share_kernel(shards, place, first, second, third, *refs):
    outs, stack = refs[:shards], refs[shards]
    rows, model = third.shape
    height = outs[0].shape[0]
    start = pl.multiple_of(place[1] * height, 16)
    if stack.shape[0] > 3 * rows:
        stack[3 * rows :, :] = jnp.zeros((stack.shape[0] - 3 * rows, model), bf16)
    stack[2 * rows : 3 * rows, :] = third[...]
    for me in range(shards):

        @pl.when(place[0] == me)
        def _(me=me):
            for k in range(shards):
                j = me ^ k
                stack[:rows, :] = first[:, j * model : (j + 1) * model]
                stack[rows : 2 * rows, :] = second[:, j * model : (j + 1) * model]
                outs[k][...] = stack[pl.ds(start, height), :]


def unshare_kernel(place, given, out):
    pages, shards, height, model = given.shape
    rows = model // shards
    for k in range(shards):
        block = given[:, k].reshape(pages * height, model)
        for i in range(3):
            start = pl.multiple_of(i * model + (place[0] ^ k) * rows, rows)
            out[pl.ds(start, rows), :] = block[i * rows : (i + 1) * rows]


GROUPS = 8


def feed_grads_kernel(shards, norm, dhidden, act, top, norm_qry, dhidden_qry, act_qry, top_qry, out):
    up_share = 2 * norm.shape[1] // (shards * GROUPS)
    down_share = 2 * act.shape[1] // GROUPS
    size = shards * up_share + down_share
    halfway = GROUPS // 2
    ups = ((norm, dhidden), (norm_qry, dhidden_qry))
    downs = ((act, top), (act_qry, top_qry))
    for k in range(2):

        @pl.when(pl.program_id(0) == k)
        def _(k=k):
            left, right = ups[k]
            result = left_tmul(left[...], right[...]).astype(bf16)
            for g in range(halfway):
                for j in range(shards):
                    start = (j * halfway + g) * up_share
                    to = (k * halfway + g) * size + j * up_share
                    out[to : to + up_share, :] = result[start : start + up_share]

        @pl.when(pl.program_id(0) == k + 2)
        def _(k=k):
            left, right = downs[k]
            result = left_tmul(left[...], right[...]).astype(bf16)
            for g in range(halfway):
                to = (k * halfway + g) * size + shards * up_share
                out[to : to + down_share, :] = result[g * down_share : (g + 1) * down_share]


def lay_out_feed_kernel(shards, place, given, up, up_qry, down, down_qry):
    halfway = GROUPS // 2
    up_share, down_share = up.shape[0] // halfway, down.shape[0] // halfway
    size, width = shards * up_share + down_share, given.shape[1]
    for me in range(shards):

        @pl.when(place[0] == me)
        def _(me=me):
            for g in range(GROUPS):
                out = (up, up_qry)[g // halfway]
                to = g % halfway * up_share
                for j in range(shards):
                    start = g * size + (me ^ j) * up_share
                    out[to : to + up_share, j * width : (j + 1) * width] = given[start : start + up_share, :].astype(f32)

    for g in range(GROUPS):
        out = (down, down_qry)[g // halfway]
        to, start = g % halfway * down_share, g * size + shards * up_share
        out[to : to + down_share, :] = given[start : start + down_share, :].astype(f32)


def split_halves_kernel(shards, part, wide, place, *refs):
    grads, keep, give = refs[:-2], refs[-2], refs[-1]
    rows = grads[0].shape[0] // shards
    half = rows // 2
    for k in range(shards):
        for out, side in ((keep, place[1]), (give, 1 - place[1])):
            start = pl.multiple_of((place[0] ^ k) * rows + side * half, half)
            columns = []
            for grad in grads:
                block = grad[pl.ds(start, half), :]
                columns += [block[:, c : c + part] for c in range(0, block.shape[1], wide)]
            out[k * half : (k + 1) * half, :] = jnp.concatenate(columns, axis=1).astype(bf16)


def lay_out_kernel(shards, pieces, halves, place, *refs):
    blocks, outs = refs[: 2 if halves else 1], refs[2 if halves else 1 :]
    rows = blocks[0].shape[0] // shards
    for me in range(shards):

        @pl.when(place[0] == me)
        def _(me=me):
            start = 0
            for out, count in zip(outs, pieces):
                step = out.shape[1] // (count * shards)
                for b, block in enumerate(blocks):
                    columns = []
                    for s in range(count):
                        for j in range(shards):
                            k = me ^ j
                            columns.append(
                                block[k * rows : (k + 1) * rows, start + s * step : start + (s + 1) * step]
                            )
                    result = jnp.concatenate(columns, axis=1).astype(f32)
                    if halves:
                        side = place[1] if b == 0 else 1 - place[1]
                        out[pl.ds(pl.multiple_of(side * rows, rows), rows), :] = result
                    else:
                        out[...] = result
                start += step * count


def kernel_call(function, grid, ins, outs, args, scratch=(), place=None, name=None, us=2):
    prefetch = () if place is None else (place,)
    return pl.pallas_call(
        function,
        grid_spec=pltpu.PrefetchScalarGridSpec(
            num_scalar_prefetch=len(prefetch),
            grid=grid,
            in_specs=ins,
            out_specs=[spec for spec, _ in outs],
            scratch_shapes=list(scratch),
        ),
        out_shape=[shape for _, shape in outs],
        compiler_params=pltpu.CompilerParams(vmem_limit_bytes=VMEM_BYTES),
        cost_estimate=pl.CostEstimate(flops=us * 10**6, bytes_accessed=10**3, transcendentals=0),
        name=name,
    )(*prefetch, *args)


def whole(shape):
    return pl.BlockSpec(tuple(shape), lambda *_: (0,) * len(shape))


def all_of(*arrays):
    return [whole(a.shape) for a in arrays]


def full_out(shape, dtype):
    return whole(shape), jax.ShapeDtypeStruct(tuple(shape), dtype)


def window_places(page_width):
    half = WS // 2
    columns = page_width // WS + 1
    top = np.zeros((columns * half * WS, WS * page_width), np.float32)
    low = np.zeros_like(top)
    for j in range(columns):
        for r in range(half):
            for c in range(WS):
                column = j * WS + c - half
                if 0 <= column < page_width:
                    place = (j * half + r) * WS + c
                    top[place, (half + r) * page_width + column] = 1.0
                    low[place, r * page_width + column] = 1.0
    cut = half * page_width
    return [jnp.asarray(m, bf16) for m in (top, low, top[:, cut:].T, low[:, :cut].T)]


def bias_slots(table, regions, page_width):
    half = WS // 2
    columns = page_width // WS + 1
    heads = table.shape[0]
    flipped = table.reshape(heads, SPAN, SPAN)[:, ::-1, ::-1]
    wide = jnp.stack([flipped[:, :, WS - 1 - c : 2 * WS - 1 - c] for c in range(WS)], axis=1)
    wide = wide.reshape(heads, WS, SPAN * WS)
    bias = jnp.stack(
        [wide[:, :, (WS - 1 - r) * WS : (2 * WS - 1 - r) * WS] for r in range(WS)], axis=1
    ).reshape(heads, WS * WS, WS * WS)
    padded = jnp.pad(regions, (half, half), constant_values=-1).reshape(columns, WS)
    of_place = jnp.tile(padded, (1, WS))
    allowed = (of_place[:, :, None] == of_place[:, None, :]) & (of_place[:, None, :] >= 0)
    mask = jnp.where(allowed, 0.0, masked_fill).astype(f32)
    slots = bias[None] + mask[:, None]
    return slots.reshape(columns * heads * WS * WS, WS * WS)


def bias_gather(grad, heads):
    shaped = grad.reshape(heads, WS, WS, WS * WS)
    wide = sum(
        jnp.pad(shaped[:, r], ((0, 0), (0, 0), ((WS - 1 - r) * WS, r * WS))) for r in range(WS)
    ).reshape(heads, WS, SPAN, WS)
    flipped = wide[:, :, ::-1, ::-1]
    table = sum(jnp.pad(flipped[:, c], ((0, 0), (0, 0), (c, WS - 1 - c))) for c in range(WS))
    return table.reshape(heads, SPAN * SPAN)


def body(
    visual,
    queries,
    query_lengths,
    column_regions,
    gain_window,
    window_qkv,
    window_out,
    position_bias,
    gain_visual,
    gain_query,
    attend_query,
    attend_kv,
    attend_out,
    cross_query,
    cross_kv,
    cross_out,
    gain_feed,
    visual_up,
    visual_down,
    gain_query_feed,
    query_up,
    query_down,
    cotangent_visual,
    cotangent_query,
):
    shards = lax.axis_size("win")
    pages = lax.axis_size("page")
    me = lax.axis_index("win").astype(jnp.int32)
    page = lax.axis_index("page").astype(jnp.int32)
    row_count, page_width, model = visual.shape[1:]
    own = row_count * page_width
    tokens = own * shards
    slots_count = queries.shape[1]
    heads = HEADS // shards
    head_size = model // HEADS
    part = heads * head_size
    wide = -(-part // LANES) * LANES
    static = (heads, head_size, head_size ** (-0.5))
    stripes = shards + 1
    rows = model // shards
    hidden = visual_down.shape[0]
    order = xor_order(shards)
    where_me = me.reshape(1)
    where_page = jnp.stack([me, page % 2])
    short = packed_rows(own, part, wide)

    def block_of(width, column=0):
        return pl.BlockSpec((own, width), lambda i, *_: (i, column))

    def token_out(width, dtype=bf16):
        return block_of(width), jax.ShapeDtypeStruct((tokens, width), dtype)

    def packed_block():
        return pl.BlockSpec((short, wide), lambda i, *_: (i, 0))

    def packed_out():
        return packed_block(), jax.ShapeDtypeStruct((short * shards, wide), bf16)

    def half_outs():
        shape = jax.ShapeDtypeStruct((tokens // 2, model), bf16)
        count = shards // 2
        return [
            (pl.BlockSpec((own, model), lambda i, *_: (jnp.minimum(i, count - 1), 0)), shape),
            (pl.BlockSpec((own, model), lambda i, *_: (jnp.maximum(i - count, 0), 0)), shape),
        ]

    gains = jnp.concatenate(
        [gain_window, gain_visual, gain_query, gain_feed, gain_query_feed, jnp.zeros((11 * rows,), bf16)]
    ).reshape(16, rows)
    to_far, to_near, chunk = kernel_call(
        functools.partial(entry_kernel, shards, 3, wide),
        (1,),
        [whole((own, model)), whole(window_qkv.shape), whole(gains.shape)],
        [
            full_out((own + 2 * rows + 16, model), bf16),
            full_out((own + rows + 16, model), bf16),
            full_out((rows, 3 * wide), bf16),
        ],
        (visual[0].reshape(own, model), window_qkv, gains),
        place=where_me,
        name="entry",
    )
    far = swap(to_far, "win", 2)
    near = swap(to_near, "win", 1)
    slots = bias_slots(position_bias.astype(f32), column_regions[0], page_width)
    far_now = tie(slots, far)[0]
    both = swap(far_now, "win", 1)

    height = -(-3 * rows // (16 * pages)) * 16
    shares = kernel_call(
        functools.partial(share_kernel, shards),
        (1,),
        all_of(visual_up, query_up, cross_out),
        [full_out((height, model), bf16)] * shards,
        (visual_up, query_up, cross_out),
        scratch=[pltpu.VMEM((height * pages, model), bf16)],
        place=jnp.stack([me, page]),
        name="share",
    )
    spread_weights = lax.all_gather(jnp.stack(exchange(shares)), "page")

    tied = tie(far, attend_kv, cross_query, attend_query, cross_kv, window_out)
    mixed_width = 6 * part
    blocks = kernel_call(
        functools.partial(split_columns_kernel, shards, [2, 1, 1, 2]),
        (1,),
        all_of(*tied[:4]),
        [full_out((rows, mixed_width), bf16)] * shards,
        tied[:4],
        place=where_me,
        name="split_columns",
    )
    mixed_parts = exchange(blocks)
    out_parts = gather_four(tied[4])

    both = tie(blocks[1], both)[0]
    places = window_places(page_width)
    row_mask = np.zeros((stripes, 1, WS * WS), np.float32)
    row_mask[0, :, : WS * WS // 2] = masked_fill
    row_mask[-1, :, WS * WS // 2 :] = masked_fill
    row_mask = jnp.asarray(row_mask)
    position = jnp.asarray(np.argsort(order), jnp.int32)[me ^ jnp.arange(shards, dtype=jnp.int32)]
    position = jnp.concatenate([position, where_me])

    def arriving(width, height=own):
        return pl.BlockSpec((height, width), lambda i, at: (at[jnp.minimum(i, shards - 1)], 0))

    def leaving(width, height=own):
        return pl.BlockSpec((height, width), lambda i, at: (at[jnp.maximum(i - 1, 0)], 0))

    def of_tokens(spec, width):
        return spec(width), jax.ShapeDtypeStruct((tokens, width), bf16)

    window_specs = all_of(*places, slots) + [pl.BlockSpec((1, 1, WS * WS), lambda i, at: (i, 0, 0))]
    window_args = (*places, slots, row_mask)
    vis_low, qkv_w, gains_all, norm_win, packed, heads_win = kernel_call(
        functools.partial(window_forward_kernel, *static),
        (stripes,),
        all_of(to_far, far, near, both, chunk) + window_specs,
        [
            of_tokens(arriving, model),
            full_out((model, 3 * wide), bf16),
            full_out((16, model), f32),
            of_tokens(arriving, model),
            of_tokens(arriving, 3 * wide),
            (leaving(wide, short), jax.ShapeDtypeStruct((short * shards, wide), bf16)),
        ],
        (to_far, far, near, both, chunk) + window_args,
        scratch=[pltpu.VMEM((own, 3 * wide), bf16)] * 2
        + [pltpu.VMEM((own // 2, wide), f32), pltpu.VMEM((own, model), bf16)],
        place=position,
        name="window_forward",
        us=17,
    )
    win_parts = gather_four(heads_win)

    tied = tie(heads_win, *mixed_parts)
    mixed_w = kernel_call(
        functools.partial(join_rows_kernel, shards, part, wide),
        (1,),
        all_of(*tied),
        [full_out((model, 6 * wide), bf16)],
        tied,
        place=where_me,
        name="join_rows",
    )[0]
    vis_w = mixed_w[:, : 3 * wide]
    qry_w = jnp.concatenate(
        [mixed_w[:, 3 * wide : 4 * wide], mixed_w[:, : 2 * wide], mixed_w[:, 4 * wide :]], axis=1
    )
    query_in = queries[0].astype(f32)
    norm_qry = norm_low(query_in, gains_all[2:3])
    proj_qry = matmul(norm_qry, qry_w).astype(bf16)
    length = query_lengths[0]
    slot_ids = jnp.arange(slots_count, dtype=jnp.int32)
    live = slot_ids < length
    live_mask = jnp.where(live, 0.0, masked_fill).astype(f32)[None]
    reach = (slot_ids[None, :] <= slot_ids[:, None]) & live[None, :]
    causal_mask = jnp.where(reach, 0.0, masked_fill).astype(f32)
    tied = tie(win_parts[1], attend_out, cotangent_visual)
    attend_parts = gather_four(tied[0])
    top_parts = gather_four(tied[1][0].reshape(own, model))

    def qry_piece(i):
        return pl.BlockSpec((slots_count, wide), lambda *_: (0, i))

    def vis_piece(i):
        return pl.BlockSpec((tokens, wide), lambda *_: (0, i))

    def piece_specs():
        return [pl.BlockSpec((short, wide), lambda i, *_, k=k: (i ^ k, 0)) for k in range(shards)]

    mid, norm_vis, proj_vis, heads_cross = kernel_call(
        functools.partial(middle_kernel, *static),
        (shards,),
        [block_of(model)]
        + piece_specs()
        + all_of(*out_parts, gains_all, vis_w)
        + [qry_piece(3), qry_piece(4)]
        + all_of(live_mask),
        [token_out(model, f32), token_out(model), token_out(3 * wide), packed_out()],
        (vis_low, *win_parts, *out_parts, gains_all, vis_w, proj_qry, proj_qry, live_mask),
        name="middle",
        us=13,
    )
    cross_parts = gather_four(heads_cross)

    query_specs = [
        qry_piece(0),
        qry_piece(1),
        qry_piece(2),
        vis_piece(0),
        vis_piece(1),
        whole(causal_mask.shape),
    ]
    query_args = (proj_qry, proj_qry, proj_qry, proj_vis, proj_vis, causal_mask)
    (heads_qry,) = kernel_call(
        functools.partial(query_forward_kernel, *static),
        (1,),
        query_specs,
        [full_out((slots_count, part), bf16)],
        query_args,
        name="query_forward",
        us=4,
    )
    qry_parts = gather_four(heads_qry)
    tied = tie(heads_qry, spread_weights, *top_parts)
    (three,) = kernel_call(
        unshare_kernel,
        (1,),
        all_of(tied[0]),
        [full_out((3 * model, model), bf16)],
        (tied[0],),
        place=where_me,
        name="unshare",
    )
    vup_w, qup_w, cross_out_w = [three[i * model : (i + 1) * model] for i in range(3)]
    top_low = jnp.concatenate(tied[1:], axis=0)
    top_now = tie(qry_parts[3], *tie(attend_parts[3], top_low))[0]

    late, norm_feed, act_vis, dhid_vis, feed_keep, feed_send = kernel_call(
        functools.partial(feed_kernel, part),
        (shards,),
        [block_of(model)]
        + piece_specs()
        + all_of(cross_out_w, gains_all, vup_w, visual_down)
        + [block_of(model)],
        [full_out((own, model), f32), token_out(model), token_out(hidden), token_out(hidden)] + half_outs(),
        (mid, *cross_parts, cross_out_w, gains_all, vup_w, visual_down, top_now),
        place=where_me,
        name="feed",
        us=18,
    )
    feed_terms, feed_second = scatter_pieces(feed_keep, feed_send)

    tied = tie(feed_second, *qry_parts, *attend_parts)
    query_mid = query_in + matmul(
        jnp.concatenate(tied[:shards], axis=1), jnp.concatenate(tied[shards:], axis=0)
    )
    norm_qfeed = norm_low(query_mid, gains_all[4:5])
    act_qry, slope_qry = gelu_both(matmul(norm_qfeed, qup_w))
    act_qry = act_qry.astype(bf16)
    dhid_qry = (right_tmul(cotangent_query[0], query_down) * slope_qry).astype(bf16)
    dqfeed_part = right_tmul(dhid_qry, qup_w)
    dqfeed, dqfeed_last = total_sum(dqfeed_part)
    pairs = (norm_feed, dhid_vis, act_vis, top_low, norm_qfeed, dhid_qry, act_qry, cotangent_query[0])
    pairs = tie(dqfeed_last, *tie(feed_second, *pairs))
    (feed_grads,) = kernel_call(
        functools.partial(feed_grads_kernel, shards),
        (4,),
        all_of(*pairs),
        [full_out((4 * hidden, model), bf16)],
        pairs,
        name="feed_grads",
        us=10,
    )
    up_share, down_share = 2 * rows // GROUPS, 2 * hidden // GROUPS

    def to_sources(group):
        stack = group[: shards * up_share].reshape(shards, up_share, model)
        return jnp.concatenate(trade(stack) + [group[shards * up_share :]], axis=0)

    if pages == GROUPS:
        feed_sum = to_sources(lax.psum_scatter(feed_grads, "page", scatter_dimension=0, tiled=True))
    else:
        summed = lax.psum(feed_grads, "page").reshape(GROUPS, -1, model)
        feed_sum = jnp.concatenate([to_sources(summed[g]) for g in range(GROUPS)], axis=0)

    def back_through_norm(line, tensor, terms, residual, dtypes):
        own_block = pl.BlockSpec((own, model), lambda *_: (0, 0))
        return kernel_call(
            functools.partial(norm_back_kernel, line),
            (1,),
            [own_block, whole(gains_all.shape)] + [own_block] * 4,
            [(own_block, jax.ShapeDtypeStruct((own, model), d)) for d in dtypes],
            (tensor, gains_all, *terms, residual),
            name="norm_back",
        )

    (last_term,) = tie(feed_grads, feed_terms[2])
    grad_late, dz_cross = back_through_norm(
        3,
        late,
        (feed_terms[0], feed_terms[1], last_term),
        cotangent_visual[0].reshape(own, model),
        [f32, bf16],
    )
    cross_dz = gather_four(dz_cross)

    (dqfeed,) = tie(dz_cross, dqfeed)
    grad_qmid = cotangent_query[0].astype(f32) + norm_back(query_mid, gains_all[4:5], dqfeed)
    dz_attend = grad_qmid.astype(bf16)
    dheads_qry = right_tmul(dz_attend, jnp.pad(attend_out, ((0, wide - part), (0, 0)))).astype(bf16)
    dq, dkq, dvq, dkv, dvv = kernel_call(
        functools.partial(query_backward_kernel, *static),
        (1,),
        query_specs + [whole((slots_count, wide))],
        [full_out((slots_count, wide), bf16)] * 3 + [full_out((tokens, wide), bf16)] * 2,
        query_args + (dheads_qry,),
        name="query_backward",
        us=8,
    )
    grad_attend_out = left_tmul(heads_qry, dz_attend)

    out_rows = jnp.pad(cross_out, ((0, wide - part), (0, 0)))
    dproj_vis, dck, dcv, grad_cross_out, vis_keep, vis_send = kernel_call(
        functools.partial(cross_backward_kernel, *static),
        (shards,),
        [block_of(3 * wide), qry_piece(3), qry_piece(4)]
        + all_of(live_mask, *cross_dz, out_rows)
        + [packed_block(), block_of(wide), block_of(wide)]
        + all_of(vis_w),
        [token_out(3 * wide)]
        + [full_out((slots_count, wide), f32)] * 2
        + [full_out((part, model), f32)]
        + half_outs(),
        (proj_vis, proj_qry, proj_qry, live_mask, *cross_dz, out_rows, heads_cross, dkv, dvv, vis_w),
        scratch=[pltpu.VMEM((own, model), bf16)],
        name="cross_backward",
        us=16,
    )
    vis_terms, vis_second = scatter_pieces(vis_keep, vis_send)

    def halves_here(*grads):
        width = sum(g.shape[1] for g in grads) // wide * part
        return kernel_call(
            functools.partial(split_halves_kernel, shards, part, wide),
            (1,),
            all_of(*grads),
            [full_out((model // 2, width), bf16)] * 2,
            grads,
            place=where_page,
            name="split_halves",
            us=3,
        )

    depth, side = page // 2, page % 2

    def laid_out(blocks, pieces, width):
        direct = pages == 2 * LINE
        return kernel_call(
            functools.partial(lay_out_kernel, shards, pieces, True),
            (1,),
            all_of(*blocks),
            [full_out((rows, count * width * shards), f32) for count in pieces],
            blocks,
            place=jnp.stack([me ^ depth, side]) if direct else where_page,
            name="lay_out",
            us=2,
        )

    def beside(tensor):
        return lax.ppermute(tensor, "page", [(i, i ^ 1) for i in range(pages)])

    def to_rows(half):
        height = half.shape[0] // shards
        return jnp.concatenate(exchange([half[k * height : (k + 1) * height] for k in range(shards)]), axis=0)

    def pair_total(keep, give):
        return keep if pages == 1 else add_low(keep, beside(give))

    def parity_sum(tensor):
        groups = [list(range(s, pages, 2)) for s in (0, 1)]
        return lax.psum(tensor, "page", axis_index_groups=groups)

    def columns_scatter(own_half):
        own_chunk = line_scatter(own_half.reshape(shards, -1, own_half.shape[1]), depth)
        pairs = [
            (p * shards + w, p * shards + (w ^ (p // 2))) for p in range(pages) for w in range(shards)
        ]
        return lax.ppermute(own_chunk, ("page", "win"), pairs)

    def columns_gather(chunk):
        here = jnp.concatenate(line_gather(chunk), axis=0)
        return here, beside(here)

    def columns_total(own_half, give):
        if pages == 1:
            return to_rows(own_half), to_rows(give)
        here = to_rows(parity_sum(own_half))
        return here, beside(here)

    def rows_halves(grad):
        stack = grad.astype(bf16).reshape(2, -1, grad.shape[1])
        return pick(stack, side), pick(stack, 1 - side)

    def rows_scatter(own_half):
        return line_scatter(own_half.reshape(LINE, -1, own_half.shape[1]), depth)

    def rows_gather(quarter):
        stack = jnp.stack(line_gather(quarter))
        here = jnp.concatenate([pick(stack, depth ^ q) for q in range(LINE)], axis=0)
        return both_halves(here, beside(here))

    def both_halves(here, other):
        first = side == 0
        return jnp.concatenate([jnp.where(first, here, other), jnp.where(first, other, here)], axis=0).astype(f32)

    def rows_total(own_half, give):
        if pages == 1:
            return both_halves(own_half, give)
        here = parity_sum(own_half)
        return both_halves(here, beside(here))

    def scattered(columns, rows_):
        if pages == 2 * LINE and shards == LINE:
            return columns_scatter(columns), rows_scatter(rows_)
        return columns, rows_

    def gathered(columns, rows_, halves, rows_half):
        if pages == 2 * LINE and shards == LINE:
            return columns_gather(columns), rows_gather(rows_)
        return columns_total(columns, halves[1]), rows_total(rows_, rows_half[1])

    (dproj_now, norm_now, dck, dcv) = tie(vis_second, dproj_vis, norm_vis, dck, dcv)
    dproj_qry = jnp.concatenate([dq, dkq, dvq, dck.astype(bf16), dcv.astype(bf16)], axis=1)
    grad_vis_w = left_tmul(norm_now, dproj_now)
    grad_qry_w = left_tmul(norm_qry, dproj_qry)
    dnorm_qry, _ = total_sum(right_tmul(dproj_qry, qry_w))
    qry_columns = [grad_qry_w[:, i * wide : (i + 1) * wide] for i in range(5)]
    mixed_halves = halves_here(
        grad_vis_w[:, :wide] + qry_columns[1],
        grad_vis_w[:, wide : 2 * wide] + qry_columns[2],
        grad_vis_w[:, 2 * wide :],
        qry_columns[0],
        qry_columns[3],
        qry_columns[4],
    )
    outs_halves = rows_halves(jnp.concatenate([grad_cross_out, grad_attend_out], axis=0))
    (last_term,) = tie(mixed_halves[0], vis_terms[2])
    grad_mid, dz_window = back_through_norm(
        1, mid, (vis_terms[0], vis_terms[1], last_term), grad_late, [f32, bf16]
    )
    window_dz = gather_four(dz_window)

    act_now, dnorm_qry = tie(dz_window, act_vis, dnorm_qry)
    final = matmul(act_now, visual_down).astype(bf16)
    final_terms, _ = scatter_pieces(final[: tokens // 2], final[tokens // 2 :])
    query_back = (grad_qmid + norm_back(query_in, gains_all[2:3], dnorm_qry)).astype(bf16)
    query_final = query_mid + total_sum(matmul(act_qry, query_down))[0]

    out_rows = jnp.pad(window_out, ((0, wide - part), (0, 0)))
    mixed_pair, outs_pair = pair_total(*mixed_halves), pair_total(*outs_halves)
    first_dz = tie(final, *tie(mixed_pair, *tie(outs_pair, window_dz[0])))[0]
    if pages == GROUPS:
        first_dz = tie(feed_sum, first_dz)[0]
        feed_sum = lax.all_gather(feed_sum, "page", axis=0, tiled=True)
    window_dz = [first_dz] + list(window_dz[1:])
    dpacked, dnorm_win, bias_grad, grad_window_out = kernel_call(
        functools.partial(window_backward_kernel, *static),
        (stripes,),
        all_of(*window_dz)
        + [arriving(3 * wide), arriving(wide, short)]
        + all_of(out_rows, qkv_w)
        + window_specs,
        [
            of_tokens(leaving, 3 * wide),
            of_tokens(leaving, model),
            full_out((heads * WS * WS, WS * WS), f32),
            full_out((part, model), f32),
        ],
        (*window_dz, packed, heads_win, out_rows, qkv_w) + window_args,
        scratch=[pltpu.VMEM((own, 3 * wide), bf16)] * 2
        + [pltpu.VMEM((own, wide), bf16)] * 2
        + [pltpu.VMEM((own // 2, 3 * wide), f32)]
        + [pltpu.VMEM((places[0].shape[0], 3 * wide), f32)] * 2
        + [pltpu.VMEM((own, model), bf16)],
        place=position,
        name="window_backward",
        us=27,
    )
    win_terms, win_second = scatter_pieces(dnorm_win[: tokens // 2], dnorm_win[tokens // 2 :])
    grad_qkv_w = left_tmul(norm_win, dpacked)
    qkv_halves = halves_here(grad_qkv_w)
    mixed_share, outs_share = scattered(mixed_pair, outs_pair)
    mixed_share, outs_share = tie(dpacked, mixed_share, outs_share)
    mixed_t, outs_t = gathered(mixed_share, outs_share, mixed_halves, outs_halves)
    wout_halves = rows_halves(grad_window_out)
    qkv_share, wout_share = scattered(pair_total(*qkv_halves), pair_total(*wout_halves))
    qkv_t, wout_t = gathered(qkv_share, wout_share, qkv_halves, wout_halves)
    (visual_back,) = back_through_norm(0, vis_low, win_terms, grad_mid, [bf16])
    visual_final = late + (
        final_terms[0][:own].astype(f32) + final_terms[1][:own].astype(f32) + final_terms[2].astype(f32)
    )

    grouped = feed_grads.reshape(2, GROUPS // 2, -1, model)[:, :, : shards * up_share]
    up_grads = grouped.reshape(2, GROUPS // 2, shards, up_share, model).transpose(0, 2, 1, 3, 4)
    up_grads = up_grads.reshape(2, shards * up_share * (GROUPS // 2), model)

    def gain_grad(line, *pairs):
        return sum(jnp.sum(w.astype(f32) * g.astype(f32), axis=1) for w, g in pairs) / gains_all[line]

    gain_grads = jnp.stack(
        [
            gain_grad(0, (qkv_w, grad_qkv_w)),
            gain_grad(1, (vis_w, grad_vis_w)),
            gain_grad(2, (qry_w, grad_qry_w)),
            gain_grad(3, (vup_w, up_grads[0])),
            gain_grad(4, (qup_w, up_grads[1])),
        ]
    )
    (bias_grad,) = tie(qkv_halves[0], bias_grad)
    small = jnp.concatenate(
        [tiny_sum(gain_grads, ("win",)).reshape(-1), bias_gather(bias_grad, heads).reshape(-1)]
    )
    small = tiny_sum(small, ("page",))
    gain_total = lax.dynamic_slice_in_dim(small[: 5 * model].reshape(5, model), me * rows, rows, 1)
    bias_total = small[5 * model :].reshape(heads, SPAN * SPAN)

    out_vup, out_vdown, out_qup, out_qdown = [
        full_out(shape, f32) for shape in ((rows, shards * hidden), (hidden, model)) * 2
    ]
    (feed_sum,) = tie(dpacked, feed_sum)
    out_vup, out_qup, out_vdown, out_qdown = kernel_call(
        functools.partial(lay_out_feed_kernel, shards),
        (1,),
        all_of(feed_sum),
        [out_vup, out_qup, out_vdown, out_qdown],
        (feed_sum,),
        place=where_me,
        name="lay_out_feed",
        us=6,
    )
    (out_qkv,) = laid_out(qkv_t, [3], part)
    out_akv, out_cq, out_aq, out_ckv = laid_out(mixed_t, [2, 1, 1, 2], part)

    return (
        visual_final.reshape(1, row_count, page_width, model).astype(bf16),
        query_final.reshape(1, slots_count, model).astype(bf16),
        visual_back.reshape(1, row_count, page_width, model),
        query_back.reshape(1, slots_count, model),
        gain_total[0],
        out_qkv,
        wout_t,
        bias_total,
        gain_total[1],
        gain_total[2],
        out_aq,
        out_akv,
        outs_t[rows:],
        out_cq,
        out_ckv,
        outs_t[:rows],
        gain_total[3],
        out_vup,
        out_vdown,
        gain_total[4],
        out_qup,
        out_qdown,
    )


def solution(mesh):
    tokens_spec = P("page", "win", None, None)
    slots_spec = P("page", None, None)
    gain, weight = P("win"), P("win", None)
    parameters = (
        gain, weight, weight, weight, gain, gain, weight, weight, weight, weight, weight, weight,
        gain, weight, weight, gain, weight, weight,
    )
    return jax.shard_map(
        body,
        mesh=mesh,
        in_specs=(tokens_spec, slots_spec, P("page"), P("page", None)) + parameters + (tokens_spec, slots_spec),
        out_specs=(tokens_spec, slots_spec, tokens_spec, slots_spec) + parameters,
        check_vma=False,
    )
```

time: 817 us -> 588 us (0.72)
  Pallas kernels: 58.8 us -> 150 us
  local copies, waits for them, and re-layouts: 170 us -> 84.3 us
  other arithmetic: 116 us -> 32.5 us
  matrix products: 77.3 us -> 17 us
  waiting for transfers between devices: 231 us -> 177 us
  starting transfers between devices: 137 us -> 103 us
    ppermute x40 -> x34, waiting for transfers between devices: 131 us -> 32.3 us  [the longest x8 17.7 us: beside(): return lax.ppermute(tensor, 'page', [(i, i ^ 1) for i in range(pages)])]
    pallas_call x6 -> x21, Pallas kernels: 58.8 us -> 150 us  [kernel_call(): pl.pallas_call(function, grid_spec=pltpu.PrefetchScalarGridSpec(num_scala...]
    ppermute x58 -> x55, waiting for transfers between devices: 100 us -> 145 us  [swap(): return lax.ppermute(tensor, axis, [(i, i ^ bit) for i in range(count)])]
    concatenate x21 -> x5, local copies, waits for them, and re-layouts: 39.7 us -> 5.58 us  [the longest x1 3.42 us: body(): jnp.concatenate([gain_window, gain_visual, gain_query, gain_feed, gain_qu...]
    dot_general x10 -> x5, matrix products: 37.6 us -> 6.83 us  [matmul(): return jnp.dot(left, right, preferred_element_type=f32)]
    ppermute x40 -> x34, starting transfers between devices: 93.3 us -> 62.8 us  [the longest x24 47 us: line_swap(): return lax.ppermute(tensor, 'page', pairs)]
    dynamic_slice x19 -> x0, local copies, waits for them, and re-layouts: 23 us -> none  [the longest x18 22.4 us: pick(): return lax.dynamic_index_in_dim(stack, index, 0, False)]
    concatenate x27 -> x4, other arithmetic: 20.6 us -> 0.86 us  [the longest x2 0.75 us: rows_gather(): jnp.concatenate([pick(stack, depth ^ q) for q in range(LINE)], axis=0)]
  transfers between devices with their start and end apart: 98 -> 92, of which waited for: 32 -> 37; matrix products, arithmetic and copies ran while one was open for 36% -> 16% of each run, Pallas kernels for 4% -> 20%
where the time goes in v2:
time: 588 us; the launch traced here: 580 us
  waiting for transfers between devices  177 us (30%)
  Pallas kernels  150 us (26%)
  starting transfers between devices  103 us (18%)
  local copies, waits for them, and re-layouts  84.3 us (14%)
  other arithmetic  32.5 us (6%)
  matrix products  17 us (3%)
  between operations  16.6 us (3%)
    pallas_call x21, Pallas kernels, kernel_call(): pl.pallas_call(function, grid_spec=pltpu.PrefetchScalarGridSpec(num_scala...  150 us
    ppermute x55, waiting for transfers between devices, swap(): return lax.ppermute(tensor, axis, [(i, i ^ bit) for i in range(count)])  145 us
    ppermute x24, starting transfers between devices, line_swap(): return lax.ppermute(tensor, 'page', pairs)  47 us
    unnamed x260, local copies, waits for them, and re-layouts  44.3 us
    ppermute x55, starting transfers between devices, swap(): return lax.ppermute(tensor, axis, [(i, i ^ bit) for i in range(count)])  39.9 us
    ppermute x8, waiting for transfers between devices, beside(): return lax.ppermute(tensor, 'page', [(i, i ^ 1) for i in range(pages)])  17.7 us
    ppermute x24, waiting for transfers between devices, line_swap(): return lax.ppermute(tensor, 'page', pairs)  14.6 us
  transfers between devices with their start and end apart: 92, of which 37 were waited for; matrix products, arithmetic and copies ran while one was open for 16% of the time, Pallas kernels for 20%

profile of v2, /device:TPU:0, one launch (start us, length us, event | category | flops | bytes accessed | tf_op | source)
XLA Modules:
  0.0 579.9 jit_solution(2808102742563176748)
XLA Ops:
  26.6 22.9 %collective-permute-done.17 = bf16[80,768]{1,0:T(8,128)(2,1)} collective-permute-done((bf16[80,768]{1,0:T(8,128)(2,1)S(1)}, bf16[80,768]{1,0:T(8,128)(2,1)}, u32[]{:S(2)}, u32[]{:S(2)}) %collective-permute-start.17) | collective-permute-done | bytes 122912 | tf_op jit(solution)/shard_map/ppermute | solution.py:25
  79.3 19.8 %window_forward.1 = (bf16[1728,768]{1,0:T(8,128)(2,1)}, bf16[768,768]{1,0:T(8,128)(2,1)S(1)}, f32[16,768]{1,0:T(8,128)S(1)}, bf16[1728,768]{1,0:T(8,128)(2,1)}, ...) custom-call(s32[5]{0:T(128)S(1)} %pad_add_fusion.2.place, bf16[832,768]{1,0:T(8,128)(2,1)S(1)} %copy-done.29, ...), custom_call_target="tpu_custom_call" | custom-call | flops 17000000 | bytes 1000 | tf_op jit(solution)/shard_map/window_forward/pallas_call | solution.py:729
  104.3 14.2 %collective-permute-done.3.second = bf16[1344,256]{1,0:T(8,128)(2,1)} collective-permute-done((bf16[1344,256]{1,0:T(8,128)(2,1)S(1)}, bf16[1344,256]{1,0:T(8,128)(2,1)}, u32[]{:S(2)}, u32[]{:S(2)}) %collective-permute-start.3) | collective-permute-done | bytes 688160 | tf_op jit(solution)/shard_map/ppermute | solution.py:25
  120.6 4.2 collective-permute-done.6.out_second
  126.6 7.8 %collective-permute-done.10.refs_2_ = bf16[192,1152]{1,0:T(8,128)(2,1)} collective-permute-done((bf16[192,1152]{1,0:T(8,128)(2,1)}, bf16[192,1152]{1,0:T(8,128)(2,1)}, u32[]{:S(2)}, u32[]{:S(2)}) %collective-permute-start.10) | collective-permute-done | bytes 442400 | tf_op jit(solution)/shard_map/ppermute | solution.py:25
  134.4 8.8 %collective-permute-done.11.refs_3_ = bf16[192,1152]{1,0:T(8,128)(2,1)} collective-permute-done((bf16[192,1152]{1,0:T(8,128)(2,1)}, bf16[192,1152]{1,0:T(8,128)(2,1)}, u32[]{:S(2)}, u32[]{:S(2)}) %collective-permute-start.11) | collective-permute-done | bytes 442400 | tf_op jit(solution)/shard_map/ppermute | solution.py:25
  148.8 14.3 %middle.1 = (f32[1728,768]{1,0:T(8,128)}, bf16[1728,768]{1,0:T(8,128)(2,1)}, bf16[1728,768]{1,0:T(8,128)(2,1)}, bf16[1344,256]{1,0:T(8,128)(2,1)S(1)}) custom-call(bf16[1728,768]{1,0:T(8,128)(2,1)} %get-tuple-element.151.visual.tensor, bf16[1344,256]{1,0:T(8,128)(2,1)S(1)} %get-tuple-element.152.own.mixed, bf16[1344,256]{1,0:T(8,128)(2,1)} %collective-permute-done.3.second, ...), custom_call_target="tpu_custom_call" | custom-call | flops 13000000 | bytes 1000 | tf_op jit(solution)/shard_map/middle/pallas_call | solution.py:729
  173.0 14.9 %collective-permute-done.23 = bf16[192,768]{1,0:T(8,128)(2,1)} collective-permute-done((bf16[192,768]{1,0:T(8,128)(2,1)S(1)}, bf16[192,768]{1,0:T(8,128)(2,1)}, u32[]{:S(2)}, u32[]{:S(2)}) %collective-permute-start.23) | collective-permute-done | bytes 294944 | tf_op jit(solution)/shard_map/ppermute | solution.py:25
  197.4 19.3 %feed.1 = (f32[432,768]{1,0:T(8,128)}, bf16[1728,768]{1,0:T(8,128)(2,1)}, bf16[1728,768]{1,0:T(8,128)(2,1)}, bf16[1728,768]{1,0:T(8,128)(2,1)}, bf16[864,768]{1,0:T(8,128)(2,1)}, /*index=5*/bf16[864,768]{1,0:T(8,128)(2,1)}) custom-call(s32[1]{0:T(128)} %bitcast.place, f32[1728,768]{1,0:T(8,128)} %get-tuple-element.162.mid.tensor, ...), custom_call_target="tpu_custom_call" | custom-call | flops 18000000 | bytes 1000 | tf_op jit(solution)/shard_map/feed/pallas_call | solution.py:729
  230.7 11.4 %feed_grads.1 = bf16[3072,768]{1,0:T(8,128)(2,1)} custom-call(bf16[1728,768]{1,0:T(8,128)(2,1)S(1)} %copy-done.19, bf16[1728,768]{1,0:T(8,128)(2,1)} %get-tuple-element.201.dhidden, bf16[1728,768]{1,0:T(8,128)(2,1)} %get-tuple-element.230.act, bf16[1728,768]{1,0:T(8,128)(2,1)} %copy-done.65, bf16[256,768]{1,0:T(8,128)(2,1)S(1)} %multiply_convert_fusion.1.norm_qry, ...), custom_call_target="tpu_custom_call" | custom-call | flops 10000000 | bytes 1000 | tf_op jit(solution)/shard_map/feed_grads/pallas_call | solution.py:729
  255.2 9.0 %collective-permute-done.29.third = bf16[432,768]{1,0:T(8,128)(2,1)S(1)} collective-permute-done((bf16[432,768]{1,0:T(8,128)(2,1)}, bf16[432,768]{1,0:T(8,128)(2,1)S(1)}, u32[]{:S(2)}, u32[]{:S(2)}) %collective-permute-start.29) | collective-permute-done | bytes 663584 | tf_op jit(solution)/shard_map/ppermute | solution.py:25
  268.3 4.3 collective-permute-done.33
  272.8 8.2 %collective-permute-done.41 = bf16[256,768]{1,0:T(8,128)(2,1)S(1)} collective-permute-done((bf16[256,768]{1,0:T(8,128)(2,1)S(1)}, bf16[256,768]{1,0:T(8,128)(2,1)S(1)}, u32[]{:S(2)}, u32[]{:S(2)}) %collective-permute-start.41) | collective-permute-done | bytes 393248 | tf_op jit(solution)/shard_map/ppermute | solution.py:25
  282.2 12.5 %collective-permute-done.30.second = bf16[432,768]{1,0:T(8,128)(2,1)S(1)} collective-permute-done((bf16[432,768]{1,0:T(8,128)(2,1)S(1)}, bf16[432,768]{1,0:T(8,128)(2,1)S(1)}, u32[]{:S(2)}, u32[]{:S(2)}) %collective-permute-start.30) | collective-permute-done | bytes 663584 | tf_op jit(solution)/shard_map/ppermute | solution.py:25
  296.8 7.0 %query_backward.1 = (bf16[256,256]{1,0:T(8,128)(2,1)S(1)}, bf16[256,256]{1,0:T(8,128)(2,1)S(1)}, bf16[256,256]{1,0:T(8,128)(2,1)S(1)}, bf16[1728,256]{1,0:T(8,128)(2,1)S(1)}, bf16[1728,256]{1,0:T(8,128)(2,1)S(1)}) custom-call(bf16[256,1280]{1,0:T(8,128)(2,1)S(1)} %convolution_convert_fusion.1.keys.values.query.keys_qry.values_qry, ...), custom_call_target="tpu_custom_call" | custom-call | flops 8000000 | bytes 1000 | tf_op jit(solution)/shard_map/query_backward/pallas_call | solution.py:729
  305.6 17.0 %cross_backward.1 = (bf16[1728,768]{1,0:T(8,128)(2,1)}, f32[256,256]{1,0:T(8,128)S(1)}, f32[256,256]{1,0:T(8,128)S(1)}, f32[192,768]{1,0:T(8,128)S(1)}, bf16[864...) custom-call(bf16[1728,768]{1,0:T(8,128)(2,1)} %get-tuple-element.164.keys_vis.values_vis.proj, ...), custom_call_target="tpu_custom_call" | custom-call | flops 16000000 | bytes 1000 | tf_op jit(solution)/shard_map/cross_backward/pallas_call | solution.py:729
  325.9 6.4 %collective-permute-done.46 = bf16[192,768]{1,0:T(8,128)(2,1)S(1)} collective-permute-done((bf16[192,768]{1,0:T(8,128)(2,1)S(1)}, bf16[192,768]{1,0:T(8,128)(2,1)S(1)}, u32[]{:S(2)}, u32[]{:S(2)}) %collective-permute-start.46) | collective-permute-done | bytes 294944 | tf_op jit(solution)/shard_map/ppermute | solution.py:1175
  332.5 3.9 collective-permute-start.80
  337.1 4.2 collective-permute-done.80
  341.3 3.7 collective-permute-done.79
  358.9 4.2 collective-permute-done.35.third
  363.0 3.7 norm_back.4
  409.9 6.4 %collective-permute-done.39 = bf16[432,768]{1,0:T(8,128)(2,1)S(1)} collective-permute-done((bf16[432,768]{1,0:T(8,128)(2,1)S(1)}, bf16[432,768]{1,0:T(8,128)(2,1)S(1)}, u32[]{:S(2)}, u32[]{:S(2)}) %collective-permute-start.39) | collective-permute-done | bytes 663584 | tf_op jit(solution)/shard_map/ppermute | solution.py:25
  420.8 29.3 %window_backward.1 = (bf16[1728,768]{1,0:T(8,128)(2,1)}, bf16[1728,768]{1,0:T(8,128)(2,1)}, f32[432,144]{1,0:T(8,128)S(1)}, f32[192,768]{1,0:T(8,128)S(1)}) custom-call(s32[5]{0:T(128)S(1)} %pad_add_fusion.2.place, bf16[432,768]{1,0:T(8,128)(2,1)} %get-tuple-element.236.near, bf16[432,768]{1,0:T(8,128)(2,1)} %collective-permute-done.47.second, ...), custom_call_target="tpu_custom_call" | custom-call | flops 27000000 | bytes 1000 | tf_op jit(solution)/shard_map/window_backward/pallas_call | solution.py:729
  454.6 4.3 multiply_reduce_fusion.2
  485.9 4.0 collective-permute-start.56
  509.2 5.1 collective-permute-start.70
  520.1 4.5 collective-permute-done.88
  534.1 6.8 %collective-permute-start.63 = (bf16[96,576]{1,0:T(8,128)(2,1)S(1)}, bf16[96,576]{1,0:T(8,128)(2,1)S(1)}, u32[]{:S(2)}, u32[]{:S(2)}) collective-permute-start(bf16[96,576]{1,0:T(8,128)(2,1)S(1)} %collective-permute-done.61), channel_id=1, source_target_pairs={{0,16},{4,20},{8,24},{12,28},{16,0},{20,4},{24,8},{28,12},{1,17},{... | collective-permute-start | bytes 331784 | tf_op jit(solution)/shard_map/ppermute | solution.py:102
  541.0 5.7 collective-permute-start.64
  556.4 4.6 collective-permute-done.65.refs_1_
  569.2 4.0 lay_out_feed.1
  (612 shorter events, 266.8 us)
Async XLA Ops:
  7.2 183.1 %all-gather.6.cloned.1.call-start = ((), (), s32[]{:S(2)}) async-start(), calls=%async_computation.3 | async-start | bytes 4423680 | tf_op jit(solution)/shard_map/all_gather | solution.py:902
  15.4 49.9 %collective-permute-start = (bf16[832,768]{1,0:T(8,128)(2,1)S(1)}, bf16[832,768]{1,0:T(8,128)(2,1)}, u32[]{:S(2)}, u32[]{:S(2)}) collective-permute-start(bf16[832,768]{1,0:T(8,128)(2,1)S(1)} %get-tuple-element.141.near), channel_id=1, source_target_pairs={{0,2},{1,3},{2,0},{3,1},{4,6},{5,7},{6,4},{7,5},{8,10},{9,11},{10,... | collective-permute-start | bytes 3833864 | tf_op jit(solution)/shard_map/ppermute | solution.py:25
  21.7 27.7 %collective-permute-start.17 = (bf16[80,768]{1,0:T(8,128)(2,1)S(1)}, bf16[80,768]{1,0:T(8,128)(2,1)}, u32[]{:S(2)}, u32[]{:S(2)}) collective-permute-start(bf16[80,768]{1,0:T(8,128)(2,1)S(1)} %get-tuple-element.168), channel_id=1, source_target_pairs={{0,3},{1,2},{2,1},{3,0},{4,7},{5,6},{6,5},{7,4},{8,11},{9,10},{10,... | collective-permute-start | bytes 368648 | tf_op jit(solution)/shard_map/ppermute | solution.py:25
  21.8 30.0 %collective-permute-start.16 = (bf16[80,768]{1,0:T(8,128)(2,1)S(1)}, bf16[80,768]{1,0:T(8,128)(2,1)}, u32[]{:S(2)}, u32[]{:S(2)}) collective-permute-start(bf16[80,768]{1,0:T(8,128)(2,1)S(1)} %get-tuple-element.167), channel_id=1, source_target_pairs={{0,2},{1,3},{2,0},{3,1},{4,6},{5,7},{6,4},{7,5},{8,10},{9,11},{10,... | collective-permute-start | bytes 368648 | tf_op jit(solution)/shard_map/ppermute | solution.py:25
  23.0 28.8 %collective-permute-start.15 = (bf16[80,768]{1,0:T(8,128)(2,1)S(1)}, bf16[80,768]{1,0:T(8,128)(2,1)}, u32[]{:S(2)}, u32[]{:S(2)}) collective-permute-start(bf16[80,768]{1,0:T(8,128)(2,1)S(1)} %get-tuple-element.166), channel_id=1, source_target_pairs={{0,1},{1,0},{2,3},{3,2},{4,5},{5,4},{6,7},{7,6},{8,9},{9,8},{10,11... | collective-permute-start | bytes 368648 | tf_op jit(solution)/shard_map/ppermute | solution.py:25
  53.6 328.0 %reduce-scatter.2.cloned.1.call-start = ((), (), s32[]{:S(2)}) async-start(), calls=%async_computation.1 | async-start | bytes 5308416 | tf_op jit(solution)/shard_map/reduce_scatter | solution.py:1086
  101.9 24.6 %collective-permute-start.9 = (bf16[192,1152]{1,0:T(8,128)(2,1)}, bf16[192,1152]{1,0:T(8,128)(2,1)}, u32[]{:S(2)}, u32[]{:S(2)}) collective-permute-start(bf16[192,1152]{1,0:T(8,128)(2,1)} %get-tuple-element.147), channel_id=1, source_target_pairs={{0,1},{1,0},{2,3},{3,2},{4,5},{5,4},{6,7},{7,6},{8,9},{9,8},{10,11... | collective-permute-start | bytes 1327112 | tf_op jit(solution)/shard_map/ppermute | solution.py:25
  102.2 22.6 %collective-permute-start.6 = (bf16[192,768]{1,0:T(8,128)(2,1)S(1)}, bf16[192,768]{1,0:T(8,128)(2,1)S(1)}, u32[]{:S(2)}, u32[]{:S(2)}) collective-permute-start(bf16[192,768]{1,0:T(8,128)(2,1)S(1)} %copy-done.34), channel_id=1, source_target_pairs={{0,2},{1,3},{2,0},{3,1},{4,6},{5,7},{6,4},{7,5},{8,10},{9,11},{10,... | collective-permute-start | bytes 884744 | tf_op jit(solution)/shard_map/ppermute | solution.py:25
  102.5 31.8 %collective-permute-start.10 = (bf16[192,1152]{1,0:T(8,128)(2,1)}, bf16[192,1152]{1,0:T(8,128)(2,1)}, u32[]{:S(2)}, u32[]{:S(2)}) collective-permute-start(bf16[192,1152]{1,0:T(8,128)(2,1)} %get-tuple-element.156), channel_id=1, source_target_pairs={{0,2},{1,3},{2,0},{3,1},{4,6},{5,7},{6,4},{7,5},{8,10},{9,11},{10,... | collective-permute-start | bytes 1327112 | tf_op jit(solution)/shard_map/ppermute | solution.py:25
  104.3 38.8 %collective-permute-start.11 = (bf16[192,1152]{1,0:T(8,128)(2,1)}, bf16[192,1152]{1,0:T(8,128)(2,1)}, u32[]{:S(2)}, u32[]{:S(2)}) collective-permute-start(bf16[192,1152]{1,0:T(8,128)(2,1)} %get-tuple-element.157), channel_id=1, source_target_pairs={{0,3},{1,2},{2,1},{3,0},{4,7},{5,6},{6,5},{7,4},{8,11},{9,10},{10,... | collective-permute-start | bytes 1327112 | tf_op jit(solution)/shard_map/ppermute | solution.py:25
  118.6 30.0 %collective-permute-start.4 = (bf16[1344,256]{1,0:T(8,128)(2,1)S(1)}, bf16[1344,256]{1,0:T(8,128)(2,1)}, u32[]{:S(2)}, u32[]{:S(2)}) collective-permute-start(bf16[1344,256]{1,0:T(8,128)(2,1)S(1)} %get-tuple-element.152.own.mixed), channel_id=1, source_target_pairs={{0,1},{1,0},{2,3},{3,2},{4,5},{5,4},{6,7},{7,6},{8,9},{9,8},{10,11... | collective-permute-start | bytes 2064392 | tf_op jit(solution)/shard_map/ppermute | solution.py:25
  124.8 40.1 %collective-permute-start.18 = (bf16[432,768]{1,0:T(8,128)(2,1)}, bf16[432,768]{1,0:T(8,128)(2,1)S(1)}, u32[]{:S(2)}, u32[]{:S(2)}) collective-permute-start(bf16[432,768]{1,0:T(8,128)(2,1)} %reshape_squeeze.10), channel_id=1, source_target_pairs={{0,2},{1,3},{2,0},{3,1},{4,6},{5,7},{6,4},{7,5},{8,10},{9,11},{10,... | collective-permute-start | bytes 1990664 | tf_op jit(solution)/shard_map/ppermute | solution.py:25
  163.1 26.7 %collective-permute-start.12 = (bf16[1344,256]{1,0:T(8,128)(2,1)S(1)}, bf16[1344,256]{1,0:T(8,128)(2,1)S(1)}, u32[]{:S(2)}, u32[]{:S(2)}) collective-permute-start(bf16[1344,256]{1,0:T(8,128)(2,1)S(1)} %get-tuple-element.163.own.mixed), channel_id=1, source_target_pairs={{0,2},{1,3},{2,0},{3,1},{4,6},{5,7},{6,4},{7,5},{8,10},{9,11},{10,... | collective-permute-start | bytes 2064392 | tf_op jit(solution)/shard_map/ppermute | solution.py:25
  164.9 23.0 %collective-permute-start.19 = (bf16[432,768]{1,0:T(8,128)(2,1)S(1)}, bf16[432,768]{1,0:T(8,128)(2,1)S(1)}, u32[]{:S(2)}, u32[]{:S(2)}) collective-permute-start(bf16[432,768]{1,0:T(8,128)(2,1)S(1)} %copy-done.85), channel_id=1, source_target_pairs={{0,1},{1,0},{2,3},{3,2},{4,5},{5,4},{6,7},{7,6},{8,9},{9,8},{10,11... | collective-permute-start | bytes 1990664 | tf_op jit(solution)/shard_map/ppermute | solution.py:25
  164.9 25.4 %collective-permute-start.20 = (bf16[432,768]{1,0:T(8,128)(2,1)S(1)}, bf16[432,768]{1,0:T(8,128)(2,1)}, u32[]{:S(2)}, u32[]{:S(2)}) collective-permute-start(bf16[432,768]{1,0:T(8,128)(2,1)S(1)} %collective-permute-done.18), channel_id=1, source_target_pairs={{0,1},{1,0},{2,3},{3,2},{4,5},{5,4},{6,7},{7,6},{8,9},{9,8},{10,11... | collective-permute-start | bytes 1990664 | tf_op jit(solution)/shard_map/ppermute | solution.py:25
  165.4 22.5 %collective-permute-start.23 = (bf16[192,768]{1,0:T(8,128)(2,1)S(1)}, bf16[192,768]{1,0:T(8,128)(2,1)}, u32[]{:S(2)}, u32[]{:S(2)}) collective-permute-start(bf16[192,768]{1,0:T(8,128)(2,1)S(1)} %copy-done.105), channel_id=1, source_target_pairs={{0,2},{1,3},{2,0},{3,1},{4,6},{5,7},{6,4},{7,5},{8,10},{9,11},{10,... | collective-permute-start | bytes 884744 | tf_op jit(solution)/shard_map/ppermute | solution.py:25
  242.2 324.7 %all-gather.4.cloned.1.call-start = ((), (), s32[]{:S(2)}) async-start(), calls=%async_computation.2 | async-start | bytes 5308416 | tf_op jit(solution)/shard_map/all_gather | solution.py:1269
  248.1 24.6 %collective-permute-start.33 = (bf16[256,768]{1,0:T(8,128)(2,1)}, bf16[256,768]{1,0:T(8,128)(2,1)S(1)}, u32[]{:S(2)}, u32[]{:S(2)}) collective-permute-start(bf16[256,768]{1,0:T(8,128)(2,1)} %fusion.32), channel_id=1, source_target_pairs={{0,2},{1,3},{2,0},{3,1},{4,6},{5,7},{6,4},{7,5},{8,10},{9,11},{10,... | collective-permute-start | bytes 1179656 | tf_op jit(solution)/shard_map/ppermute | solution.py:25
  249.7 31.3 %collective-permute-start.41 = (bf16[256,768]{1,0:T(8,128)(2,1)S(1)}, bf16[256,768]{1,0:T(8,128)(2,1)S(1)}, u32[]{:S(2)}, u32[]{:S(2)}) collective-permute-start(bf16[256,768]{1,0:T(8,128)(2,1)S(1)} %fusion.34), channel_id=1, source_target_pairs={{0,2},{1,3},{2,0},{3,1},{4,6},{5,7},{6,4},{7,5},{8,10},{9,11},{10,... | collective-permute-start | bytes 1179656 | tf_op jit(solution)/shard_map/ppermute | solution.py:25
  266.5 28.2 %collective-permute-start.30 = (bf16[432,768]{1,0:T(8,128)(2,1)S(1)}, bf16[432,768]{1,0:T(8,128)(2,1)S(1)}, u32[]{:S(2)}, u32[]{:S(2)}) collective-permute-start(bf16[432,768]{1,0:T(8,128)(2,1)S(1)} %get-tuple-element.209.near), channel_id=1, source_target_pairs={{0,2},{1,3},{2,0},{3,1},{4,6},{5,7},{6,4},{7,5},{8,10},{9,11},{10,... | collective-permute-start | bytes 1990664 | tf_op jit(solution)/shard_map/ppermute | solution.py:25
  268.3 36.7 %collective-permute-start.31 = (bf16[432,768]{1,0:T(8,128)(2,1)S(1)}, bf16[432,768]{1,0:T(8,128)(2,1)S(1)}, u32[]{:S(2)}, u32[]{:S(2)}) collective-permute-start(bf16[432,768]{1,0:T(8,128)(2,1)S(1)} %get-tuple-element.209.near), channel_id=1, source_target_pairs={{0,1},{1,0},{2,3},{3,2},{4,5},{5,4},{6,7},{7,6},{8,9},{9,8},{10,11... | collective-permute-start | bytes 1990664 | tf_op jit(solution)/shard_map/ppermute | solution.py:25
  366.8 36.2 %collective-permute-start.47 = (bf16[432,768]{1,0:T(8,128)(2,1)}, bf16[432,768]{1,0:T(8,128)(2,1)}, u32[]{:S(2)}, u32[]{:S(2)}) collective-permute-start(bf16[432,768]{1,0:T(8,128)(2,1)} %get-tuple-element.236.near), channel_id=1, source_target_pairs={{0,2},{1,3},{2,0},{3,1},{4,6},{5,7},{6,4},{7,5},{8,10},{9,11},{10,... | collective-permute-start | bytes 1990664 | tf_op jit(solution)/shard_map/ppermute | solution.py:25
  380.5 22.5 %collective-permute-start.76 = (bf16[96,1152]{1,0:T(8,128)(2,1)}, bf16[96,1152]{1,0:T(8,128)(2,1)}, u32[]{:S(2)}, u32[]{:S(2)}) collective-permute-start(bf16[96,1152]{1,0:T(8,128)(2,1)} %get-tuple-element.287), channel_id=1, source_target_pairs={{0,24},{4,28},{8,16},{12,20},{16,8},{20,12},{24,0},{28,4},{1,25},{... | collective-permute-start | bytes 663560 | tf_op jit(solution)/shard_map/ppermute | solution.py:102
  406.3 43.8 %collective-permute-start.77 = (bf16[96,1152]{1,0:T(8,128)(2,1)}, bf16[96,1152]{1,0:T(8,128)(2,1)}, u32[]{:S(2)}, u32[]{:S(2)}) collective-permute-start(bf16[96,1152]{1,0:T(8,128)(2,1)} %fusion.38), channel_id=1, source_target_pairs={{0,0},{1,1},{2,2},{3,3},{4,4},{5,5},{6,6},{7,7},{8,9},{9,8},{10,11... | collective-permute-start | bytes 663560 | tf_op jit(solution)/shard_map/ppermute | solution.py:1193
  450.1 29.7 %collective-permute-start.87 = (bf16[48,768]{1,0:T(8,128)(2,1)S(1)}, bf16[48,768]{1,0:T(8,128)(2,1)}, u32[]{:S(2)}, u32[]{:S(2)}) collective-permute-start(bf16[48,768]{1,0:T(8,128)(2,1)S(1)} %fusion.62), channel_id=1, source_target_pairs={{0,24},{4,28},{8,16},{12,20},{16,8},{20,12},{24,0},{28,4},{1,25},{... | collective-permute-start | bytes 221192 | tf_op jit(solution)/shard_map/ppermute | solution.py:102
  452.0 29.9 %collective-permute-start.86 = (bf16[48,768]{1,0:T(8,128)(2,1)S(1)}, bf16[48,768]{1,0:T(8,128)(2,1)}, u32[]{:S(2)}, u32[]{:S(2)}) collective-permute-start(bf16[48,768]{1,0:T(8,128)(2,1)S(1)} %fusion.62), channel_id=1, source_target_pairs={{0,16},{4,20},{8,24},{12,28},{16,0},{20,4},{24,8},{28,12},{1,17},{... | collective-permute-start | bytes 221192 | tf_op jit(solution)/shard_map/ppermute | solution.py:102
  452.0 29.9 %collective-permute-start.85 = (bf16[48,768]{1,0:T(8,128)(2,1)S(1)}, bf16[48,768]{1,0:T(8,128)(2,1)}, u32[]{:S(2)}, u32[]{:S(2)}) collective-permute-start(bf16[48,768]{1,0:T(8,128)(2,1)S(1)} %fusion.62), channel_id=1, source_target_pairs={{0,8},{4,12},{8,0},{12,4},{16,24},{20,28},{24,16},{28,20},{1,9},{5... | collective-permute-start | bytes 221192 | tf_op jit(solution)/shard_map/ppermute | solution.py:102
  463.6 41.5 %collective-permute-start.81 = (bf16[96,1152]{1,0:T(8,128)(2,1)}, bf16[96,1152]{1,0:T(8,128)(2,1)}, u32[]{:S(2)}, u32[]{:S(2)}) collective-permute-start(bf16[96,1152]{1,0:T(8,128)(2,1)} %collective-permute-done.77), channel_id=1, source_target_pairs={{0,8},{4,12},{8,0},{12,4},{16,24},{20,28},{24,16},{28,20},{1,9},{5... | collective-permute-start | bytes 663560 | tf_op jit(solution)/shard_map/ppermute | solution.py:102
  477.5 30.7 %collective-permute-start.82 = (bf16[96,1152]{1,0:T(8,128)(2,1)}, bf16[96,1152]{1,0:T(8,128)(2,1)}, u32[]{:S(2)}, u32[]{:S(2)}) collective-permute-start(bf16[96,1152]{1,0:T(8,128)(2,1)} %collective-permute-done.77), channel_id=1, source_target_pairs={{0,16},{4,20},{8,24},{12,28},{16,0},{20,4},{24,8},{28,12},{1,17},{... | collective-permute-start | bytes 663560 | tf_op jit(solution)/shard_map/ppermute | solution.py:102
  502.9 45.3 %collective-permute-start.50 = (bf16[864,768]{1,0:T(8,128)(2,1)}, bf16[864,768]{1,0:T(8,128)(2,1)S(1)}, u32[]{:S(2)}, u32[]{:S(2)}) collective-permute-start(bf16[864,768]{1,0:T(8,128)(2,1)} %get-tuple-element.277), channel_id=1, source_target_pairs={{0,1},{1,0},{2,3},{3,2},{4,5},{5,4},{6,7},{7,6},{8,9},{9,8},{10,11... | collective-permute-start | bytes 3981320 | tf_op jit(solution)/shard_map/ppermute | solution.py:25
  516.0 37.6 %collective-permute-start.84 = (bf16[384,1152]{1,0:T(8,128)(2,1)S(1)}, bf16[384,1152]{1,0:T(8,128)(2,1)S(1)}, u32[]{:S(2)}, u32[]{:S(2)}) collective-permute-start(bf16[384,1152]{1,0:T(8,128)(2,1)S(1)} %constant_dynamic-update-slice_fusion.40.refs_0_), channel_id=1, source_target_pairs={{0,4},{4,0},{8,12},{12,8},{16,20},{20,16},{24,28},{28,24},{1,5},{5... | collective-permute-start | bytes 2654216 | tf_op jit(solution)/shard_map/ppermute | solution.py:1175
  525.2 27.5 %collective-permute-start.73 = (bf16[96,768]{1,0:T(8,128)(2,1)S(1)}, bf16[96,768]{1,0:T(8,128)(2,1)S(1)}, u32[]{:S(2)}, u32[]{:S(2)}) collective-permute-start(bf16[96,768]{1,0:T(8,128)(2,1)S(1)} %pad_maximum_fusion.6), channel_id=1, source_target_pairs={{0,4},{4,0},{8,12},{12,8},{16,20},{20,16},{24,28},{28,24},{1,5},{5... | collective-permute-start | bytes 442376 | tf_op jit(solution)/shard_map/ppermute | solution.py:1175
  (170 other events, 1851.2 us)
Sparse Core Ops, SparseCore 0:
  53.8 71.5 all-gather.5
  242.3 101.5 reduce-scatter.1
  398.1 86.5 all-gather.3

commit v3 on v2

--- a/solution.py
+++ b/solution.py
@@ -102,8 +102,11 @@
     return lax.ppermute(tensor, "page", pairs)
 
 
-def line_scatter(parts, depth):
-    terms = [pick(parts, depth)] + [line_swap(pick(parts, depth ^ k), k) for k in range(1, LINE)]
+def line_send(parts, depth):
+    return [pick(parts, depth)] + [line_swap(pick(parts, depth ^ k), k) for k in range(1, LINE)]
+
+
+def line_add(terms):
     return rounded(total([t.astype(f32) for t in terms])).astype(bf16)
 
 
@@ -125,6 +128,10 @@
     for bit in bits_of(count):
         parts = parts + [swap(p, axis, bit) for p in parts]
     return parts
+
+
+def fence(*values):
+    return lax.optimization_barrier(values)
 
 
 def scatter_pieces(keep, send):
@@ -240,8 +247,8 @@
 
 
 def window_forward_kernel(
-    heads, head_size, scale, place, near, second, third, fourth, chunk, top_in, low_in, top_out, low_out,
-    slots, rows, visual, weight, gains, norm, packed, mixed, before, after, held, chosen,
+    heads, head_size, scale, place, near, second, third, fourth, chunk, gain_own, gain_second, gain_third,
+    gain_fourth, top_in, low_in, top_out, low_out, slots, rows, visual, weight, gains, norm, packed, mixed, before, after, held, chosen,
 ):
     step, last = pl.program_id(0), pl.num_programs(0) - 1
     cells = WS * WS
@@ -250,7 +257,7 @@
     blocks = (near, second, third, fourth)
     shards = len(blocks)
     me = place[shards]
-    own, piece = chosen.shape[0], chunk.shape[0]
+    own, piece, part = chosen.shape[0], chunk.shape[0], heads * head_size
 
     @pl.when(step == 0)
     def _():
@@ -260,14 +267,19 @@
         starts = (None, own, own, own + piece)
         for p, k in enumerate(order):
             source = chunk[...] if p == 0 else blocks[p][starts[p] : starts[p] + piece, :]
-            weight[pl.ds(pl.multiple_of((me ^ k) * piece, piece), piece), :] = source
+            rows_here = weight.shape[0] // shards
+            source = unfold(source, rows_here, 3 * part)
+            gap = jnp.zeros((rows_here, width - part), bf16)
+            columns = [x for s in range(3) for x in (source[:, s * part : (s + 1) * part], gap)]
+            at = pl.ds(pl.multiple_of((me ^ k) * rows_here, rows_here), rows_here)
+            weight[at, :] = jnp.concatenate(columns, axis=1)
         for device in range(shards):
 
             @pl.when(me == device)
             def _(device=device):
                 lines = [None] * shards
-                for p, k in enumerate(order):
-                    lines[device ^ k] = blocks[p][blocks[p].shape[0] - 16 :, :piece].astype(f32)
+                for p, ref in enumerate((gain_own, gain_second, gain_third, gain_fourth)):
+                    lines[device ^ order[p]] = ref[...].astype(f32)
                 gains[...] = jnp.concatenate(lines, axis=1)
 
     @pl.when(step < last)
@@ -399,8 +411,8 @@
 
 
 def feed_kernel(
-    part, place, mid, own, second, third, fourth, weight_out, gains, up, down, cotangent,
-    late, norm, act, dhidden, keep, send,
+    part, place, mid, own, second, third, fourth, weight_out, gains, up, down, top_own, top_second, top_third,
+    top_fourth, late, norm, act, dhidden, top, keep, send, cotangent,
 ):
     step, halfway = pl.program_id(0), pl.num_programs(0) // 2
     pieces = (own, second, third, fourth)
@@ -418,6 +430,13 @@
     norm[...] = low
     value, slope = gelu_both(matmul(low, up[...]))
     act[...] = value.astype(bf16)
+    for k, ref in enumerate((top_own, top_second, top_third, top_fourth)):
+
+        @pl.when(step == k)
+        def _(ref=ref):
+            cotangent[...] = ref[ref.shape[0] - cotangent.shape[0] :, :]
+
+    top[...] = cotangent[...]
     back = (right_tmul(cotangent[...], down[...]) * slope).astype(bf16)
     dhidden[...] = back
     dnorm = right_tmul(back, up[...]).astype(bf16)
@@ -429,6 +448,35 @@
     @pl.when(step >= halfway)
     def _():
         send[...] = dnorm
+
+
+def query_feed_kernel(
+    query, own, second, third, fourth, top_own, top_second, top_third, top_fourth, gains, up, down, top,
+    mid, norm, act, dhidden, dnorm,
+):
+    pieces, weights = (own, second, third, fourth), (top_own, top_second, top_third, top_fourth)
+    result = query[...].astype(f32) + total([matmul(p[...], w[...]) for p, w in zip(pieces, weights)])
+    mid[...] = result
+    low = norm_low(result, gains[4:5, :])
+    norm[...] = low
+    value, slope = gelu_both(matmul(low, up[...]))
+    act[...] = value.astype(bf16)
+    back = (right_tmul(top[...], down[...]) * slope).astype(bf16)
+    dhidden[...] = back
+    dnorm[...] = right_tmul(back, up[...]).astype(bf16)
+
+
+def halves_kernel(left, right, keep, send):
+    step, halfway = pl.program_id(0), pl.num_programs(0) // 2
+    result = matmul(left[...], right[...]).astype(bf16)
+
+    @pl.when(step < halfway)
+    def _():
+        keep[...] = result
+
+    @pl.when(step >= halfway)
+    def _():
+        send[...] = result
 
 
 def query_scores(query, keys_vis, keys_qry, causal, mask):
@@ -465,17 +513,22 @@
 
 
 def query_backward_kernel(
-    heads, head_size, scale, query, keys_qry, values_qry, keys_vis, values_vis, causal, upstream,
-    dquery, dkeys_qry, dvalues_qry, dkeys_vis, dvalues_vis,
+    heads, head_size, scale, query, keys_qry, values_qry, keys_vis, values_vis, causal, mid, gains, top, dnorm,
+    weight_out, dquery, dkeys_qry, dvalues_qry, dkeys_vis, dvalues_vis, dmid, dz,
 ):
     width = query.shape[1]
+    result = top[...].astype(f32) + norm_back(mid[...], gains[4:5, :], dnorm[...])
+    dmid[...] = result
+    low = result.astype(bf16)
+    dz[...] = low
+    upstream = right_tmul(low, weight_out[...]).astype(bf16)
     sums = [[], [], [], [], []]
     for h in range(heads):
         masked, score_vis, score_qry = query_scores(
             query[...], keys_vis[...], keys_qry[...], causal[...], head_mask(h, head_size, width, scale)
         )
         prob_vis, prob_qry = joint_softmax(score_vis, score_qry)
-        given = upstream[...] * head_mask(h, head_size, width, 1.0)
+        given = upstream * head_mask(h, head_size, width, 1.0)
         dprob_vis = right_tmul(given, values_vis[...])
         dprob_qry = right_tmul(given, values_qry[...])
         inner = jnp.sum(prob_vis * dprob_vis, axis=-1, keepdims=True) + jnp.sum(
@@ -543,63 +596,72 @@
         out[...] = result.astype(out.dtype)
 
 
-def split_columns_kernel(shards, pieces, place, *refs):
-    weights, outs = refs[: len(pieces)], refs[len(pieces) :]
+def entry_kernel(shards, pieces, place, visual, weight, to_far, to_near, chunk):
+    own, rows = visual.shape[0], weight.shape[0]
+    part = weight.shape[1] // (pieces * shards)
+    to_far[:own, :] = visual[...]
+    to_near[:own, :] = visual[...]
     for me in range(shards):
 
         @pl.when(place[0] == me)
         def _(me=me):
             for k in range(shards):
-                j = me ^ k
-                blocks = []
-                for weight, count in zip(weights, pieces):
-                    step = weight.shape[1] // (count * shards)
-                    for s in range(count):
-                        start = (s * shards + j) * step
-                        blocks.append(weight[:, start : start + step])
-                outs[k][...] = jnp.concatenate(blocks, axis=1)
-
-
-def join_rows_kernel(shards, part, wide, place, *refs):
-    blocks, out = refs[:shards], refs[shards]
-    rows = blocks[0].shape[0]
-    for k in range(shards):
-        block = blocks[k][...]
-        if wide != part:
-            gap = jnp.zeros((rows, wide - part), block.dtype)
-            columns = []
-            for start in range(0, block.shape[1], part):
-                columns += [block[:, start : start + part], gap]
-            block = jnp.concatenate(columns, axis=1)
-        out[pl.ds(pl.multiple_of((place[0] ^ k) * rows, rows), rows), :] = block
-
-
-def entry_kernel(shards, pieces, wide, place, visual, weight, gains, to_far, to_near, chunk):
-    own, rows = visual.shape[0], weight.shape[0]
-    part = weight.shape[1] // (pieces * shards)
-    lanes = visual.shape[1]
-    gap = jnp.zeros((rows, wide - part), bf16)
-    line = jnp.concatenate([gains[...], jnp.zeros((gains.shape[0], lanes - gains.shape[1]), bf16)], axis=1)
-    to_far[:own, :] = visual[...]
-    to_near[:own, :] = visual[...]
-    to_far[own + 2 * rows :, :] = line
-    to_near[own + rows :, :] = line
+                starts = [(s * shards + (me ^ k)) * part for s in range(pieces)]
+                block = jnp.concatenate([weight[:, c : c + part] for c in starts], axis=1)
+                folded = fold(block, visual.shape[1])
+                height = folded.shape[0]
+                if k == 0:
+                    chunk[...] = folded
+                elif k == 1:
+                    to_near[own : own + height, :] = folded
+                else:
+                    to_far[own + (k - 2) * height : own + (k - 1) * height, :] = folded
+
+
+def split_columns_kernel(shards, place, attend, query, attend_qry, cross, out_weight, to_far, to_near, chunk):
+    rows, model = out_weight.shape
+    part = model // shards
+    sources = ((attend, 0), (attend, 1), (query, 0), (attend_qry, 0), (cross, 0), (cross, 1))
+    to_far[3 * rows :, :] = out_weight[...]
+    to_near[2 * rows :, :] = out_weight[...]
     for me in range(shards):
 
         @pl.when(place[0] == me)
         def _(me=me):
+            blocks = []
             for k in range(shards):
-                columns = []
-                for s in range(pieces):
-                    start = (s * shards + (me ^ k)) * part
-                    columns += [weight[:, start : start + part], gap]
-                block = jnp.concatenate(columns, axis=1)
-                if k == 0:
-                    chunk[...] = block
-                elif k == 1:
-                    to_near[own : own + rows, :] = block
-                else:
-                    to_far[own + (k - 2) * rows : own + (k - 1) * rows, :] = block
+                starts = [(s * shards + (me ^ k)) * part for _, s in sources]
+                pieces = [ref[:, c : c + part] for (ref, _), c in zip(sources, starts)]
+                blocks.append((jnp.concatenate(pieces[:4], axis=1), jnp.concatenate(pieces[4:], axis=1)))
+            chunk[:rows, :] = blocks[0][0]
+            chunk[rows:, : 2 * part] = blocks[0][1]
+            to_near[:rows, :] = blocks[1][0]
+            to_near[rows : 2 * rows, : 2 * part] = blocks[1][1]
+            to_far[:rows, :] = blocks[2][0]
+            to_far[rows : 2 * rows, :] = blocks[3][0]
+            to_far[2 * rows : 3 * rows, :] = jnp.concatenate([blocks[2][1], blocks[3][1]], axis=1)
+
+    chunk[rows:, 2 * part :] = jnp.zeros((rows, model - 2 * part), bf16)
+    to_near[rows : 2 * rows, 2 * part :] = jnp.zeros((rows, model - 2 * part), bf16)
+
+
+def join_columns_kernel(shards, wide, place, chunk, near, far, both, visual, query):
+    rows, model = chunk.shape[0] // 2, chunk.shape[1]
+    part = model // shards
+    gap = jnp.zeros((rows, wide - part), bf16)
+    sources = (
+        (0, chunk, 0, rows, 0), (1, near, 0, rows, 0), (2, far, 0, 2 * rows, 0), (3, both, rows, 2 * rows, 2 * part)
+    )
+    for k, ref, first, second, lane in sources:
+        block = ref[first : first + rows, :]
+        rest = ref[second : second + rows, :][:, lane : lane + 2 * part]
+        pieces = [block[:, s * part : (s + 1) * part] for s in range(4)]
+        pieces += [rest[:, s * part : (s + 1) * part] for s in range(2)]
+
+        at = pl.ds(pl.multiple_of((place[0] ^ k) * rows, rows), rows)
+        for out, items in ((visual, (0, 1, 2)), (query, (3, 0, 1, 4, 5))):
+            for place_, item in enumerate(items):
+                out[at, place_ * wide : (place_ + 1) * wide] = jnp.concatenate([pieces[item], gap], axis=1)
 
 
 def share_kernel(shards, place, first, second, third, *refs):
@@ -662,31 +724,71 @@
                 out[to : to + down_share, :] = result[g * down_share : (g + 1) * down_share]
 
 
-def lay_out_feed_kernel(shards, place, given, up, up_qry, down, down_qry):
-    halfway = GROUPS // 2
-    up_share, down_share = up.shape[0] // halfway, down.shape[0] // halfway
-    size, width = shards * up_share + down_share, given.shape[1]
+def lay_out_feed_kernel(shards, place, ups, downs, up, up_qry, down, down_qry):
+    rows, height, width = up.shape[0], down.shape[0], ups.shape[1]
     for me in range(shards):
 
         @pl.when(place[0] == me)
         def _(me=me):
-            for g in range(GROUPS):
-                out = (up, up_qry)[g // halfway]
-                to = g % halfway * up_share
-                for j in range(shards):
-                    start = g * size + (me ^ j) * up_share
-                    out[to : to + up_share, j * width : (j + 1) * width] = given[start : start + up_share, :].astype(f32)
-
-    for g in range(GROUPS):
-        out = (down, down_qry)[g // halfway]
-        to, start = g % halfway * down_share, g * size + shards * up_share
-        out[to : to + down_share, :] = given[start : start + down_share, :].astype(f32)
+            for j in range(shards):
+                start = (me ^ j) * 2 * rows
+                at = slice(j * width, (j + 1) * width)
+                up[:, at] = ups[start : start + rows, :].astype(f32)
+                up_qry[:, at] = ups[start + rows : start + 2 * rows, :].astype(f32)
+
+    down[...] = downs[:height, :].astype(f32)
+    down_qry[...] = downs[height:, :].astype(f32)
+
+
+def fold(block, width):
+    rows, lanes = block.shape
+    if lanes > width:
+        rest = block[:, width:]
+        count = width // rest.shape[1]
+        step = rows // count
+        return jnp.concatenate(
+            [block[:, :width], jnp.concatenate([rest[i * step : (i + 1) * step] for i in range(count)], axis=1)], axis=0
+        )
+    half = rows // 2
+    first, second = block[:half], block[half:]
+    gap = width - lanes
+    rest = second[:, gap:]
+    count = width // rest.shape[1]
+    step = half // count
+    return jnp.concatenate(
+        [
+            jnp.concatenate([first, second[:, :gap]], axis=1),
+            jnp.concatenate([rest[i * step : (i + 1) * step] for i in range(count)], axis=1),
+        ],
+        axis=0,
+    )
+
+
+def unfold(block, rows, lanes):
+    width = block.shape[1]
+    if lanes > width:
+        count = width // (lanes - width)
+        part = lanes - width
+        last = block[rows:]
+        return jnp.concatenate(
+            [block[:rows], jnp.concatenate([last[:, i * part : (i + 1) * part] for i in range(count)], axis=0)], axis=1
+        )
+    half = rows // 2
+    gap = width - lanes
+    part = lanes - gap
+    last = block[half:]
+    rest = jnp.concatenate([last[:, i * part : (i + 1) * part] for i in range(width // part)], axis=0)
+    first = block[:half]
+    return jnp.concatenate(
+        [first[:, :lanes], jnp.concatenate([first[:, lanes:], rest], axis=1)], axis=0
+    )
 
 
 def split_halves_kernel(shards, part, wide, place, *refs):
-    grads, keep, give = refs[:-2], refs[-2], refs[-1]
+    grads, own_rows, keep, give = refs[:-3], refs[-3], refs[-2], refs[-1]
     rows = grads[0].shape[0] // shards
-    half = rows // 2
+    half, entry = rows // 2, keep.shape[0] // shards
+    quarter = own_rows.shape[0] // (2 * shards)
     for k in range(shards):
         for out, side in ((keep, place[1]), (give, 1 - place[1])):
             start = pl.multiple_of((place[0] ^ k) * rows + side * half, half)
@@ -694,34 +796,69 @@
             for grad in grads:
                 block = grad[pl.ds(start, half), :]
                 columns += [block[:, c : c + part] for c in range(0, block.shape[1], wide)]
-            out[k * half : (k + 1) * half, :] = jnp.concatenate(columns, axis=1).astype(bf16)
-
-
-def lay_out_kernel(shards, pieces, halves, place, *refs):
-    blocks, outs = refs[: 2 if halves else 1], refs[2 if halves else 1 :]
-    rows = blocks[0].shape[0] // shards
-    for me in range(shards):
-
-        @pl.when(place[0] == me)
-        def _(me=me):
-            start = 0
-            for out, count in zip(outs, pieces):
-                step = out.shape[1] // (count * shards)
-                for b, block in enumerate(blocks):
+            out[k * entry : k * entry + half, :] = jnp.concatenate(columns, axis=1).astype(bf16)
+            start = pl.multiple_of(side * quarter * shards + k * quarter, 8)
+            block = own_rows[pl.ds(start, quarter), :]
+            out[k * entry + half : (k + 1) * entry, :] = fold(block, out.shape[1]).astype(bf16)
+
+
+def lay_out_kernel(shards, pieces, direct, place, here, other, *outs):
+    outs, own_rows = outs[:-1], outs[-1]
+    half = outs[0].shape[0] // 2
+    entry = here.shape[0] // shards
+    quarter = own_rows.shape[0] // (2 * shards)
+    depth = place[2] if direct else 0
+    for first in range(shards):
+
+        @pl.when((place[0] ^ depth) == first)
+        def _(first=first):
+            for block, side in ((here, place[1]), (other, 1 - place[1])):
+                start = 0
+                for out, count in zip(outs, pieces):
+                    step = out.shape[1] // (count * shards)
                     columns = []
                     for s in range(count):
                         for j in range(shards):
-                            k = me ^ j
-                            columns.append(
-                                block[k * rows : (k + 1) * rows, start + s * step : start + (s + 1) * step]
-                            )
+                            at = (first ^ j) * entry
+                            columns.append(block[at : at + half, start + s * step : start + (s + 1) * step])
                     result = jnp.concatenate(columns, axis=1).astype(f32)
-                    if halves:
-                        side = place[1] if b == 0 else 1 - place[1]
-                        out[pl.ds(pl.multiple_of(side * rows, rows), rows), :] = result
-                    else:
-                        out[...] = result
-                start += step * count
+                    out[pl.ds(pl.multiple_of(side * half, 8), half), :] = result
+                    start += step * count
+
+    for block, side in ((here, place[1]), (other, 1 - place[1])):
+        for k in range(shards):
+            piece = block[k * entry + half : (k + 1) * entry, :].astype(f32)
+            start = pl.multiple_of(side * quarter * shards + (k ^ depth) * quarter, 8)
+            own_rows[pl.ds(start, quarter), :] = unfold(piece, quarter, own_rows.shape[1])
+
+
+def lay_out_pages_kernel(shards, pieces, place, blocks, *outs):
+    outs, own_rows = outs[:-1], outs[-1]
+    half = outs[0].shape[0] // 2
+    entry = blocks.shape[0] // (2 * shards)
+    quarter = own_rows.shape[0] // (2 * shards)
+    for me in range(shards):
+
+        @pl.when(place[0] == me)
+        def _(me=me):
+            for side in range(2):
+                start = 0
+                for out, count in zip(outs, pieces):
+                    step = out.shape[1] // (count * shards)
+                    columns = []
+                    for s in range(count):
+                        for j in range(shards):
+                            at = (2 * (me ^ j) + side) * entry
+                            columns.append(blocks[at : at + half, start + s * step : start + (s + 1) * step])
+                    out[side * half : (side + 1) * half, :] = jnp.concatenate(columns, axis=1).astype(f32)
+                    start += step * count
+
+    for side in range(2):
+        for k in range(shards):
+            at = (2 * k + side) * entry
+            piece = blocks[at + half : at + entry, :].astype(f32)
+            start = (side * shards + k) * quarter
+            own_rows[start : start + quarter, :] = unfold(piece, quarter, own_rows.shape[1])
 
 
 def kernel_call(function, grid, ins, outs, args, scratch=(), place=None, name=None, us=2):
@@ -866,27 +1003,26 @@
             (pl.BlockSpec((own, model), lambda i, *_: (jnp.maximum(i - count, 0), 0)), shape),
         ]
 
-    gains = jnp.concatenate(
-        [gain_window, gain_visual, gain_query, gain_feed, gain_query_feed, jnp.zeros((11 * rows,), bf16)]
-    ).reshape(16, rows)
+    visual_own = visual[0].reshape(own, model)
+    folded_rows = rows * 3 * part // model
     to_far, to_near, chunk = kernel_call(
-        functools.partial(entry_kernel, shards, 3, wide),
+        functools.partial(entry_kernel, shards, 3),
         (1,),
-        [whole((own, model)), whole(window_qkv.shape), whole(gains.shape)],
+        [whole((own, model)), whole(window_qkv.shape)],
         [
-            full_out((own + 2 * rows + 16, model), bf16),
-            full_out((own + rows + 16, model), bf16),
-            full_out((rows, 3 * wide), bf16),
+            full_out((own + 2 * folded_rows, model), bf16),
+            full_out((own + folded_rows, model), bf16),
+            full_out((folded_rows, model), bf16),
         ],
-        (visual[0].reshape(own, model), window_qkv, gains),
+        (visual_own, window_qkv),
         place=where_me,
         name="entry",
     )
     far = swap(to_far, "win", 2)
     near = swap(to_near, "win", 1)
-    slots = bias_slots(position_bias.astype(f32), column_regions[0], page_width)
-    far_now = tie(slots, far)[0]
-    both = swap(far_now, "win", 1)
+    gain_tied = tie(to_far, gain_window, gain_visual, gain_query, gain_feed, gain_query_feed)
+    gains = jnp.concatenate([*gain_tied, jnp.zeros((11 * rows,), bf16)]).reshape(16, rows)
+    gain_parts = gather_four(gains)
 
     height = -(-3 * rows // (16 * pages)) * 16
     shares = kernel_call(
@@ -899,23 +1035,31 @@
         place=jnp.stack([me, page]),
         name="share",
     )
-    spread_weights = lax.all_gather(jnp.stack(exchange(shares)), "page")
-
-    tied = tie(far, attend_kv, cross_query, attend_query, cross_kv, window_out)
-    mixed_width = 6 * part
-    blocks = kernel_call(
-        functools.partial(split_columns_kernel, shards, [2, 1, 1, 2]),
+    shares = exchange(shares)
+
+    mixed_far, mixed_near, mixed_own = kernel_call(
+        functools.partial(split_columns_kernel, shards),
         (1,),
-        all_of(*tied[:4]),
-        [full_out((rows, mixed_width), bf16)] * shards,
-        tied[:4],
+        all_of(attend_kv, cross_query, attend_query, cross_kv, window_out),
+        [
+            full_out((4 * rows, model), bf16),
+            full_out((3 * rows, model), bf16),
+            full_out((2 * rows, model), bf16),
+        ],
+        (attend_kv, cross_query, attend_query, cross_kv, window_out),
         place=where_me,
         name="split_columns",
     )
-    mixed_parts = exchange(blocks)
-    out_parts = gather_four(tied[4])
-
-    both = tie(blocks[1], both)[0]
+    slots = bias_slots(position_bias.astype(f32), column_regions[0], page_width)
+    far, slots, mixed_far, mixed_near, mixed_own, *rest = fence(
+        far, slots, mixed_far, mixed_near, mixed_own, *shares, *gain_parts
+    )
+    shares, gain_parts = rest[:shards], rest[shards:]
+    spread_weights = lax.all_gather(jnp.stack(shares), "page")
+    both = swap(far, "win", 1)
+    mixed_from_far = swap(mixed_far, "win", 2)
+    mixed_from_near = swap(mixed_near, "win", 1)
+
     places = window_places(page_width)
     row_mask = np.zeros((stripes, 1, WS * WS), np.float32)
     row_mask[0, :, : WS * WS // 2] = masked_fill
@@ -938,7 +1082,7 @@
     vis_low, qkv_w, gains_all, norm_win, packed, heads_win = kernel_call(
         functools.partial(window_forward_kernel, *static),
         (stripes,),
-        all_of(to_far, far, near, both, chunk) + window_specs,
+        all_of(to_far, far, near, both, chunk, *gain_parts) + window_specs,
         [
             of_tokens(arriving, model),
             full_out((model, 3 * wide), bf16),
@@ -947,41 +1091,51 @@
             of_tokens(arriving, 3 * wide),
             (leaving(wide, short), jax.ShapeDtypeStruct((short * shards, wide), bf16)),
         ],
-        (to_far, far, near, both, chunk) + window_args,
+        (to_far, far, near, both, chunk, *gain_parts) + window_args,
         scratch=[pltpu.VMEM((own, 3 * wide), bf16)] * 2
         + [pltpu.VMEM((own // 2, wide), f32), pltpu.VMEM((own, model), bf16)],
         place=position,
         name="window_forward",
         us=17,
     )
-    win_parts = gather_four(heads_win)
-
-    tied = tie(heads_win, *mixed_parts)
-    mixed_w = kernel_call(
-        functools.partial(join_rows_kernel, shards, part, wide),
-        (1,),
-        all_of(*tied),
-        [full_out((model, 6 * wide), bf16)],
-        tied,
-        place=where_me,
-        name="join_rows",
-    )[0]
-    vis_w = mixed_w[:, : 3 * wide]
-    qry_w = jnp.concatenate(
-        [mixed_w[:, 3 * wide : 4 * wide], mixed_w[:, : 2 * wide], mixed_w[:, 4 * wide :]], axis=1
-    )
-    query_in = queries[0].astype(f32)
-    norm_qry = norm_low(query_in, gains_all[2:3])
-    proj_qry = matmul(norm_qry, qry_w).astype(bf16)
+    packed, norm_win, vis_low, gains_all, qkv_w, heads_win, mixed_from_far, mixed_from_near = fence(
+        packed, norm_win, vis_low, gains_all, qkv_w, heads_win, mixed_from_far, mixed_from_near
+    )
+    win_far, win_near = swap(heads_win, "win", 2), swap(heads_win, "win", 1)
+    late_inputs = tie(heads_win, window_out, cross_out, attend_out, cotangent_visual)
     length = query_lengths[0]
     slot_ids = jnp.arange(slots_count, dtype=jnp.int32)
     live = slot_ids < length
     live_mask = jnp.where(live, 0.0, masked_fill).astype(f32)[None]
     reach = (slot_ids[None, :] <= slot_ids[:, None]) & live[None, :]
     causal_mask = jnp.where(reach, 0.0, masked_fill).astype(f32)
-    tied = tie(win_parts[1], attend_out, cotangent_visual)
-    attend_parts = gather_four(tied[0])
-    top_parts = gather_four(tied[1][0].reshape(own, model))
+    window_rows_out = jnp.pad(late_inputs[0], ((0, wide - part), (0, 0)))
+    cross_rows_out = jnp.pad(late_inputs[1], ((0, wide - part), (0, 0)))
+    attend_rows_out = jnp.pad(late_inputs[2], ((0, wide - part), (0, 0)))
+    top_own = late_inputs[3][0].reshape(own, model)
+    mixed_from_both = swap(mixed_from_far, "win", 1)
+
+    vis_w, qry_w = kernel_call(
+        functools.partial(join_columns_kernel, shards, wide),
+        (1,),
+        all_of(mixed_own, mixed_from_near, mixed_from_far, mixed_from_both),
+        [full_out((model, 3 * wide), bf16), full_out((model, 5 * wide), bf16)],
+        (mixed_own, mixed_from_near, mixed_from_far, mixed_from_both),
+        place=where_me,
+        name="join_columns",
+    )
+    query_in = queries[0].astype(f32)
+    norm_qry = norm_low(query_in, gains_all[2:3])
+    proj_qry = matmul(norm_qry, qry_w).astype(bf16)
+    (
+        vis_w, qry_w, proj_qry, live_mask, causal_mask, window_rows_out, cross_rows_out, attend_rows_out, top_own,
+        win_far
+    ) = fence(
+        vis_w, qry_w, proj_qry, live_mask, causal_mask, window_rows_out, cross_rows_out, attend_rows_out, top_own,
+        win_far
+    )
+    win_parts = [heads_win, win_far, win_near, swap(win_far, "win", 1)]
+    top_far = swap(top_own, "win", 2)
 
     def qry_piece(i):
         return pl.BlockSpec((slots_count, wide), lambda *_: (0, i))
@@ -991,21 +1145,31 @@
 
     def piece_specs():
         return [pl.BlockSpec((short, wide), lambda i, *_, k=k: (i ^ k, 0)) for k in range(shards)]
+
+    def rows_block(i):
+        return pl.BlockSpec((rows, model), lambda *_: (i, 0))
 
     mid, norm_vis, proj_vis, heads_cross = kernel_call(
         functools.partial(middle_kernel, *static),
         (shards,),
         [block_of(model)]
         + piece_specs()
-        + all_of(*out_parts, gains_all, vis_w)
+        + [rows_block(0), rows_block(3), rows_block(2), rows_block(3)]
+        + all_of(gains_all, vis_w)
         + [qry_piece(3), qry_piece(4)]
         + all_of(live_mask),
         [token_out(model, f32), token_out(model), token_out(3 * wide), packed_out()],
-        (vis_low, *win_parts, *out_parts, gains_all, vis_w, proj_qry, proj_qry, live_mask),
+        (
+            vis_low, *win_parts, window_out, mixed_from_far, mixed_from_near, mixed_from_both, gains_all, vis_w,
+            proj_qry, proj_qry, live_mask,
+        ),
         name="middle",
         us=13,
     )
-    cross_parts = gather_four(heads_cross)
+    mid, norm_vis, proj_vis, heads_cross, top_far = fence(mid, norm_vis, proj_vis, heads_cross, top_far)
+    cross_far, cross_near = swap(heads_cross, "win", 2), swap(heads_cross, "win", 1)
+    top_near = swap(top_own, "win", 1)
+    top_both = swap(top_far, "win", 1)
 
     query_specs = [
         qry_piece(0),
@@ -1025,48 +1189,60 @@
         name="query_forward",
         us=4,
     )
-    qry_parts = gather_four(heads_qry)
-    tied = tie(heads_qry, spread_weights, *top_parts)
     (three,) = kernel_call(
         unshare_kernel,
         (1,),
-        all_of(tied[0]),
+        all_of(spread_weights),
         [full_out((3 * model, model), bf16)],
-        (tied[0],),
+        tie(heads_qry, spread_weights),
         place=where_me,
         name="unshare",
     )
     vup_w, qup_w, cross_out_w = [three[i * model : (i + 1) * model] for i in range(3)]
-    top_low = jnp.concatenate(tied[1:], axis=0)
-    top_now = tie(qry_parts[3], *tie(attend_parts[3], top_low))[0]
-
-    late, norm_feed, act_vis, dhid_vis, feed_keep, feed_send = kernel_call(
+    qry_far = swap(heads_qry, "win", 2)
+    qry_near = swap(heads_qry, "win", 1)
+    vup_w, qup_w, cross_out_w, qry_far, cross_far = fence(vup_w, qup_w, cross_out_w, qry_far, cross_far)
+    qry_parts = [heads_qry, qry_far, qry_near, swap(qry_far, "win", 1)]
+    cross_parts = [heads_cross, cross_far, cross_near, swap(cross_far, "win", 1)]
+    top_parts = [top_own, top_far, top_near, top_both]
+    attend_far = swap(tie(cross_far, attend_out)[0], "win", 2)
+    attend_near = swap(attend_out, "win", 1)
+
+    late, norm_feed, act_vis, dhid_vis, top_low, feed_keep, feed_send = kernel_call(
         functools.partial(feed_kernel, part),
         (shards,),
         [block_of(model)]
         + piece_specs()
-        + all_of(cross_out_w, gains_all, vup_w, visual_down)
-        + [block_of(model)],
-        [full_out((own, model), f32), token_out(model), token_out(hidden), token_out(hidden)] + half_outs(),
-        (mid, *cross_parts, cross_out_w, gains_all, vup_w, visual_down, top_now),
+        + all_of(cross_out_w, gains_all, vup_w, visual_down, *top_parts),
+        [full_out((own, model), f32), token_out(model), token_out(hidden), token_out(hidden), token_out(model)]
+        + half_outs(),
+        (mid, *cross_parts, cross_out_w, gains_all, vup_w, visual_down, *top_parts),
+        scratch=[pltpu.VMEM((own, model), bf16)],
         place=where_me,
         name="feed",
         us=18,
     )
+    late, norm_feed, act_vis, dhid_vis, top_low, feed_keep, feed_send, attend_far, *qry_parts = fence(
+        late, norm_feed, act_vis, dhid_vis, top_low, feed_keep, feed_send, attend_far, *qry_parts
+    )
+    attend_parts = [attend_out, attend_far, attend_near, swap(attend_far, "win", 1)]
     feed_terms, feed_second = scatter_pieces(feed_keep, feed_send)
 
-    tied = tie(feed_second, *qry_parts, *attend_parts)
-    query_mid = query_in + matmul(
-        jnp.concatenate(tied[:shards], axis=1), jnp.concatenate(tied[shards:], axis=0)
-    )
-    norm_qfeed = norm_low(query_mid, gains_all[4:5])
-    act_qry, slope_qry = gelu_both(matmul(norm_qfeed, qup_w))
-    act_qry = act_qry.astype(bf16)
-    dhid_qry = (right_tmul(cotangent_query[0], query_down) * slope_qry).astype(bf16)
-    dqfeed_part = right_tmul(dhid_qry, qup_w)
+    tied = tie(feed_send, *qry_parts, *attend_parts)
+    feed_args = (queries[0], *tied, gains_all, qup_w, query_down, cotangent_query[0])
+    slot_shape = (slots_count, model)
+    query_mid, norm_qfeed, act_qry, dhid_qry, dqfeed_part = kernel_call(
+        query_feed_kernel,
+        (1,),
+        all_of(*feed_args),
+        [full_out(slot_shape, f32)] + [full_out(slot_shape, bf16)] * 4,
+        feed_args,
+        name="query_feed",
+        us=6,
+    )
     dqfeed, dqfeed_last = total_sum(dqfeed_part)
     pairs = (norm_feed, dhid_vis, act_vis, top_low, norm_qfeed, dhid_qry, act_qry, cotangent_query[0])
-    pairs = tie(dqfeed_last, *tie(feed_second, *pairs))
+    pairs = tie(dqfeed_last, *pairs)
     (feed_grads,) = kernel_call(
         functools.partial(feed_grads_kernel, shards),
         (4,),
@@ -1076,17 +1252,33 @@
         name="feed_grads",
         us=10,
     )
+    act_now, act_qry_now = tie(feed_grads, act_vis, act_qry)
+    final_keep, final_send = kernel_call(
+        halves_kernel,
+        (shards,),
+        [block_of(hidden), whole(visual_down.shape)],
+        half_outs(),
+        (act_now, visual_down),
+        name="visual_final",
+        us=4,
+    )
+    query_final_part = matmul(act_qry_now, query_down).astype(bf16)
+    query_mid, dqfeed_last, feed_last, feed_grads, final_keep, final_send, query_final_part = fence(
+        query_mid, dqfeed_last, feed_terms[2], feed_grads, final_keep, final_send, query_final_part
+    )
+    feed_terms = (feed_terms[0], feed_terms[1], feed_last)
     up_share, down_share = 2 * rows // GROUPS, 2 * hidden // GROUPS
 
-    def to_sources(group):
-        stack = group[: shards * up_share].reshape(shards, up_share, model)
-        return jnp.concatenate(trade(stack) + [group[shards * up_share :]], axis=0)
+    def to_sources(summed):
+        groups = summed.reshape(GROUPS, -1, model)
+        ups = groups[:, : shards * up_share].reshape(GROUPS, shards, up_share, model).transpose(1, 0, 2, 3)
+        ups = trade(ups.reshape(shards, GROUPS * up_share, model))
+        return jnp.concatenate(ups, axis=0), groups[:, shards * up_share :].reshape(-1, model)
 
     if pages == GROUPS:
-        feed_sum = to_sources(lax.psum_scatter(feed_grads, "page", scatter_dimension=0, tiled=True))
+        feed_sum = lax.psum_scatter(feed_grads, "page", scatter_dimension=0, tiled=True)
     else:
-        summed = lax.psum(feed_grads, "page").reshape(GROUPS, -1, model)
-        feed_sum = jnp.concatenate([to_sources(summed[g]) for g in range(GROUPS)], axis=0)
+        feed_sum = lax.psum(feed_grads, "page")
 
     def back_through_norm(line, tensor, terms, residual, dtypes):
         own_block = pl.BlockSpec((own, model), lambda *_: (0, 0))
@@ -1099,32 +1291,28 @@
             name="norm_back",
         )
 
-    (last_term,) = tie(feed_grads, feed_terms[2])
-    grad_late, dz_cross = back_through_norm(
-        3,
-        late,
-        (feed_terms[0], feed_terms[1], last_term),
-        cotangent_visual[0].reshape(own, model),
-        [f32, bf16],
-    )
+    grad_late, dz_cross = back_through_norm(3, late, feed_terms, top_own, [f32, bf16])
+    grad_late, dz_cross = fence(grad_late, dz_cross)
     cross_dz = gather_four(dz_cross)
 
-    (dqfeed,) = tie(dz_cross, dqfeed)
-    grad_qmid = cotangent_query[0].astype(f32) + norm_back(query_mid, gains_all[4:5], dqfeed)
-    dz_attend = grad_qmid.astype(bf16)
-    dheads_qry = right_tmul(dz_attend, jnp.pad(attend_out, ((0, wide - part), (0, 0)))).astype(bf16)
-    dq, dkq, dvq, dkv, dvv = kernel_call(
+    back_args = query_args + (query_mid, gains_all, cotangent_query[0], dqfeed, attend_rows_out)
+    dq, dkq, dvq, dkv, dvv, grad_qmid, dz_attend = kernel_call(
         functools.partial(query_backward_kernel, *static),
         (1,),
-        query_specs + [whole((slots_count, wide))],
-        [full_out((slots_count, wide), bf16)] * 3 + [full_out((tokens, wide), bf16)] * 2,
-        query_args + (dheads_qry,),
+        query_specs + all_of(*back_args[len(query_args) :]),
+        [full_out((slots_count, wide), bf16)] * 3
+        + [full_out((tokens, wide), bf16)] * 2
+        + [full_out(slot_shape, f32), full_out(slot_shape, bf16)],
+        back_args,
         name="query_backward",
         us=8,
     )
-    grad_attend_out = left_tmul(heads_qry, dz_attend)
-
-    out_rows = jnp.pad(cross_out, ((0, wide - part), (0, 0)))
+    query_total, query_last = total_sum(query_final_part)
+    (final_own, final_near, final_last), final_second = scatter_pieces(final_keep, final_send)
+    dkv, final_second, query_last, cross_far = fence(dkv, final_second, query_last, cross_dz[1])
+    cross_dz = [cross_dz[0], cross_far, cross_dz[2], swap(cross_far, "win", 1)]
+
+    out_rows = cross_rows_out
     dproj_vis, dck, dcv, grad_cross_out, vis_keep, vis_send = kernel_call(
         functools.partial(cross_backward_kernel, *static),
         (shards,),
@@ -1141,133 +1329,153 @@
         name="cross_backward",
         us=16,
     )
+    dproj_vis, dck, dcv, grad_cross_out, vis_keep, vis_send, grad_qmid, dz_attend, final_last, query_total = fence(
+        dproj_vis, dck, dcv, grad_cross_out, vis_keep, vis_send, grad_qmid, dz_attend, final_last, query_total
+    )
     vis_terms, vis_second = scatter_pieces(vis_keep, vis_send)
 
-    def halves_here(*grads):
+    depth, side = page // 2, page % 2
+    direct = pages == 2 * LINE and shards == LINE
+    where_all = jnp.stack([me, side, depth])
+
+    def halves_here(grads, own_rows):
         width = sum(g.shape[1] for g in grads) // wide * part
+        entry = rows // 2 + own_rows.shape[0] * model // (2 * shards * width)
         return kernel_call(
             functools.partial(split_halves_kernel, shards, part, wide),
             (1,),
-            all_of(*grads),
-            [full_out((model // 2, width), bf16)] * 2,
-            grads,
-            place=where_page,
+            all_of(*grads, own_rows),
+            [full_out((shards * entry, width), bf16)] * 2,
+            (*grads, own_rows),
+            place=where_all,
             name="split_halves",
             us=3,
         )
 
-    depth, side = page // 2, page % 2
-
-    def laid_out(blocks, pieces, width):
-        direct = pages == 2 * LINE
+    def laid_out(here, other, pieces, width, row_count_):
         return kernel_call(
-            functools.partial(lay_out_kernel, shards, pieces, True),
+            functools.partial(lay_out_kernel, shards, pieces, direct),
             (1,),
-            all_of(*blocks),
-            [full_out((rows, count * width * shards), f32) for count in pieces],
-            blocks,
-            place=jnp.stack([me ^ depth, side]) if direct else where_page,
+            all_of(here, other),
+            [full_out((rows, count * width * shards), f32) for count in pieces]
+            + [full_out((row_count_, model), f32)],
+            (here, other),
+            place=where_all,
             name="lay_out",
             us=2,
         )
 
+    def laid_out_pages(blocks, pieces, width, row_count_):
+        return kernel_call(
+            functools.partial(lay_out_pages_kernel, shards, pieces),
+            (1,),
+            all_of(blocks),
+            [full_out((rows, count * width * shards), f32) for count in pieces]
+            + [full_out((row_count_, model), f32)],
+            (blocks,),
+            place=where_all,
+            name="lay_out_pages",
+            us=2,
+        )
+
     def beside(tensor):
-        return lax.ppermute(tensor, "page", [(i, i ^ 1) for i in range(pages)])
-
-    def to_rows(half):
-        height = half.shape[0] // shards
-        return jnp.concatenate(exchange([half[k * height : (k + 1) * height] for k in range(shards)]), axis=0)
+        return lax.ppermute(tensor, "page", [(i, i ^ 1) for i in range(pages)]) if pages > 1 else tensor
 
     def pair_total(keep, give):
         return keep if pages == 1 else add_low(keep, beside(give))
 
-    def parity_sum(tensor):
-        groups = [list(range(s, pages, 2)) for s in (0, 1)]
-        return lax.psum(tensor, "page", axis_index_groups=groups)
-
-    def columns_scatter(own_half):
-        own_chunk = line_scatter(own_half.reshape(shards, -1, own_half.shape[1]), depth)
+    def line_terms(own_half):
+        return line_send(own_half.reshape(shards, -1, own_half.shape[1]), depth) if direct else [own_half]
+
+    def line_entry(terms):
+        if not direct:
+            return terms[0]
+        entry = line_add(terms)
         pairs = [
             (p * shards + w, p * shards + (w ^ (p // 2))) for p in range(pages) for w in range(shards)
         ]
-        return lax.ppermute(own_chunk, ("page", "win"), pairs)
-
-    def columns_gather(chunk):
-        here = jnp.concatenate(line_gather(chunk), axis=0)
+        moved = lax.ppermute(entry[: rows // 2], ("page", "win"), pairs)
+        return jnp.concatenate([moved, entry[rows // 2 :]], axis=0)
+
+    def line_here(entry):
+        return jnp.concatenate(line_gather(entry), axis=0) if direct else entry
+
+    def page_gather(entry, give):
+        if direct:
+            return entry, beside(entry)
+
+        def to_columns(half):
+            entries = half.reshape(shards, -1, half.shape[1])
+            moved = exchange([entries[k, : rows // 2] for k in range(shards)])
+            return jnp.concatenate(
+                [x for k in range(shards) for x in (moved[k], entries[k, rows // 2 :])], axis=0
+            )
+
+        if pages == 1:
+            return to_columns(entry), to_columns(give)
+        groups = [list(range(s, pages, 2)) for s in (0, 1)]
+        here = to_columns(lax.psum(entry, "page", axis_index_groups=groups))
         return here, beside(here)
 
-    def columns_total(own_half, give):
-        if pages == 1:
-            return to_rows(own_half), to_rows(give)
-        here = to_rows(parity_sum(own_half))
-        return here, beside(here)
-
-    def rows_halves(grad):
-        stack = grad.astype(bf16).reshape(2, -1, grad.shape[1])
-        return pick(stack, side), pick(stack, 1 - side)
-
-    def rows_scatter(own_half):
-        return line_scatter(own_half.reshape(LINE, -1, own_half.shape[1]), depth)
-
-    def rows_gather(quarter):
-        stack = jnp.stack(line_gather(quarter))
-        here = jnp.concatenate([pick(stack, depth ^ q) for q in range(LINE)], axis=0)
-        return both_halves(here, beside(here))
-
-    def both_halves(here, other):
-        first = side == 0
-        return jnp.concatenate([jnp.where(first, here, other), jnp.where(first, other, here)], axis=0).astype(f32)
-
-    def rows_total(own_half, give):
-        if pages == 1:
-            return both_halves(own_half, give)
-        here = parity_sum(own_half)
-        return both_halves(here, beside(here))
-
-    def scattered(columns, rows_):
-        if pages == 2 * LINE and shards == LINE:
-            return columns_scatter(columns), rows_scatter(rows_)
-        return columns, rows_
-
-    def gathered(columns, rows_, halves, rows_half):
-        if pages == 2 * LINE and shards == LINE:
-            return columns_gather(columns), rows_gather(rows_)
-        return columns_total(columns, halves[1]), rows_total(rows_, rows_half[1])
-
-    (dproj_now, norm_now, dck, dcv) = tie(vis_second, dproj_vis, norm_vis, dck, dcv)
+    grouped = feed_grads.reshape(2, GROUPS // 2, -1, model)[:, :, : shards * up_share]
+    up_grads = grouped.reshape(2, GROUPS // 2, shards, up_share, model).transpose(0, 2, 1, 3, 4)
+    up_grads = up_grads.reshape(2, shards * up_share * (GROUPS // 2), model)
+
+    def gain_sum(line, weight, grad):
+        return jnp.sum(weight.astype(f32) * grad.astype(f32), axis=1) / gains_all[line]
+
+    dproj_now, norm_now, dck, dcv, dz_attend = tie(vis_second, dproj_vis, norm_vis, dck, dcv, dz_attend)
     dproj_qry = jnp.concatenate([dq, dkq, dvq, dck.astype(bf16), dcv.astype(bf16)], axis=1)
+    dnorm_qry, dnorm_last = total_sum(right_tmul(dproj_qry, qry_w))
     grad_vis_w = left_tmul(norm_now, dproj_now)
     grad_qry_w = left_tmul(norm_qry, dproj_qry)
-    dnorm_qry, _ = total_sum(right_tmul(dproj_qry, qry_w))
+    grad_attend_out = left_tmul(heads_qry, dz_attend)
     qry_columns = [grad_qry_w[:, i * wide : (i + 1) * wide] for i in range(5)]
     mixed_halves = halves_here(
-        grad_vis_w[:, :wide] + qry_columns[1],
-        grad_vis_w[:, wide : 2 * wide] + qry_columns[2],
-        grad_vis_w[:, 2 * wide :],
-        qry_columns[0],
-        qry_columns[3],
-        qry_columns[4],
-    )
-    outs_halves = rows_halves(jnp.concatenate([grad_cross_out, grad_attend_out], axis=0))
-    (last_term,) = tie(mixed_halves[0], vis_terms[2])
-    grad_mid, dz_window = back_through_norm(
-        1, mid, (vis_terms[0], vis_terms[1], last_term), grad_late, [f32, bf16]
-    )
+        (
+            grad_vis_w[:, :wide] + qry_columns[1],
+            grad_vis_w[:, wide : 2 * wide] + qry_columns[2],
+            grad_vis_w[:, 2 * wide :],
+            qry_columns[0],
+            qry_columns[3],
+            qry_columns[4],
+        ),
+        jnp.concatenate([grad_cross_out, grad_attend_out], axis=0),
+    )
+    *mixed_halves, vis_last = fence(*mixed_halves, vis_terms[2])
+    vis_terms = (vis_terms[0], vis_terms[1], vis_last)
+    grad_mid, dz_window = back_through_norm(1, mid, vis_terms, grad_late, [f32, bf16])
+    grad_mid, dz_window = fence(grad_mid, dz_window)
     window_dz = gather_four(dz_window)
-
-    act_now, dnorm_qry = tie(dz_window, act_vis, dnorm_qry)
-    final = matmul(act_now, visual_down).astype(bf16)
-    final_terms, _ = scatter_pieces(final[: tokens // 2], final[tokens // 2 :])
+    mixed_pair = pair_total(*mixed_halves)
+
+    final_last, query_total = tie(dz_window, final_last, query_total)
+    visual_final = late + (
+        final_own[:own].astype(f32) + final_near[:own].astype(f32) + final_last.astype(f32)
+    )
+    visual_final = visual_final.astype(bf16)
+    query_final = (query_mid + query_total).astype(bf16)
     query_back = (grad_qmid + norm_back(query_in, gains_all[2:3], dnorm_qry)).astype(bf16)
-    query_final = query_mid + total_sum(matmul(act_qry, query_down))[0]
-
-    out_rows = jnp.pad(window_out, ((0, wide - part), (0, 0)))
-    mixed_pair, outs_pair = pair_total(*mixed_halves), pair_total(*outs_halves)
-    first_dz = tie(final, *tie(mixed_pair, *tie(outs_pair, window_dz[0])))[0]
     if pages == GROUPS:
-        first_dz = tie(feed_sum, first_dz)[0]
+        feed_sum = tie(window_dz[1], feed_sum)[0]
+    gain_rows = [
+        gain_sum(i, w, g)
+        for i, w, g in (
+            (1, vis_w, grad_vis_w),
+            (2, qry_w, grad_qry_w),
+            (3, vup_w, up_grads[0]),
+            (4, qup_w, up_grads[1]),
+        )
+    ]
+    mixed_pair, feed_sum, query_back, visual_final, query_final, *rest = fence(
+        mixed_pair, feed_sum, query_back, visual_final, query_final, *window_dz, *gain_rows
+    )
+    window_dz, gain_rows = rest[:shards], rest[shards:]
+    if pages == GROUPS:
         feed_sum = lax.all_gather(feed_sum, "page", axis=0, tiled=True)
-    window_dz = [first_dz] + list(window_dz[1:])
+    mixed_terms = line_terms(mixed_pair)
+
+    out_rows = window_rows_out
     dpacked, dnorm_win, bias_grad, grad_window_out = kernel_call(
         functools.partial(window_backward_kernel, *static),
         (stripes,),
@@ -1291,69 +1499,73 @@
         name="window_backward",
         us=27,
     )
-    win_terms, win_second = scatter_pieces(dnorm_win[: tokens // 2], dnorm_win[tokens // 2 :])
+    dpacked, dnorm_win, bias_grad, grad_window_out, *mixed_terms = fence(
+        dpacked, dnorm_win, bias_grad, grad_window_out, *mixed_terms
+    )
+    mixed_entry = line_entry(mixed_terms)
     grad_qkv_w = left_tmul(norm_win, dpacked)
-    qkv_halves = halves_here(grad_qkv_w)
-    mixed_share, outs_share = scattered(mixed_pair, outs_pair)
-    mixed_share, outs_share = tie(dpacked, mixed_share, outs_share)
-    mixed_t, outs_t = gathered(mixed_share, outs_share, mixed_halves, outs_halves)
-    wout_halves = rows_halves(grad_window_out)
-    qkv_share, wout_share = scattered(pair_total(*qkv_halves), pair_total(*wout_halves))
-    qkv_t, wout_t = gathered(qkv_share, wout_share, qkv_halves, wout_halves)
-    (visual_back,) = back_through_norm(0, vis_low, win_terms, grad_mid, [bf16])
-    visual_final = late + (
-        final_terms[0][:own].astype(f32) + final_terms[1][:own].astype(f32) + final_terms[2].astype(f32)
-    )
-
-    grouped = feed_grads.reshape(2, GROUPS // 2, -1, model)[:, :, : shards * up_share]
-    up_grads = grouped.reshape(2, GROUPS // 2, shards, up_share, model).transpose(0, 2, 1, 3, 4)
-    up_grads = up_grads.reshape(2, shards * up_share * (GROUPS // 2), model)
-
-    def gain_grad(line, *pairs):
-        return sum(jnp.sum(w.astype(f32) * g.astype(f32), axis=1) for w, g in pairs) / gains_all[line]
-
-    gain_grads = jnp.stack(
-        [
-            gain_grad(0, (qkv_w, grad_qkv_w)),
-            gain_grad(1, (vis_w, grad_vis_w)),
-            gain_grad(2, (qry_w, grad_qry_w)),
-            gain_grad(3, (vup_w, up_grads[0])),
-            gain_grad(4, (qup_w, up_grads[1])),
-        ]
-    )
-    (bias_grad,) = tie(qkv_halves[0], bias_grad)
-    small = jnp.concatenate(
-        [tiny_sum(gain_grads, ("win",)).reshape(-1), bias_gather(bias_grad, heads).reshape(-1)]
-    )
-    small = tiny_sum(small, ("page",))
-    gain_total = lax.dynamic_slice_in_dim(small[: 5 * model].reshape(5, model), me * rows, rows, 1)
-    bias_total = small[5 * model :].reshape(heads, SPAN * SPAN)
-
+    qkv_halves = halves_here((grad_qkv_w,), grad_window_out)
+    qkv_keep, qkv_give, dnorm_win, bias_grad, grad_qkv_w, mixed_entry = fence(
+        *qkv_halves, dnorm_win, bias_grad, grad_qkv_w, mixed_entry
+    )
+    qkv_halves = (qkv_keep, qkv_give)
+    qkv_beside = beside(qkv_give)
+    if direct:
+        mixed_all = lax.all_gather(mixed_entry, "page", axis=0, tiled=True)
+    else:
+        mixed_here, mixed_other = page_gather(mixed_entry, mixed_halves[1])
+
+    (win_own, win_near, win_last), win_second = scatter_pieces(dnorm_win[: tokens // 2], dnorm_win[tokens // 2 :])
+    bias_part = bias_gather(bias_grad, heads)
+    qkv_beside, win_second, bias_part, grad_qkv_w = fence(qkv_beside, win_second, bias_part, grad_qkv_w)
+    qkv_terms = line_terms(qkv_keep if pages == 1 else add_low(qkv_keep, qkv_beside))
+    small = tiny_sum(jnp.stack([gain_sum(0, qkv_w, grad_qkv_w)] + gain_rows), ("win",))
+    small = jnp.concatenate([small.reshape(-1), bias_part.reshape(-1)])
+    win_last, small, *qkv_terms = fence(win_last, small, *qkv_terms)
+    qkv_entry = line_entry(qkv_terms)
+    (visual_back,) = back_through_norm(0, vis_low, (win_own, win_near, win_last), grad_mid, [bf16])
+    page_bits = [k for k in reversed(bits_of(pages))]
+    for bit in page_bits[:1]:
+        small = small + swap(small, "page", bit)
+    qkv_entry, small, visual_back = fence(qkv_entry, small, visual_back)
+    feed_rows = to_sources(tie(dpacked, feed_sum)[0])
     out_vup, out_vdown, out_qup, out_qdown = [
         full_out(shape, f32) for shape in ((rows, shards * hidden), (hidden, model)) * 2
     ]
-    (feed_sum,) = tie(dpacked, feed_sum)
     out_vup, out_qup, out_vdown, out_qdown = kernel_call(
         functools.partial(lay_out_feed_kernel, shards),
         (1,),
-        all_of(feed_sum),
+        all_of(*feed_rows),
         [out_vup, out_qup, out_vdown, out_qdown],
-        (feed_sum,),
+        feed_rows,
         place=where_me,
         name="lay_out_feed",
         us=6,
     )
-    (out_qkv,) = laid_out(qkv_t, [3], part)
-    out_akv, out_cq, out_aq, out_ckv = laid_out(mixed_t, [2, 1, 1, 2], part)
+    qkv_here = line_here(qkv_entry)
+    for bit in page_bits[1:]:
+        small = small + swap(small, "page", bit)
+    out_vup, out_qup, out_vdown, out_qdown, qkv_here = fence(out_vup, out_qup, out_vdown, out_qdown, qkv_here)
+    qkv_here, qkv_other = page_gather(qkv_here, qkv_halves[1])
+    gain_total = lax.dynamic_slice_in_dim(small[: 5 * model].reshape(5, model), me * rows, rows, 1)
+    bias_total = small[5 * model :].reshape(heads, SPAN * SPAN)
+
+    out_qkv, out_wout = laid_out(qkv_here, qkv_other, [3], part, rows)
+    mixed_pieces = [2, 1, 1, 2]
+    if direct:
+        mixed_outs = laid_out_pages(mixed_all, mixed_pieces, part, 2 * rows)
+    else:
+        mixed_outs = laid_out(mixed_here, mixed_other, mixed_pieces, part, 2 * rows)
+    out_akv, out_cq, out_aq, out_ckv, outs_t = mixed_outs
 
     return (
-        visual_final.reshape(1, row_count, page_width, model).astype(bf16),
-        query_final.reshape(1, slots_count, model).astype(bf16),
+        visual_final.reshape(1, row_count, page_width, model),
+        query_final.reshape(1, slots_count, model),
         visual_back.reshape(1, row_count, page_width, model),
         query_back.reshape(1, slots_count, model),
         gain_total[0],
         out_qkv,
-        wout_t,
+        out_wout,
         bias_total,
         gain_total[1],
         gain_total[2],

time: 588 us -> 514 us (0.87)
  starting transfers between devices: 103 us -> 74.2 us
  waiting for transfers between devices: 177 us -> 150 us
  local copies, waits for them, and re-layouts: 84.3 us -> 60.3 us
  Pallas kernels: 150 us -> 166 us
  other arithmetic: 32.5 us -> 24.8 us
    ppermute x55, waiting for transfers between devices: 145 us -> 81.2 us  [swap(): return lax.ppermute(tensor, axis, [(i, i ^ bit) for i in range(count)])]
    ppermute x24 -> x9, waiting for transfers between devices: 14.6 us -> 33 us  [line_swap(): return lax.ppermute(tensor, 'page', pairs)]
    unnamed x260 -> x304, local copies, waits for them, and re-layouts: 44.3 us -> 26.5 us
    pallas_call x21 -> x23, Pallas kernels: 150 us -> 166 us  [kernel_call(): pl.pallas_call(function, grid_spec=pltpu.PrefetchScalarGridSpec(num_scala...]
    ppermute x24 -> x9, starting transfers between devices: 47 us -> 35.9 us  [line_swap(): return lax.ppermute(tensor, 'page', pairs)]
    ppermute x10 -> x5, starting transfers between devices: 15.8 us -> 5.7 us  [the longest x3 4.01 us: beside(): lax.ppermute(tensor, 'page', [(i, i ^ 1) for i in range(pages)])]
    all_gather x1 -> x2, waiting for transfers between devices: 0.01 us -> 9.06 us  [the longest x1 9.06 us: body(): mixed_all = lax.all_gather(mixed_entry, 'page', axis=0, tiled=True)]
    ppermute x10 -> x5, waiting for transfers between devices: 17.7 us -> 26.6 us  [the longest x3 26.6 us: beside(): lax.ppermute(tensor, 'page', [(i, i ^ 1) for i in range(pages)])]
  transfers between devices with their start and end apart: 92 -> 73, of which waited for: 37 -> 29; matrix products, arithmetic and copies ran while one was open for 16% -> 14% of each run, Pallas kernels for 20% -> 32%
where the time goes in v3:
time: 514 us; the launch traced here: 505 us
  Pallas kernels  166 us (32%)
  waiting for transfers between devices  150 us (29%)
  starting transfers between devices  74.2 us (14%)
  local copies, waits for them, and re-layouts  60.3 us (12%)
  other arithmetic  24.8 us (5%)
  between operations  16.8 us (3%)
  matrix products  13.4 us (3%)
    pallas_call x23, Pallas kernels, kernel_call(): pl.pallas_call(function, grid_spec=pltpu.PrefetchScalarGridSpec(num_scala...  166 us
    ppermute x55, waiting for transfers between devices, swap(): return lax.ppermute(tensor, axis, [(i, i ^ bit) for i in range(count)])  81.2 us
    ppermute x9, starting transfers between devices, line_swap(): return lax.ppermute(tensor, 'page', pairs)  35.9 us
    ppermute x9, waiting for transfers between devices, line_swap(): return lax.ppermute(tensor, 'page', pairs)  33 us
    ppermute x55, starting transfers between devices, swap(): return lax.ppermute(tensor, axis, [(i, i ^ bit) for i in range(count)])  32.2 us
    ppermute x3, waiting for transfers between devices, beside(): lax.ppermute(tensor, 'page', [(i, i ^ 1) for i in range(pages)])  26.6 us
    unnamed x304, local copies, waits for them, and re-layouts  26.5 us
  transfers between devices with their start and end apart: 73, of which 29 were waited for; matrix products, arithmetic and copies ran while one was open for 14% of the time, Pallas kernels for 32%

profile of v3, /device:TPU:0, one launch (start us, length us, event | category | flops | bytes accessed | tf_op | source)
XLA Modules:
  0.0 505.1 jit_solution(31236208472217659)
XLA Ops:
  13.3 3.0 collective-permute-start.4
  29.9 16.4 %collective-permute-done.2 = bf16[80,768]{1,0:T(8,128)(2,1)S(1)} collective-permute-done((bf16[80,768]{1,0:T(8,128)(2,1)}, bf16[80,768]{1,0:T(8,128)(2,1)S(1)}, u32[]{:S(2)}, u32[]{:S(2)}) %collective-permute-start.2) | collective-permute-done | bytes 122912 | tf_op jit(solution)/shard_map/ppermute | solution.py:25
  51.7 3.7 collective-permute-done.7.third
  58.7 20.8 %window_forward.1 = (bf16[1728,768]{1,0:T(8,128)(2,1)}, bf16[768,768]{1,0:T(8,128)(2,1)}, f32[16,768]{1,0:T(8,128)S(1)}, bf16[1728,768]{1,0:T(8,128)(2,1)}, bf16...) custom-call(s32[5]{0:T(128)S(1)} %pad_add_fusion.3.place, bf16[720,768]{1,0:T(8,128)(2,1)S(1)} %copy-done.55, ...), custom_call_target="tpu_custom_call" | custom-call | flops 17000000 | bytes 1000 | tf_op jit(solution)/shard_map/window_forward/pallas_call | solution.py:866
  92.7 5.6 %collective-permute-done.12.second = bf16[1344,256]{1,0:T(8,128)(2,1)} collective-permute-done((bf16[1344,256]{1,0:T(8,128)(2,1)}, bf16[1344,256]{1,0:T(8,128)(2,1)}, u32[]{:S(2)}, u32[]{:S(2)}) %collective-permute-start.12) | collective-permute-done | bytes 688160 | tf_op jit(solution)/shard_map/ppermute | solution.py:25
  100.7 14.5 %middle.1 = (f32[1728,768]{1,0:T(8,128)}, bf16[1728,768]{1,0:T(8,128)(2,1)}, bf16[1728,768]{1,0:T(8,128)(2,1)}, bf16[1344,256]{1,0:T(8,128)(2,1)}) custom-call(bf16[1728,768]{1,0:T(8,128)(2,1)} %get-tuple-element.279.visual.tensor, bf16[1344,256]{1,0:T(8,128)(2,1)} %get-tuple-element.280.own.mixed, bf16[1344,256]{1,0:T(8,128)(2,1)} %collective-permute-done.12.second, ...), custom_call_target="tpu_custom_call" | custom-call | flops 13000000 | bytes 1000 | tf_op jit(solution)/shard_map/middle/pallas_call | solution.py:866
  119.5 3.5 query_forward.1.own
  127.6 8.3 %collective-permute-done.16.second = bf16[256,192]{1,0:T(8,128)(2,1)} collective-permute-done((bf16[256,192]{1,0:T(8,128)(2,1)S(1)}, bf16[256,192]{1,0:T(8,128)(2,1)}, u32[]{:S(2)}, u32[]{:S(2)}) %collective-permute-start.16) | collective-permute-done | bytes 98336 | tf_op jit(solution)/shard_map/ppermute | solution.py:25
  138.4 21.6 %feed.1 = (f32[432,768]{1,0:T(8,128)}, bf16[1728,768]{1,0:T(8,128)(2,1)}, bf16[1728,768]{1,0:T(8,128)(2,1)}, bf16[1728,768]{1,0:T(8,128)(2,1)}, bf16[1728,768]{1...) custom-call(s32[1]{0:T(128)} %bitcast.place, f32[1728,768]{1,0:T(8,128)} %get-tuple-element.301.mid.tensor, ...), custom_call_target="tpu_custom_call" | custom-call | flops 18000000 | bytes 1000 | tf_op jit(solution)/shard_map/feed/pallas_call | solution.py:866
  163.9 3.6 query_feed.1
  171.3 11.6 %feed_grads.1 = bf16[3072,768]{1,0:T(8,128)(2,1)} custom-call(bf16[1728,768]{1,0:T(8,128)(2,1)S(1)} %copy-done.23, bf16[1728,768]{1,0:T(8,128)(2,1)} %get-tuple-element.349.dhidden, bf16[1728,768]{1,0:T(8,128)(2,1)} %get-tuple-element.356.act.left, bf16[1728,768]{1,0:T(8,128)(2,1)} %get-tuple-element.351.top, ...), custom_call_target="tpu_custom_call" | custom-call | flops 10000000 | bytes 1000 | tf_op jit(solution)/shard_map/feed_grads/pallas_call | solution.py:866
  184.2 4.6 visual_final.1
  199.8 3.7 collective-permute-done.30
  203.9 9.7 %query_backward.1 = (bf16[256,256]{1,0:T(8,128)(2,1)S(1)}, bf16[256,256]{1,0:T(8,128)(2,1)S(1)}, bf16[256,256]{1,0:T(8,128)(2,1)S(1)}, bf16[1728,256]{1,0:T(8,12...) custom-call(bf16[256,1280]{1,0:T(8,128)(2,1)S(1)} %convolution_convert_fusion.keys.valu, ...), custom_call_target="tpu_custom_call" | custom-call | flops 8000000 | bytes 1000 | tf_op jit(solution)/shard_map/query_backward/pallas_call | solution.py:866
  218.5 7.5 %collective-permute-done.37 = bf16[256,768]{1,0:T(8,128)(2,1)S(1)} collective-permute-done((bf16[256,768]{1,0:T(8,128)(2,1)S(1)}, bf16[256,768]{1,0:T(8,128)(2,1)S(1)}, u32[]{:S(2)}, u32[]{:S(2)}) %collective-permute-start.37) | collective-permute-done | bytes 393248 | tf_op jit(solution)/shard_map/ppermute | solution.py:25
  227.1 17.0 %cross_backward.1 = (bf16[1728,768]{1,0:T(8,128)(2,1)}, f32[256,256]{1,0:T(8,128)S(1)}, f32[256,256]{1,0:T(8,128)S(1)}, f32[192,768]{1,0:T(8,128)S(1)}, bf16[864...) custom-call(bf16[1728,768]{1,0:T(8,128)(2,1)} %get-tuple-element.300.keys_vis.values_vis.proj, ...), custom_call_target="tpu_custom_call" | custom-call | flops 16000000 | bytes 1000 | tf_op jit(solution)/shard_map/cross_backward/pallas_call | solution.py:866
  265.0 3.2 split_halves.2
  280.8 12.8 %collective-permute-done.41.second = bf16[432,768]{1,0:T(8,128)(2,1)S(1)} collective-permute-done((bf16[432,768]{1,0:T(8,128)(2,1)S(1)}, bf16[432,768]{1,0:T(8,128)(2,1)S(1)}, u32[]{:S(2)}, u32[]{:S(2)}) %collective-permute-start.41) | collective-permute-done | bytes 663584 | tf_op jit(solution)/shard_map/ppermute | solution.py:25
  294.6 8.0 %collective-permute-done.40 = bf16[512,1152]{1,0:T(8,128)(2,1)S(1)} collective-permute-done((bf16[512,1152]{1,0:T(8,128)(2,1)S(1)}, bf16[512,1152]{1,0:T(8,128)(2,1)S(1)}, u32[]{:S(2)}, u32[]{:S(2)}) %collective-permute-start.40) | collective-permute-done | bytes 1179680 | tf_op jit(solution)/shard_map/ppermute | solution.py:1382
  310.0 29.4 %window_backward.1 = (bf16[1728,768]{1,0:T(8,128)(2,1)}, bf16[1728,768]{1,0:T(8,128)(2,1)}, f32[432,144]{1,0:T(8,128)S(1)}, f32[192,768]{1,0:T(8,128)S(1)}) custom-call(s32[5]{0:T(128)S(1)} %copy-done.90, bf16[432,768]{1,0:T(8,128)(2,1)S(1)} %get-tuple-element.414.near, bf16[432,768]{1,0:T(8,128)(2,1)S(1)} %collective-permute-done.41.second, ...), custom_call_target="tpu_custom_call" | custom-call | flops 27000000 | bytes 1000 | tf_op jit(solution)/shard_map/window_backward/pallas_call | solution.py:866
  340.7 4.1 fusion.36.refs_0_
  347.2 3.5 fusion.29
  360.4 18.6 %collective-permute-done.52 = bf16[512,576]{0,1:T(8,128)(2,1)} collective-permute-done((bf16[512,576]{0,1:T(8,128)(2,1)}, bf16[512,576]{0,1:T(8,128)(2,1)}, u32[]{:S(2)}, u32[]{:S(2)}) %collective-permute-start.52) | collective-permute-done | bytes 589856 | tf_op jit(solution)/shard_map/ppermute | solution.py:1382
  383.5 20.0 %collective-permute-start.55 = (bf16[128,576]{1,0:T(8,128)(2,1)}, bf16[128,576]{1,0:T(8,128)(2,1)}, u32[]{:S(2)}, u32[]{:S(2)}) collective-permute-start(bf16[128,576]{1,0:T(8,128)(2,1)} %get-tuple-element.514), channel_id=1, source_target_pairs={{0,8},{4,12},{8,0},{12,4},{16,24},{20,28},{24,16},{28,20},{1,9},{5... | collective-permute-start | bytes 442376 | tf_op jit(solution)/shard_map/ppermute | solution.py:102
  413.0 6.7 %collective-permute-done.55 = bf16[128,576]{1,0:T(8,128)(2,1)} collective-permute-done((bf16[128,576]{1,0:T(8,128)(2,1)}, bf16[128,576]{1,0:T(8,128)(2,1)}, u32[]{:S(2)}, u32[]{:S(2)}) %collective-permute-start.55) | collective-permute-done | bytes 147488 | tf_op jit(solution)/shard_map/ppermute | solution.py:102
  421.3 4.9 collective-permute-done.57
  437.3 6.0 %collective-permute-start.65 = (bf16[128,576]{1,0:T(8,128)(2,1)S(1)}, bf16[128,576]{1,0:T(8,128)(2,1)S(1)}, u32[]{:S(2)}, u32[]{:S(2)}) collective-permute-start(bf16[128,576]{1,0:T(8,128)(2,1)S(1)} %pad_maximum_fusion.5), channel_id=1, source_target_pairs={{0,8},{4,12},{8,0},{12,4},{16,24},{20,28},{24,16},{28,20},{1,9},{5... | collective-permute-start | bytes 442376 | tf_op jit(solution)/shard_map/ppermute | solution.py:102
  443.4 12.9 %collective-permute-done.65 = bf16[128,576]{1,0:T(8,128)(2,1)S(1)} collective-permute-done((bf16[128,576]{1,0:T(8,128)(2,1)S(1)}, bf16[128,576]{1,0:T(8,128)(2,1)S(1)}, u32[]{:S(2)}, u32[]{:S(2)}) %collective-permute-start.65) | collective-permute-done | bytes 147488 | tf_op jit(solution)/shard_map/ppermute | solution.py:102
  457.8 6.6 %collective-permute-done.67 = bf16[128,576]{1,0:T(8,128)(2,1)S(1)} collective-permute-done((bf16[128,576]{1,0:T(8,128)(2,1)S(1)}, bf16[128,576]{1,0:T(8,128)(2,1)S(1)}, u32[]{:S(2)}, u32[]{:S(2)}) %collective-permute-start.67) | collective-permute-done | bytes 147488 | tf_op jit(solution)/shard_map/ppermute | solution.py:102
  464.6 4.0 lay_out_feed.1
  471.2 4.0 collective-permute-done.60
  481.3 9.1 %all-gather.7.cloned.1.call-done.blocks = bf16[1024,1152]{1,0:T(8,128)(2,1)} async-done(((bf16[128,1152]{1,0:T(8,128)(2,1)}), bf16[1024,1152]{1,0:T(8,128)(2,1)}) %all-gather.7.cloned.1.call-update) | async-done | bytes 2359312 | tf_op jit(solution)/shard_map/all_gather | solution.py:1514
  (605 shorter events, 179.4 us)
Async XLA Ops:
  7.2 116.4 %all-gather.9.cloned.1.call-start = ((), (), s32[]{:S(2)}) async-start(), calls=%async_computation.4 | async-start | bytes 4423680 | tf_op jit(solution)/shard_map/all_gather | solution.py:1058
  16.3 31.9 %collective-permute-start = (bf16[720,768]{1,0:T(8,128)(2,1)}, bf16[720,768]{1,0:T(8,128)(2,1)}, u32[]{:S(2)}, u32[]{:S(2)}) collective-permute-start(bf16[720,768]{1,0:T(8,128)(2,1)} %copy-done.54), channel_id=1, source_target_pairs={{0,2},{1,3},{2,0},{3,1},{4,6},{5,7},{6,4},{7,5},{8,10},{9,11},{10,... | collective-permute-start | bytes 3317768 | tf_op jit(solution)/shard_map/ppermute | solution.py:25
  18.3 28.0 %collective-permute-start.2 = (bf16[80,768]{1,0:T(8,128)(2,1)}, bf16[80,768]{1,0:T(8,128)(2,1)S(1)}, u32[]{:S(2)}, u32[]{:S(2)}) collective-permute-start(bf16[80,768]{1,0:T(8,128)(2,1)} %get-tuple-element.256), channel_id=1, source_target_pairs={{0,2},{1,3},{2,0},{3,1},{4,6},{5,7},{6,4},{7,5},{8,10},{9,11},{10,... | collective-permute-start | bytes 368648 | tf_op jit(solution)/shard_map/ppermute | solution.py:25
  24.8 23.4 %collective-permute-start.3 = (bf16[80,768]{1,0:T(8,128)(2,1)S(1)}, bf16[80,768]{1,0:T(8,128)(2,1)S(1)}, u32[]{:S(2)}, u32[]{:S(2)}) collective-permute-start(bf16[80,768]{1,0:T(8,128)(2,1)S(1)} %get-tuple-element.257), channel_id=1, source_target_pairs={{0,3},{1,2},{2,1},{3,0},{4,7},{5,6},{6,5},{7,4},{8,11},{9,10},{10,... | collective-permute-start | bytes 368648 | tf_op jit(solution)/shard_map/ppermute | solution.py:25
  49.0 254.9 %reduce-scatter.2.cloned.1.call-start = ((), (), s32[]{:S(2)}) async-start(), calls=%async_computation.1 | async-start | bytes 5308416 | tf_op jit(solution)/shard_map/reduce_scatter | solution.py:1279
  49.3 30.2 %collective-permute-start.9 = (bf16[768,768]{1,0:T(8,128)(2,1)}, bf16[768,768]{1,0:T(8,128)(2,1)S(1)}, u32[]{:S(2)}, u32[]{:S(2)}) collective-permute-start(bf16[768,768]{1,0:T(8,128)(2,1)} %copy-done.92), channel_id=1, source_target_pairs={{0,2},{1,3},{2,0},{3,1},{4,6},{5,7},{6,4},{7,5},{8,10},{9,11},{10,... | collective-permute-start | bytes 3538952 | tf_op jit(solution)/shard_map/ppermute | solution.py:25
  50.3 29.2 %collective-permute-start.10 = (bf16[576,768]{1,0:T(8,128)(2,1)}, bf16[576,768]{1,0:T(8,128)(2,1)S(1)}, u32[]{:S(2)}, u32[]{:S(2)}) collective-permute-start(bf16[576,768]{1,0:T(8,128)(2,1)} %copy-done.93), channel_id=1, source_target_pairs={{0,1},{1,0},{2,3},{3,2},{4,5},{5,4},{6,7},{7,6},{8,9},{9,8},{10,11... | collective-permute-start | bytes 2654216 | tf_op jit(solution)/shard_map/ppermute | solution.py:25
  117.3 20.4 %collective-permute-start.20 = (bf16[432,768]{1,0:T(8,128)(2,1)S(1)}, bf16[432,768]{1,0:T(8,128)(2,1)}, u32[]{:S(2)}, u32[]{:S(2)}) collective-permute-start(bf16[432,768]{1,0:T(8,128)(2,1)S(1)} %reshape_squeeze.7.top_own.residual), channel_id=1, source_target_pairs={{0,1},{1,0},{2,3},{3,2},{4,5},{5,4},{6,7},{7,6},{8,9},{9,8},{10,11... | collective-permute-start | bytes 1990664 | tf_op jit(solution)/shard_map/ppermute | solution.py:25
  117.3 20.9 %collective-permute-start.18 = (bf16[1344,256]{1,0:T(8,128)(2,1)}, bf16[1344,256]{1,0:T(8,128)(2,1)}, u32[]{:S(2)}, u32[]{:S(2)}) collective-permute-start(bf16[1344,256]{1,0:T(8,128)(2,1)} %get-tuple-element.302.own.mixed), channel_id=1, source_target_pairs={{0,1},{1,0},{2,3},{3,2},{4,5},{5,4},{6,7},{7,6},{8,9},{9,8},{10,11... | collective-permute-start | bytes 2064392 | tf_op jit(solution)/shard_map/ppermute | solution.py:25
  136.0 23.9 %collective-permute-start.22 = (bf16[192,768]{1,0:T(8,128)(2,1)S(1)}, bf16[192,768]{1,0:T(8,128)(2,1)S(1)}, u32[]{:S(2)}, u32[]{:S(2)}) collective-permute-start(bf16[192,768]{1,0:T(8,128)(2,1)S(1)} %copy-done.46), channel_id=1, source_target_pairs={{0,2},{1,3},{2,0},{3,1},{4,6},{5,7},{6,4},{7,5},{8,10},{9,11},{10,... | collective-permute-start | bytes 884744 | tf_op jit(solution)/shard_map/ppermute | solution.py:25
  137.6 22.3 %collective-permute-start.23 = (bf16[256,192]{1,0:T(8,128)(2,1)}, bf16[256,192]{1,0:T(8,128)(2,1)S(1)}, u32[]{:S(2)}, u32[]{:S(2)}) collective-permute-start(bf16[256,192]{1,0:T(8,128)(2,1)} %copy-done.51), channel_id=1, source_target_pairs={{0,1},{1,0},{2,3},{3,2},{4,5},{5,4},{6,7},{7,6},{8,9},{9,8},{10,11... | collective-permute-start | bytes 294920 | tf_op jit(solution)/shard_map/ppermute | solution.py:25
  137.8 22.1 %collective-permute-start.24 = (bf16[256,192]{1,0:T(8,128)(2,1)}, bf16[256,192]{1,0:T(8,128)(2,1)S(1)}, u32[]{:S(2)}, u32[]{:S(2)}) collective-permute-start(bf16[256,192]{1,0:T(8,128)(2,1)} %collective-permute-done.16.second), channel_id=1, source_target_pairs={{0,1},{1,0},{2,3},{3,2},{4,5},{5,4},{6,7},{7,6},{8,9},{9,8},{10,11... | collective-permute-start | bytes 294920 | tf_op jit(solution)/shard_map/ppermute | solution.py:25
  168.9 22.2 %collective-permute-start.29 = (bf16[432,768]{1,0:T(8,128)(2,1)}, bf16[432,768]{1,0:T(8,128)(2,1)}, u32[]{:S(2)}, u32[]{:S(2)}) collective-permute-start(bf16[432,768]{1,0:T(8,128)(2,1)} %add_convert_fusion.4), channel_id=1, source_target_pairs={{0,2},{1,3},{2,0},{3,1},{4,6},{5,7},{6,4},{7,5},{8,10},{9,11},{10,... | collective-permute-start | bytes 1990664 | tf_op jit(solution)/shard_map/ppermute | solution.py:25
  191.2 237.2 %all-gather.5.cloned.1.call-start = ((), (), s32[]{:S(2)}) async-start(), calls=%async_computation.2 | async-start | bytes 5308416 | tf_op jit(solution)/shard_map/all_gather | solution.py:1475
  191.2 23.6 %collective-permute-start.31 = (bf16[864,768]{1,0:T(8,128)(2,1)}, bf16[864,768]{1,0:T(8,128)(2,1)S(1)}, u32[]{:S(2)}, u32[]{:S(2)}) collective-permute-start(bf16[864,768]{1,0:T(8,128)(2,1)} %copy-done.91), channel_id=1, source_target_pairs={{0,1},{1,0},{2,3},{3,2},{4,5},{5,4},{6,7},{7,6},{8,9},{9,8},{10,11... | collective-permute-start | bytes 3981320 | tf_op jit(solution)/shard_map/ppermute | solution.py:25
  203.7 23.4 %collective-permute-start.34 = (bf16[432,768]{1,0:T(8,128)(2,1)S(1)}, bf16[432,768]{1,0:T(8,128)(2,1)S(1)}, u32[]{:S(2)}, u32[]{:S(2)}) collective-permute-start(bf16[432,768]{1,0:T(8,128)(2,1)S(1)} %get-tuple-element.361.near), channel_id=1, source_target_pairs={{0,1},{1,0},{2,3},{3,2},{4,5},{5,4},{6,7},{7,6},{8,9},{9,8},{10,11... | collective-permute-start | bytes 1990664 | tf_op jit(solution)/shard_map/ppermute | solution.py:25
  217.6 28.7 %collective-permute-start.36 = (bf16[432,768]{1,0:T(8,128)(2,1)S(1)}, bf16[432,768]{1,0:T(8,128)(2,1)S(1)}, u32[]{:S(2)}, u32[]{:S(2)}) collective-permute-start(bf16[432,768]{1,0:T(8,128)(2,1)S(1)} %add_convert_fusion.3), channel_id=1, source_target_pairs={{0,2},{1,3},{2,0},{3,1},{4,6},{5,7},{6,4},{7,5},{8,10},{9,11},{10,... | collective-permute-start | bytes 1990664 | tf_op jit(solution)/shard_map/ppermute | solution.py:25
  273.2 20.4 %collective-permute-start.41 = (bf16[432,768]{1,0:T(8,128)(2,1)S(1)}, bf16[432,768]{1,0:T(8,128)(2,1)S(1)}, u32[]{:S(2)}, u32[]{:S(2)}) collective-permute-start(bf16[432,768]{1,0:T(8,128)(2,1)S(1)} %get-tuple-element.414.near), channel_id=1, source_target_pairs={{0,2},{1,3},{2,0},{3,1},{4,6},{5,7},{6,4},{7,5},{8,10},{9,11},{10,... | collective-permute-start | bytes 1990664 | tf_op jit(solution)/shard_map/ppermute | solution.py:25
  274.2 29.7 %collective-permute-start.44 = (bf16[432,768]{1,0:T(8,128)(2,1)S(1)}, bf16[432,768]{1,0:T(8,128)(2,1)S(1)}, u32[]{:S(2)}, u32[]{:S(2)}) collective-permute-start(bf16[432,768]{1,0:T(8,128)(2,1)S(1)} %get-tuple-element.414.near), channel_id=1, source_target_pairs={{0,1},{1,0},{2,3},{3,2},{4,5},{5,4},{6,7},{7,6},{8,9},{9,8},{10,11... | collective-permute-start | bytes 1990664 | tf_op jit(solution)/shard_map/ppermute | solution.py:25
  274.2 28.4 %collective-permute-start.40 = (bf16[512,1152]{1,0:T(8,128)(2,1)S(1)}, bf16[512,1152]{1,0:T(8,128)(2,1)S(1)}, u32[]{:S(2)}, u32[]{:S(2)}) collective-permute-start(bf16[512,1152]{1,0:T(8,128)(2,1)S(1)} %copy-done.137), channel_id=1, source_target_pairs={{0,4},{4,0},{8,12},{12,8},{16,20},{20,16},{24,28},{28,24},{1,5},{5... | collective-permute-start | bytes 3538952 | tf_op jit(solution)/shard_map/ppermute | solution.py:1382
  304.0 186.3 %all-gather.7.cloned.1.call-start = ((), (), s32[]{:S(2)}) async-start(), calls=%async_computation.3 | async-start | bytes 2654208 | tf_op jit(solution)/shard_map/all_gather | solution.py:1514
  305.5 33.9 %collective-permute-start.46 = (bf16[128,1152]{1,0:T(8,128)(2,1)S(1)}, bf16[128,1152]{1,0:T(8,128)(2,1)S(1)}, u32[]{:S(2)}, u32[]{:S(2)}) collective-permute-start(bf16[128,1152]{1,0:T(8,128)(2,1)S(1)} %get-tuple-element.510), channel_id=1, source_target_pairs={{0,8},{4,12},{8,0},{12,4},{16,24},{20,28},{24,16},{28,20},{1,9},{5... | collective-permute-start | bytes 884744 | tf_op jit(solution)/shard_map/ppermute | solution.py:102
  307.1 32.3 %collective-permute-start.47 = (bf16[128,1152]{1,0:T(8,128)(2,1)S(1)}, bf16[128,1152]{1,0:T(8,128)(2,1)S(1)}, u32[]{:S(2)}, u32[]{:S(2)}) collective-permute-start(bf16[128,1152]{1,0:T(8,128)(2,1)S(1)} %get-tuple-element.509), channel_id=1, source_target_pairs={{0,16},{4,20},{8,24},{12,28},{16,0},{20,4},{24,8},{28,12},{1,17},{... | collective-permute-start | bytes 884744 | tf_op jit(solution)/shard_map/ppermute | solution.py:102
  309.8 29.9 %collective-permute-start.48 = (bf16[128,1152]{1,0:T(8,128)(2,1)S(1)}, bf16[128,1152]{1,0:T(8,128)(2,1)S(1)}, u32[]{:S(2)}, u32[]{:S(2)}) collective-permute-start(bf16[128,1152]{1,0:T(8,128)(2,1)S(1)} %get-tuple-element.508), channel_id=1, source_target_pairs={{0,24},{4,28},{8,16},{12,20},{16,8},{20,12},{24,0},{28,4},{1,25},{... | collective-permute-start | bytes 884744 | tf_op jit(solution)/shard_map/ppermute | solution.py:102
  354.3 24.7 %collective-permute-start.52 = (bf16[512,576]{0,1:T(8,128)(2,1)}, bf16[512,576]{0,1:T(8,128)(2,1)}, u32[]{:S(2)}, u32[]{:S(2)}) collective-permute-start(bf16[512,576]{0,1:T(8,128)(2,1)} %copy.116), channel_id=1, source_target_pairs={{0,4},{4,0},{8,12},{12,8},{16,20},{20,16},{24,28},{28,24},{1,5},{5... | collective-permute-start | bytes 1769480 | tf_op jit(solution)/shard_map/ppermute | solution.py:1382
  359.4 66.8 %collective-permute-start.51 = (bf16[432,768]{1,0:T(8,128)(2,1)}, bf16[432,768]{1,0:T(8,128)(2,1)S(1)}, u32[]{:S(2)}, u32[]{:S(2)}) collective-permute-start(bf16[432,768]{1,0:T(8,128)(2,1)} %add_convert_fusion), channel_id=1, source_target_pairs={{0,2},{1,3},{2,0},{3,1},{4,6},{5,7},{6,4},{7,5},{8,10},{9,11},{10,... | collective-permute-start | bytes 1990664 | tf_op jit(solution)/shard_map/ppermute | solution.py:25
  383.5 36.2 %collective-permute-start.55 = (bf16[128,576]{1,0:T(8,128)(2,1)}, bf16[128,576]{1,0:T(8,128)(2,1)}, u32[]{:S(2)}, u32[]{:S(2)}) collective-permute-start(bf16[128,576]{1,0:T(8,128)(2,1)} %get-tuple-element.514), channel_id=1, source_target_pairs={{0,8},{4,12},{8,0},{12,4},{16,24},{20,28},{24,16},{28,20},{1,9},{5... | collective-permute-start | bytes 442376 | tf_op jit(solution)/shard_map/ppermute | solution.py:102
  406.0 20.3 %collective-permute-start.57 = (bf16[128,576]{1,0:T(8,128)(2,1)S(1)}, bf16[128,576]{1,0:T(8,128)(2,1)}, u32[]{:S(2)}, u32[]{:S(2)}) collective-permute-start(bf16[128,576]{1,0:T(8,128)(2,1)S(1)} %get-tuple-element.512), channel_id=1, source_target_pairs={{0,24},{4,28},{8,16},{12,20},{16,8},{20,12},{24,0},{28,4},{1,25},{... | collective-permute-start | bytes 442376 | tf_op jit(solution)/shard_map/ppermute | solution.py:102
  431.4 33.0 %collective-permute-start.62 = (bf16[384,768]{1,0:T(8,128)(2,1)S(1)}, bf16[384,768]{1,0:T(8,128)(2,1)S(1)}, u32[]{:S(2)}, u32[]{:S(2)}) collective-permute-start(bf16[384,768]{1,0:T(8,128)(2,1)S(1)} %get-tuple-element.503), channel_id=1, source_target_pairs={{0,1},{1,0},{2,3},{3,2},{4,5},{5,4},{6,7},{7,6},{8,9},{9,8},{10,11... | collective-permute-start | bytes 1769480 | tf_op jit(solution)/shard_map/ppermute | solution.py:25
  431.5 32.9 %collective-permute-start.63 = (bf16[384,768]{1,0:T(8,128)(2,1)S(1)}, bf16[384,768]{1,0:T(8,128)(2,1)S(1)}, u32[]{:S(2)}, u32[]{:S(2)}) collective-permute-start(bf16[384,768]{1,0:T(8,128)(2,1)S(1)} %get-tuple-element.502), channel_id=1, source_target_pairs={{0,2},{1,3},{2,0},{3,1},{4,6},{5,7},{6,4},{7,5},{8,10},{9,11},{10,... | collective-permute-start | bytes 1769480 | tf_op jit(solution)/shard_map/ppermute | solution.py:25
  432.6 31.8 %collective-permute-start.64 = (bf16[384,768]{1,0:T(8,128)(2,1)S(1)}, bf16[384,768]{1,0:T(8,128)(2,1)S(1)}, u32[]{:S(2)}, u32[]{:S(2)}) collective-permute-start(bf16[384,768]{1,0:T(8,128)(2,1)S(1)} %get-tuple-element.501), channel_id=1, source_target_pairs={{0,3},{1,2},{2,1},{3,0},{4,7},{5,6},{6,5},{7,4},{8,11},{9,10},{10,... | collective-permute-start | bytes 1769480 | tf_op jit(solution)/shard_map/ppermute | solution.py:25
  468.9 26.9 %collective-permute-start.68 = (bf16[512,576]{0,1:T(8,128)(2,1)S(1)}, bf16[512,576]{0,1:T(8,128)(2,1)S(1)}, u32[]{:S(2)}, u32[]{:S(2)}) collective-permute-start(bf16[512,576]{0,1:T(8,128)(2,1)S(1)} %copy.141), channel_id=1, source_target_pairs={{0,4},{4,0},{8,12},{12,8},{16,20},{20,16},{24,28},{28,24},{1,5},{5... | collective-permute-start | bytes 1769480 | tf_op jit(solution)/shard_map/ppermute | solution.py:1382
  (182 other events, 1318.5 us)
Sparse Core Ops, SparseCore 0:
  49.2 70.4 all-gather.8
  191.3 96.0 reduce-scatter.1
  304.1 123.5 all-gather.4
  430.3 59.9 all-gather.6

commit v4 on v3

--- a/solution.py
+++ b/solution.py
@@ -54,6 +54,15 @@
         last = mine.astype(bf16)
         part = mine + swap(last, axis, bit).astype(f32)
     return part, last
+
+
+def total_terms(part, axis="win"):
+    bits = list(reversed(bits_of(lax.axis_size(axis))))
+    for bit in bits[:-1]:
+        mine = lax.reduce_precision(part.astype(f32), 8, 7)
+        part = mine + swap(mine.astype(bf16), axis, bit).astype(f32)
+    mine = lax.reduce_precision(part.astype(f32), 8, 7).astype(bf16)
+    return mine, swap(mine, axis, bits[-1])
 
 
 def tiny_sum(part, axes):
@@ -1307,7 +1316,7 @@
         name="query_backward",
         us=8,
     )
-    query_total, query_last = total_sum(query_final_part)
+    query_last, query_arrived = total_terms(query_final_part)
     (final_own, final_near, final_last), final_second = scatter_pieces(final_keep, final_send)
     dkv, final_second, query_last, cross_far = fence(dkv, final_second, query_last, cross_dz[1])
     cross_dz = [cross_dz[0], cross_far, cross_dz[2], swap(cross_far, "win", 1)]
@@ -1329,8 +1338,8 @@
         name="cross_backward",
         us=16,
     )
-    dproj_vis, dck, dcv, grad_cross_out, vis_keep, vis_send, grad_qmid, dz_attend, final_last, query_total = fence(
-        dproj_vis, dck, dcv, grad_cross_out, vis_keep, vis_send, grad_qmid, dz_attend, final_last, query_total
+    dproj_vis, dck, dcv, grad_cross_out, vis_keep, vis_send, grad_qmid, dz_attend, final_last, query_arrived = fence(
+        dproj_vis, dck, dcv, grad_cross_out, vis_keep, vis_send, grad_qmid, dz_attend, final_last, query_arrived
     )
     vis_terms, vis_second = scatter_pieces(vis_keep, vis_send)
 
@@ -1449,7 +1458,8 @@
     window_dz = gather_four(dz_window)
     mixed_pair = pair_total(*mixed_halves)
 
-    final_last, query_total = tie(dz_window, final_last, query_total)
+    final_last, query_arrived = tie(dz_window, final_last, query_arrived)
+    query_total = query_last.astype(f32) + query_arrived.astype(f32)
     visual_final = late + (
         final_own[:own].astype(f32) + final_near[:own].astype(f32) + final_last.astype(f32)
     )
@@ -1553,7 +1563,7 @@
     out_qkv, out_wout = laid_out(qkv_here, qkv_other, [3], part, rows)
     mixed_pieces = [2, 1, 1, 2]
     if direct:
-        mixed_outs = laid_out_pages(mixed_all, mixed_pieces, part, 2 * rows)
+        mixed_outs = laid_out_pages(tie(out_wout, mixed_all)[0], mixed_pieces, part, 2 * rows)
     else:
         mixed_outs = laid_out(mixed_here, mixed_other, mixed_pieces, part, 2 * rows)
     out_akv, out_cq, out_aq, out_ckv, outs_t = mixed_outs

time: 514 us -> 509 us (level)
    all_gather x1, waiting for transfers between devices: 9.06 us -> 0.01 us  [body(): mixed_all = lax.all_gather(mixed_entry, 'page', axis=0, tiled=True)]
    ppermute x3, waiting for transfers between devices: 26.6 us -> 34.8 us  [beside(): lax.ppermute(tensor, 'page', [(i, i ^ 1) for i in range(pages)])]
    unnamed x304 -> x310, local copies, waits for them, and re-layouts: 26.5 us -> 28.2 us
  transfers between devices with their start and end apart: 73 -> 73, of which waited for: 29 -> 30; matrix products, arithmetic and copies ran while one was open for 14% -> 14% of each run, Pallas kernels for 32% -> 32%
where the time goes in v4:
time: 509 us; the launch traced here: 500 us
  Pallas kernels  165 us (32%)
  waiting for transfers between devices  145 us (28%)
  starting transfers between devices  73.9 us (15%)
  local copies, waits for them, and re-layouts  62 us (12%)
  other arithmetic  23.8 us (5%)
  between operations  16.8 us (3%)
  matrix products  13.4 us (3%)
    pallas_call x23, Pallas kernels, kernel_call(): pl.pallas_call(function, grid_spec=pltpu.PrefetchScalarGridSpec(num_scala...  165 us
    ppermute x55, waiting for transfers between devices, swap(): return lax.ppermute(tensor, axis, [(i, i ^ bit) for i in range(count)])  76.8 us
    ppermute x9, starting transfers between devices, line_swap(): return lax.ppermute(tensor, 'page', pairs)  35.1 us
    ppermute x3, waiting for transfers between devices, beside(): lax.ppermute(tensor, 'page', [(i, i ^ 1) for i in range(pages)])  34.8 us
    ppermute x9, waiting for transfers between devices, line_swap(): return lax.ppermute(tensor, 'page', pairs)  33.4 us
    ppermute x55, starting transfers between devices, swap(): return lax.ppermute(tensor, axis, [(i, i ^ bit) for i in range(count)])  32.4 us
    unnamed x310, local copies, waits for them, and re-layouts  28.2 us
  transfers between devices with their start and end apart: 73, of which 30 were waited for; matrix products, arithmetic and copies ran while one was open for 14% of the time, Pallas kernels for 32%

profile of v4, /device:TPU:0, one launch (start us, length us, event | category | flops | bytes accessed | tf_op | source)
XLA Modules:
  0.0 500.4 jit_solution(7778373572726860469)
XLA Ops:
  13.3 3.0 collective-permute-start.4
  29.9 16.4 %collective-permute-done.2 = bf16[80,768]{1,0:T(8,128)(2,1)S(1)} collective-permute-done((bf16[80,768]{1,0:T(8,128)(2,1)}, bf16[80,768]{1,0:T(8,128)(2,1)S(1)}, u32[]{:S(2)}, u32[]{:S(2)}) %collective-permute-start.2) | collective-permute-done | bytes 122912 | tf_op jit(solution)/shard_map/ppermute | solution.py:25
  51.7 3.7 collective-permute-done.7.third
  58.7 20.8 %window_forward.1 = (bf16[1728,768]{1,0:T(8,128)(2,1)}, bf16[768,768]{1,0:T(8,128)(2,1)}, f32[16,768]{1,0:T(8,128)S(1)}, bf16[1728,768]{1,0:T(8,128)(2,1)}, bf16...) custom-call(s32[5]{0:T(128)S(1)} %pad_add_fusion.3.place, bf16[720,768]{1,0:T(8,128)(2,1)S(1)} %copy-done.55, ...), custom_call_target="tpu_custom_call" | custom-call | flops 17000000 | bytes 1000 | tf_op jit(solution)/shard_map/window_forward/pallas_call | solution.py:875
  92.7 5.6 %collective-permute-done.12.second = bf16[1344,256]{1,0:T(8,128)(2,1)} collective-permute-done((bf16[1344,256]{1,0:T(8,128)(2,1)}, bf16[1344,256]{1,0:T(8,128)(2,1)}, u32[]{:S(2)}, u32[]{:S(2)}) %collective-permute-start.12) | collective-permute-done | bytes 688160 | tf_op jit(solution)/shard_map/ppermute | solution.py:25
  100.7 14.5 %middle.1 = (f32[1728,768]{1,0:T(8,128)}, bf16[1728,768]{1,0:T(8,128)(2,1)}, bf16[1728,768]{1,0:T(8,128)(2,1)}, bf16[1344,256]{1,0:T(8,128)(2,1)}) custom-call(bf16[1728,768]{1,0:T(8,128)(2,1)} %get-tuple-element.281.visual.tensor, bf16[1344,256]{1,0:T(8,128)(2,1)} %get-tuple-element.282.own.mixed, bf16[1344,256]{1,0:T(8,128)(2,1)} %collective-permute-done.12.second, ...), custom_call_target="tpu_custom_call" | custom-call | flops 13000000 | bytes 1000 | tf_op jit(solution)/shard_map/middle/pallas_call | solution.py:875
  119.5 3.5 query_forward.1.own
  127.6 8.3 %collective-permute-done.16.second = bf16[256,192]{1,0:T(8,128)(2,1)} collective-permute-done((bf16[256,192]{1,0:T(8,128)(2,1)S(1)}, bf16[256,192]{1,0:T(8,128)(2,1)}, u32[]{:S(2)}, u32[]{:S(2)}) %collective-permute-start.16) | collective-permute-done | bytes 98336 | tf_op jit(solution)/shard_map/ppermute | solution.py:25
  138.4 21.6 %feed.1 = (f32[432,768]{1,0:T(8,128)}, bf16[1728,768]{1,0:T(8,128)(2,1)}, bf16[1728,768]{1,0:T(8,128)(2,1)}, bf16[1728,768]{1,0:T(8,128)(2,1)}, bf16[1728,768]{1...) custom-call(s32[1]{0:T(128)} %bitcast.place, f32[1728,768]{1,0:T(8,128)} %get-tuple-element.303.mid.tensor, ...), custom_call_target="tpu_custom_call" | custom-call | flops 18000000 | bytes 1000 | tf_op jit(solution)/shard_map/feed/pallas_call | solution.py:875
  163.9 3.6 query_feed.1
  171.3 11.6 %feed_grads.1 = bf16[3072,768]{1,0:T(8,128)(2,1)} custom-call(bf16[1728,768]{1,0:T(8,128)(2,1)S(1)} %copy-done.23, bf16[1728,768]{1,0:T(8,128)(2,1)} %get-tuple-element.351.dhidden, bf16[1728,768]{1,0:T(8,128)(2,1)} %get-tuple-element.358.act.left, bf16[1728,768]{1,0:T(8,128)(2,1)} %get-tuple-element.353.top, ...), custom_call_target="tpu_custom_call" | custom-call | flops 10000000 | bytes 1000 | tf_op jit(solution)/shard_map/feed_grads/pallas_call | solution.py:875
  184.2 4.6 visual_final.1
  199.8 3.7 collective-permute-done.30
  203.9 9.7 %query_backward.1 = (bf16[256,256]{1,0:T(8,128)(2,1)S(1)}, bf16[256,256]{1,0:T(8,128)(2,1)S(1)}, bf16[256,256]{1,0:T(8,128)(2,1)S(1)}, bf16[1728,256]{1,0:T(8,12...) custom-call(bf16[256,1280]{1,0:T(8,128)(2,1)S(1)} %convolution_convert_fusion.keys.valu, ...), custom_call_target="tpu_custom_call" | custom-call | flops 8000000 | bytes 1000 | tf_op jit(solution)/shard_map/query_backward/pallas_call | solution.py:875
  219.4 17.0 %cross_backward.1 = (bf16[1728,768]{1,0:T(8,128)(2,1)}, f32[256,256]{1,0:T(8,128)S(1)}, f32[256,256]{1,0:T(8,128)S(1)}, f32[192,768]{1,0:T(8,128)S(1)}, bf16[864...) custom-call(bf16[1728,768]{1,0:T(8,128)(2,1)} %get-tuple-element.302.keys_vis.values_vis.proj, ...), custom_call_target="tpu_custom_call" | custom-call | flops 16000000 | bytes 1000 | tf_op jit(solution)/shard_map/cross_backward/pallas_call | solution.py:875
  238.6 4.4 collective-permute-done.37
  261.7 3.2 split_halves.2
  277.6 12.9 %collective-permute-done.41.second = bf16[432,768]{1,0:T(8,128)(2,1)S(1)} collective-permute-done((bf16[432,768]{1,0:T(8,128)(2,1)S(1)}, bf16[432,768]{1,0:T(8,128)(2,1)S(1)}, u32[]{:S(2)}, u32[]{:S(2)}) %collective-permute-start.41) | collective-permute-done | bytes 663584 | tf_op jit(solution)/shard_map/ppermute | solution.py:25
  291.5 8.0 %collective-permute-done.40 = bf16[512,1152]{1,0:T(8,128)(2,1)S(1)} collective-permute-done((bf16[512,1152]{1,0:T(8,128)(2,1)S(1)}, bf16[512,1152]{1,0:T(8,128)(2,1)S(1)}, u32[]{:S(2)}, u32[]{:S(2)}) %collective-permute-start.40) | collective-permute-done | bytes 1179680 | tf_op jit(solution)/shard_map/ppermute | solution.py:1391
  306.9 29.3 %window_backward.1 = (bf16[1728,768]{1,0:T(8,128)(2,1)}, bf16[1728,768]{1,0:T(8,128)(2,1)}, f32[432,144]{1,0:T(8,128)S(1)}, f32[192,768]{1,0:T(8,128)S(1)}) custom-call(s32[5]{0:T(128)S(1)} %copy-done.90, bf16[432,768]{1,0:T(8,128)(2,1)S(1)} %get-tuple-element.417.near, bf16[432,768]{1,0:T(8,128)(2,1)S(1)} %collective-permute-done.41.second, ...), custom_call_target="tpu_custom_call" | custom-call | flops 27000000 | bytes 1000 | tf_op jit(solution)/shard_map/window_backward/pallas_call | solution.py:875
  337.9 4.1 fusion.35.refs_0_
  344.5 3.5 fusion.28
  357.2 19.5 %collective-permute-done.52 = bf16[512,576]{0,1:T(8,128)(2,1)} collective-permute-done((bf16[512,576]{0,1:T(8,128)(2,1)}, bf16[512,576]{0,1:T(8,128)(2,1)}, u32[]{:S(2)}, u32[]{:S(2)}) %collective-permute-start.52) | collective-permute-done | bytes 589856 | tf_op jit(solution)/shard_map/ppermute | solution.py:1391
  381.2 19.2 %collective-permute-start.55 = (bf16[128,576]{1,0:T(8,128)(2,1)}, bf16[128,576]{1,0:T(8,128)(2,1)}, u32[]{:S(2)}, u32[]{:S(2)}) collective-permute-start(bf16[128,576]{1,0:T(8,128)(2,1)} %get-tuple-element.518), channel_id=1, source_target_pairs={{0,8},{4,12},{8,0},{12,4},{16,24},{20,28},{24,16},{28,20},{1,9},{5... | collective-permute-start | bytes 442376 | tf_op jit(solution)/shard_map/ppermute | solution.py:111
  409.7 6.8 %collective-permute-done.55 = bf16[128,576]{1,0:T(8,128)(2,1)} collective-permute-done((bf16[128,576]{1,0:T(8,128)(2,1)}, bf16[128,576]{1,0:T(8,128)(2,1)}, u32[]{:S(2)}, u32[]{:S(2)}) %collective-permute-start.55) | collective-permute-done | bytes 147488 | tf_op jit(solution)/shard_map/ppermute | solution.py:111
  418.3 4.7 collective-permute-done.57
  434.2 5.9 %collective-permute-start.65 = (bf16[128,576]{1,0:T(8,128)(2,1)S(1)}, bf16[128,576]{1,0:T(8,128)(2,1)S(1)}, u32[]{:S(2)}, u32[]{:S(2)}) collective-permute-start(bf16[128,576]{1,0:T(8,128)(2,1)S(1)} %pad_maximum_fusion.5), channel_id=1, source_target_pairs={{0,8},{4,12},{8,0},{12,4},{16,24},{20,28},{24,16},{28,20},{1,9},{5... | collective-permute-start | bytes 442376 | tf_op jit(solution)/shard_map/ppermute | solution.py:111
  440.2 12.9 %collective-permute-done.65 = bf16[128,576]{1,0:T(8,128)(2,1)S(1)} collective-permute-done((bf16[128,576]{1,0:T(8,128)(2,1)S(1)}, bf16[128,576]{1,0:T(8,128)(2,1)S(1)}, u32[]{:S(2)}, u32[]{:S(2)}) %collective-permute-start.65) | collective-permute-done | bytes 147488 | tf_op jit(solution)/shard_map/ppermute | solution.py:111
  454.8 6.5 %collective-permute-done.67 = bf16[128,576]{1,0:T(8,128)(2,1)S(1)} collective-permute-done((bf16[128,576]{1,0:T(8,128)(2,1)S(1)}, bf16[128,576]{1,0:T(8,128)(2,1)S(1)}, u32[]{:S(2)}, u32[]{:S(2)}) %collective-permute-start.67) | collective-permute-done | bytes 147488 | tf_op jit(solution)/shard_map/ppermute | solution.py:111
  461.6 4.0 lay_out_feed.1
  468.6 3.5 collective-permute-done.60
  478.4 7.4 %collective-permute-done.68 = bf16[512,576]{0,1:T(8,128)(2,1)S(1)} collective-permute-done((bf16[512,576]{0,1:T(8,128)(2,1)S(1)}, bf16[512,576]{0,1:T(8,128)(2,1)S(1)}, u32[]{:S(2)}, u32[]{:S(2)}) %collective-permute-start.68) | collective-permute-done | bytes 589856 | tf_op jit(solution)/shard_map/ppermute | solution.py:1391
  (610 shorter events, 180.3 us)
Async XLA Ops:
  7.2 116.4 %all-gather.9.cloned.1.call-start = ((), (), s32[]{:S(2)}) async-start(), calls=%async_computation.4 | async-start | bytes 4423680 | tf_op jit(solution)/shard_map/all_gather | solution.py:1067
  16.3 31.9 %collective-permute-start = (bf16[720,768]{1,0:T(8,128)(2,1)}, bf16[720,768]{1,0:T(8,128)(2,1)}, u32[]{:S(2)}, u32[]{:S(2)}) collective-permute-start(bf16[720,768]{1,0:T(8,128)(2,1)} %copy-done.54), channel_id=1, source_target_pairs={{0,2},{1,3},{2,0},{3,1},{4,6},{5,7},{6,4},{7,5},{8,10},{9,11},{10,... | collective-permute-start | bytes 3317768 | tf_op jit(solution)/shard_map/ppermute | solution.py:25
  18.3 28.0 %collective-permute-start.2 = (bf16[80,768]{1,0:T(8,128)(2,1)}, bf16[80,768]{1,0:T(8,128)(2,1)S(1)}, u32[]{:S(2)}, u32[]{:S(2)}) collective-permute-start(bf16[80,768]{1,0:T(8,128)(2,1)} %get-tuple-element.258), channel_id=1, source_target_pairs={{0,2},{1,3},{2,0},{3,1},{4,6},{5,7},{6,4},{7,5},{8,10},{9,11},{10,... | collective-permute-start | bytes 368648 | tf_op jit(solution)/shard_map/ppermute | solution.py:25
  24.8 23.4 %collective-permute-start.3 = (bf16[80,768]{1,0:T(8,128)(2,1)S(1)}, bf16[80,768]{1,0:T(8,128)(2,1)S(1)}, u32[]{:S(2)}, u32[]{:S(2)}) collective-permute-start(bf16[80,768]{1,0:T(8,128)(2,1)S(1)} %get-tuple-element.259), channel_id=1, source_target_pairs={{0,3},{1,2},{2,1},{3,0},{4,7},{5,6},{6,5},{7,4},{8,11},{9,10},{10,... | collective-permute-start | bytes 368648 | tf_op jit(solution)/shard_map/ppermute | solution.py:25
  49.0 251.7 %reduce-scatter.2.cloned.1.call-start = ((), (), s32[]{:S(2)}) async-start(), calls=%async_computation.1 | async-start | bytes 5308416 | tf_op jit(solution)/shard_map/reduce_scatter | solution.py:1288
  49.3 30.2 %collective-permute-start.9 = (bf16[768,768]{1,0:T(8,128)(2,1)}, bf16[768,768]{1,0:T(8,128)(2,1)S(1)}, u32[]{:S(2)}, u32[]{:S(2)}) collective-permute-start(bf16[768,768]{1,0:T(8,128)(2,1)} %copy-done.92), channel_id=1, source_target_pairs={{0,2},{1,3},{2,0},{3,1},{4,6},{5,7},{6,4},{7,5},{8,10},{9,11},{10,... | collective-permute-start | bytes 3538952 | tf_op jit(solution)/shard_map/ppermute | solution.py:25
  50.3 29.2 %collective-permute-start.10 = (bf16[576,768]{1,0:T(8,128)(2,1)}, bf16[576,768]{1,0:T(8,128)(2,1)S(1)}, u32[]{:S(2)}, u32[]{:S(2)}) collective-permute-start(bf16[576,768]{1,0:T(8,128)(2,1)} %copy-done.93), channel_id=1, source_target_pairs={{0,1},{1,0},{2,3},{3,2},{4,5},{5,4},{6,7},{7,6},{8,9},{9,8},{10,11... | collective-permute-start | bytes 2654216 | tf_op jit(solution)/shard_map/ppermute | solution.py:25
  117.3 20.4 %collective-permute-start.20 = (bf16[432,768]{1,0:T(8,128)(2,1)S(1)}, bf16[432,768]{1,0:T(8,128)(2,1)}, u32[]{:S(2)}, u32[]{:S(2)}) collective-permute-start(bf16[432,768]{1,0:T(8,128)(2,1)S(1)} %reshape_squeeze.7.top_own.residual), channel_id=1, source_target_pairs={{0,1},{1,0},{2,3},{3,2},{4,5},{5,4},{6,7},{7,6},{8,9},{9,8},{10,11... | collective-permute-start | bytes 1990664 | tf_op jit(solution)/shard_map/ppermute | solution.py:25
  117.3 20.9 %collective-permute-start.18 = (bf16[1344,256]{1,0:T(8,128)(2,1)}, bf16[1344,256]{1,0:T(8,128)(2,1)}, u32[]{:S(2)}, u32[]{:S(2)}) collective-permute-start(bf16[1344,256]{1,0:T(8,128)(2,1)} %get-tuple-element.304.own.mixed), channel_id=1, source_target_pairs={{0,1},{1,0},{2,3},{3,2},{4,5},{5,4},{6,7},{7,6},{8,9},{9,8},{10,11... | collective-permute-start | bytes 2064392 | tf_op jit(solution)/shard_map/ppermute | solution.py:25
  136.0 23.9 %collective-permute-start.22 = (bf16[192,768]{1,0:T(8,128)(2,1)S(1)}, bf16[192,768]{1,0:T(8,128)(2,1)S(1)}, u32[]{:S(2)}, u32[]{:S(2)}) collective-permute-start(bf16[192,768]{1,0:T(8,128)(2,1)S(1)} %copy-done.46), channel_id=1, source_target_pairs={{0,2},{1,3},{2,0},{3,1},{4,6},{5,7},{6,4},{7,5},{8,10},{9,11},{10,... | collective-permute-start | bytes 884744 | tf_op jit(solution)/shard_map/ppermute | solution.py:25
  137.6 22.3 %collective-permute-start.23 = (bf16[256,192]{1,0:T(8,128)(2,1)}, bf16[256,192]{1,0:T(8,128)(2,1)S(1)}, u32[]{:S(2)}, u32[]{:S(2)}) collective-permute-start(bf16[256,192]{1,0:T(8,128)(2,1)} %copy-done.51), channel_id=1, source_target_pairs={{0,1},{1,0},{2,3},{3,2},{4,5},{5,4},{6,7},{7,6},{8,9},{9,8},{10,11... | collective-permute-start | bytes 294920 | tf_op jit(solution)/shard_map/ppermute | solution.py:25
  137.8 22.1 %collective-permute-start.24 = (bf16[256,192]{1,0:T(8,128)(2,1)}, bf16[256,192]{1,0:T(8,128)(2,1)S(1)}, u32[]{:S(2)}, u32[]{:S(2)}) collective-permute-start(bf16[256,192]{1,0:T(8,128)(2,1)} %collective-permute-done.16.second), channel_id=1, source_target_pairs={{0,1},{1,0},{2,3},{3,2},{4,5},{5,4},{6,7},{7,6},{8,9},{9,8},{10,11... | collective-permute-start | bytes 294920 | tf_op jit(solution)/shard_map/ppermute | solution.py:25
  168.9 22.2 %collective-permute-start.29 = (bf16[432,768]{1,0:T(8,128)(2,1)}, bf16[432,768]{1,0:T(8,128)(2,1)}, u32[]{:S(2)}, u32[]{:S(2)}) collective-permute-start(bf16[432,768]{1,0:T(8,128)(2,1)} %add_convert_fusion.4), channel_id=1, source_target_pairs={{0,2},{1,3},{2,0},{3,1},{4,6},{5,7},{6,4},{7,5},{8,10},{9,11},{10,... | collective-permute-start | bytes 1990664 | tf_op jit(solution)/shard_map/ppermute | solution.py:25
  191.2 234.0 %all-gather.5.cloned.1.call-start = ((), (), s32[]{:S(2)}) async-start(), calls=%async_computation.2 | async-start | bytes 5308416 | tf_op jit(solution)/shard_map/all_gather | solution.py:1485
  191.2 23.4 %collective-permute-start.31 = (bf16[864,768]{1,0:T(8,128)(2,1)}, bf16[864,768]{1,0:T(8,128)(2,1)S(1)}, u32[]{:S(2)}, u32[]{:S(2)}) collective-permute-start(bf16[864,768]{1,0:T(8,128)(2,1)} %copy-done.91), channel_id=1, source_target_pairs={{0,1},{1,0},{2,3},{3,2},{4,5},{5,4},{6,7},{7,6},{8,9},{9,8},{10,11... | collective-permute-start | bytes 3981320 | tf_op jit(solution)/shard_map/ppermute | solution.py:25
  193.5 21.0 %collective-permute-start.32 = (bf16[256,768]{1,0:T(8,128)(2,1)S(1)}, bf16[256,768]{1,0:T(8,128)(2,1)S(1)}, u32[]{:S(2)}, u32[]{:S(2)}) collective-permute-start(bf16[256,768]{1,0:T(8,128)(2,1)S(1)} %fusion.14), channel_id=1, source_target_pairs={{0,1},{1,0},{2,3},{3,2},{4,5},{5,4},{6,7},{7,6},{8,9},{9,8},{10,11... | collective-permute-start | bytes 1179656 | tf_op jit(solution)/shard_map/ppermute | solution.py:25
  217.3 25.8 %collective-permute-start.36 = (bf16[432,768]{1,0:T(8,128)(2,1)S(1)}, bf16[432,768]{1,0:T(8,128)(2,1)S(1)}, u32[]{:S(2)}, u32[]{:S(2)}) collective-permute-start(bf16[432,768]{1,0:T(8,128)(2,1)S(1)} %add_convert_fusion.3), channel_id=1, source_target_pairs={{0,2},{1,3},{2,0},{3,1},{4,6},{5,7},{6,4},{7,5},{8,10},{9,11},{10,... | collective-permute-start | bytes 1990664 | tf_op jit(solution)/shard_map/ppermute | solution.py:25
  218.3 24.7 %collective-permute-start.37 = (bf16[256,768]{1,0:T(8,128)(2,1)S(1)}, bf16[256,768]{1,0:T(8,128)(2,1)S(1)}, u32[]{:S(2)}, u32[]{:S(2)}) collective-permute-start(bf16[256,768]{1,0:T(8,128)(2,1)S(1)} %reduce-precision_convert_fusion.2), channel_id=1, source_target_pairs={{0,2},{1,3},{2,0},{3,1},{4,6},{5,7},{6,4},{7,5},{8,10},{9,11},{10,... | collective-permute-start | bytes 1179656 | tf_op jit(solution)/shard_map/ppermute | solution.py:25
  270.0 20.4 %collective-permute-start.41 = (bf16[432,768]{1,0:T(8,128)(2,1)S(1)}, bf16[432,768]{1,0:T(8,128)(2,1)S(1)}, u32[]{:S(2)}, u32[]{:S(2)}) collective-permute-start(bf16[432,768]{1,0:T(8,128)(2,1)S(1)} %get-tuple-element.417.near), channel_id=1, source_target_pairs={{0,2},{1,3},{2,0},{3,1},{4,6},{5,7},{6,4},{7,5},{8,10},{9,11},{10,... | collective-permute-start | bytes 1990664 | tf_op jit(solution)/shard_map/ppermute | solution.py:25
  271.1 29.7 %collective-permute-start.44 = (bf16[432,768]{1,0:T(8,128)(2,1)S(1)}, bf16[432,768]{1,0:T(8,128)(2,1)S(1)}, u32[]{:S(2)}, u32[]{:S(2)}) collective-permute-start(bf16[432,768]{1,0:T(8,128)(2,1)S(1)} %get-tuple-element.417.near), channel_id=1, source_target_pairs={{0,1},{1,0},{2,3},{3,2},{4,5},{5,4},{6,7},{7,6},{8,9},{9,8},{10,11... | collective-permute-start | bytes 1990664 | tf_op jit(solution)/shard_map/ppermute | solution.py:25
  271.1 28.4 %collective-permute-start.40 = (bf16[512,1152]{1,0:T(8,128)(2,1)S(1)}, bf16[512,1152]{1,0:T(8,128)(2,1)S(1)}, u32[]{:S(2)}, u32[]{:S(2)}) collective-permute-start(bf16[512,1152]{1,0:T(8,128)(2,1)S(1)} %copy-done.140), channel_id=1, source_target_pairs={{0,4},{4,0},{8,12},{12,8},{16,20},{20,16},{24,28},{28,24},{1,5},{5... | collective-permute-start | bytes 3538952 | tf_op jit(solution)/shard_map/ppermute | solution.py:1391
  300.9 187.3 %all-gather.7.cloned.1.call-start = ((), (), s32[]{:S(2)}) async-start(), calls=%async_computation.3 | async-start | bytes 2654208 | tf_op jit(solution)/shard_map/all_gather | solution.py:1524
  302.4 33.8 %collective-permute-start.46 = (bf16[128,1152]{1,0:T(8,128)(2,1)S(1)}, bf16[128,1152]{1,0:T(8,128)(2,1)S(1)}, u32[]{:S(2)}, u32[]{:S(2)}) collective-permute-start(bf16[128,1152]{1,0:T(8,128)(2,1)S(1)} %get-tuple-element.514), channel_id=1, source_target_pairs={{0,8},{4,12},{8,0},{12,4},{16,24},{20,28},{24,16},{28,20},{1,9},{5... | collective-permute-start | bytes 884744 | tf_op jit(solution)/shard_map/ppermute | solution.py:111
  304.1 32.1 %collective-permute-start.47 = (bf16[128,1152]{1,0:T(8,128)(2,1)S(1)}, bf16[128,1152]{1,0:T(8,128)(2,1)S(1)}, u32[]{:S(2)}, u32[]{:S(2)}) collective-permute-start(bf16[128,1152]{1,0:T(8,128)(2,1)S(1)} %get-tuple-element.513), channel_id=1, source_target_pairs={{0,16},{4,20},{8,24},{12,28},{16,0},{20,4},{24,8},{28,12},{1,17},{... | collective-permute-start | bytes 884744 | tf_op jit(solution)/shard_map/ppermute | solution.py:111
  306.7 30.2 %collective-permute-start.48 = (bf16[128,1152]{1,0:T(8,128)(2,1)S(1)}, bf16[128,1152]{1,0:T(8,128)(2,1)S(1)}, u32[]{:S(2)}, u32[]{:S(2)}) collective-permute-start(bf16[128,1152]{1,0:T(8,128)(2,1)S(1)} %get-tuple-element.512), channel_id=1, source_target_pairs={{0,24},{4,28},{8,16},{12,20},{16,8},{20,12},{24,0},{28,4},{1,25},{... | collective-permute-start | bytes 884744 | tf_op jit(solution)/shard_map/ppermute | solution.py:111
  351.6 25.2 %collective-permute-start.52 = (bf16[512,576]{0,1:T(8,128)(2,1)}, bf16[512,576]{0,1:T(8,128)(2,1)}, u32[]{:S(2)}, u32[]{:S(2)}) collective-permute-start(bf16[512,576]{0,1:T(8,128)(2,1)} %copy.116), channel_id=1, source_target_pairs={{0,4},{4,0},{8,12},{12,8},{16,20},{20,16},{24,28},{28,24},{1,5},{5... | collective-permute-start | bytes 1769480 | tf_op jit(solution)/shard_map/ppermute | solution.py:1391
  356.9 66.2 %collective-permute-start.51 = (bf16[432,768]{1,0:T(8,128)(2,1)}, bf16[432,768]{1,0:T(8,128)(2,1)S(1)}, u32[]{:S(2)}, u32[]{:S(2)}) collective-permute-start(bf16[432,768]{1,0:T(8,128)(2,1)} %add_convert_fusion), channel_id=1, source_target_pairs={{0,2},{1,3},{2,0},{3,1},{4,6},{5,7},{6,4},{7,5},{8,10},{9,11},{10,... | collective-permute-start | bytes 1990664 | tf_op jit(solution)/shard_map/ppermute | solution.py:25
  381.2 35.3 %collective-permute-start.55 = (bf16[128,576]{1,0:T(8,128)(2,1)}, bf16[128,576]{1,0:T(8,128)(2,1)}, u32[]{:S(2)}, u32[]{:S(2)}) collective-permute-start(bf16[128,576]{1,0:T(8,128)(2,1)} %get-tuple-element.518), channel_id=1, source_target_pairs={{0,8},{4,12},{8,0},{12,4},{16,24},{20,28},{24,16},{28,20},{1,9},{5... | collective-permute-start | bytes 442376 | tf_op jit(solution)/shard_map/ppermute | solution.py:111
  402.7 20.3 %collective-permute-start.57 = (bf16[128,576]{1,0:T(8,128)(2,1)S(1)}, bf16[128,576]{1,0:T(8,128)(2,1)}, u32[]{:S(2)}, u32[]{:S(2)}) collective-permute-start(bf16[128,576]{1,0:T(8,128)(2,1)S(1)} %get-tuple-element.516), channel_id=1, source_target_pairs={{0,24},{4,28},{8,16},{12,20},{16,8},{20,12},{24,0},{28,4},{1,25},{... | collective-permute-start | bytes 442376 | tf_op jit(solution)/shard_map/ppermute | solution.py:111
  428.2 33.1 %collective-permute-start.62 = (bf16[384,768]{1,0:T(8,128)(2,1)S(1)}, bf16[384,768]{1,0:T(8,128)(2,1)S(1)}, u32[]{:S(2)}, u32[]{:S(2)}) collective-permute-start(bf16[384,768]{1,0:T(8,128)(2,1)S(1)} %get-tuple-element.507), channel_id=1, source_target_pairs={{0,1},{1,0},{2,3},{3,2},{4,5},{5,4},{6,7},{7,6},{8,9},{9,8},{10,11... | collective-permute-start | bytes 1769480 | tf_op jit(solution)/shard_map/ppermute | solution.py:25
  428.3 33.1 %collective-permute-start.63 = (bf16[384,768]{1,0:T(8,128)(2,1)S(1)}, bf16[384,768]{1,0:T(8,128)(2,1)S(1)}, u32[]{:S(2)}, u32[]{:S(2)}) collective-permute-start(bf16[384,768]{1,0:T(8,128)(2,1)S(1)} %get-tuple-element.506), channel_id=1, source_target_pairs={{0,2},{1,3},{2,0},{3,1},{4,6},{5,7},{6,4},{7,5},{8,10},{9,11},{10,... | collective-permute-start | bytes 1769480 | tf_op jit(solution)/shard_map/ppermute | solution.py:25
  429.5 31.9 %collective-permute-start.64 = (bf16[384,768]{1,0:T(8,128)(2,1)S(1)}, bf16[384,768]{1,0:T(8,128)(2,1)S(1)}, u32[]{:S(2)}, u32[]{:S(2)}) collective-permute-start(bf16[384,768]{1,0:T(8,128)(2,1)S(1)} %get-tuple-element.505), channel_id=1, source_target_pairs={{0,3},{1,2},{2,1},{3,0},{4,7},{5,6},{6,5},{7,4},{8,11},{9,10},{10,... | collective-permute-start | bytes 1769480 | tf_op jit(solution)/shard_map/ppermute | solution.py:25
  (185 other events, 1341.7 us)
Sparse Core Ops, SparseCore 0:
  49.2 70.4 all-gather.8
  191.3 96.0 reduce-scatter.1
  300.9 123.4 all-gather.4
  427.1 60.1 all-gather.6
